TPU v7x, 1024 devices: a whole 4x8x16 slice. The times are simulated.
1024 devices in a mesh: gx: 8 (over x, core), gy: 8 (over y), gz: 16 (over z).
Axes of the slice: x: 4, y: 8, z: 16, core: 2. Of those that a mesh axis runs over, the one named last changes fastest.
Arguments:
- right_side: float32 [64, 256, 2048], P('gx', 'gy', 'gz'), may hold values from -6 to 6
- sigma: float32 [64, 256, 2048], P('gx', 'gy', 'gz'), may hold values from 0.0001 to 0.001
- kappa: float32 [3, 64, 256, 2048], P(None, 'gx', 'gy', 'gz'), may hold values from 0.5 to 2
- coarse_inverse: float32 [1024, 1024], P(('gx', 'gy', 'gz')), as said below
Outputs:
- solution_field: float32 [64, 256, 2048], P('gx', 'gy', 'gz')
- residual: float32 [64, 256, 2048], P('gx', 'gy', 'gz')
Inputs may be any that keep to these rules, and one draw needn't show every extreme that they name: `coarse_inverse`: symmetric, with a positive diagonal that dominates each row.
All inputs are finite; a program needn't handle non-finite values.
Results may differ from a plain program's by a relative error of at most 0.0003.
Values sent between devices are 32-bit elements; how exact they have to be, the bound alone decides.
No kernel may reach another device: no remote copies, remote signals or barrier semaphores. Data moves between devices by JAX's collectives and lax.ppermute only.
A program may use at most 32 MiB of HBM per device.

v0:
```python
import functools

import jax
import jax.numpy as jnp
from jax import lax
from jax.experimental import pallas as pl
from jax.experimental.pallas import tpu as pltpu
from jax.sharding import PartitionSpec as P

CX, CY, CZ = 8, 32, 128
CELLS = 16
LINES = 16
THETA = 1.0 / 128.0
WEIGHT = 0.6
PART_AT, LOW_AT, HIGH_AT = 32, 64, 96
HIGHEST = lax.Precision.HIGHEST
F32 = jnp.float32


def iota(shape, dim):
    return lax.broadcasted_iota(jnp.int32, shape, dim)


def dot(a, b):
    return lax.dot_general(
        a, b, (((1,), (0,)), ((), ())), precision=HIGHEST, preferred_element_type=F32
    )


def dot_t(a, b):
    return lax.dot_general(
        a, b, (((1,), (1,)), ((), ())), precision=HIGHEST, preferred_element_type=F32
    )


def one_where(cond):
    return jnp.where(cond, 1.0, 0.0).astype(F32)


def lines_of(field):
    low = (field[0] + field[1]) + (field[2] + field[3])
    high = (field[4] + field[5]) + (field[6] + field[7])
    stacked = jnp.concatenate([low, high], axis=0)
    by_line = one_where(iota((128, 64), 1) // 4 == iota((128, 64), 0))
    by_cell = one_where(iota((CELLS, 128), 1) // 8 == iota((CELLS, 128), 0))
    return dot_t(by_cell, dot(by_line, stacked))


def faces_of(field):
    lane, row = iota((CX, CY, 128), 2), iota((CX, CY, 128), 1)
    low = jnp.where(lane == LOW_AT + row, field[:, :, 0:1], 0.0)
    both = jnp.where(lane == HIGH_AT + row, field[:, :, CZ - 1 : CZ], low)
    return jnp.sum(both, axis=1)


def write_z_message(zmsg_ref, rows, faces, spread_inverse, total, sizes):
    lane = iota((8, 128), 1)
    zero = jnp.zeros((1, 128), F32)
    head = jnp.concatenate(rows + [zero] * (8 - len(rows)), axis=0)
    base = jnp.where(lane < LINES, head, faces)
    mine = spread_inverse * total
    inside = (lane >= PART_AT) & (lane < PART_AT + 24)
    for p in range(sizes[2]):
        moved = pltpu.roll(mine, (PART_AT + 8 - 8 * p) % 128, 1)
        zmsg_ref[p] = jnp.where(inside, moved, base)


def write_planes(field, planes):
    xlo, xhi, ylo, yhi = planes
    xlo[...] = field[0]
    xhi[...] = field[CX - 1]
    ylo[...] = field[:, 0, :]
    yhi[...] = field[:, CY - 1, :]


def begin_kernel(
    sizes, r_ref, sigma_ref, kappa_ref, inv_ref,
    jac_ref, dinv_ref, zmsg_ref, loc_ref, alpha_ref, spread_ref, *planes
):
    r, sigma = r_ref[...], sigma_ref[...]
    kx, ky, kz = kappa_ref[0], kappa_ref[1], kappa_ref[2]
    dinv = WEIGHT / (sigma + 2.0 * (kx + ky + kz))
    jac = dinv * r
    dinv_ref[...] = dinv
    jac_ref[...] = jac
    write_planes(jac, planes)
    unused = iota((CELLS, 128), 1) >= LINES
    e = jnp.where(unused, 1.0, lines_of(sigma))
    g = jnp.where(unused, 1.0, lines_of(kz) * 0.125)
    rhs = lines_of(r)
    row = lambda a, k: a[k : k + 1, :]
    first, mid, last = row(e, 0), row(g, 0), row(e, 1)
    cur_first, cur = row(rhs, 0), row(rhs, 1)
    zero = jnp.zeros((1, 128), F32)
    for c in range(3):
        for k in (0, CELLS - 1):
            loc_ref[c, k : k + 1, :] = zero
    for k in (0, CELLS - 1):
        alpha_ref[k : k + 1, :] = zero
    for k in range(1, CELLS - 1):
        inv = 1.0 / (mid + last + row(g, k))
        mu, gam = mid * inv, row(g, k) * inv
        loc_ref[0, k : k + 1, :] = mu
        loc_ref[1, k : k + 1, :] = gam
        loc_ref[2, k : k + 1, :] = inv
        alpha_ref[k : k + 1, :] = cur * inv
        first = first + mu * last
        mid = mu * row(g, k)
        last = row(e, k + 1) + gam * last
        cur_first = cur_first + mu * cur
        cur = row(rhs, k + 1) + gam * cur
    move = one_where((iota((128, 128), 0) % 16) * 8 + iota((128, 128), 0) // 16 == iota((128, 128), 1))
    spread_inverse = dot(inv_ref[...], move)
    spread_ref[...] = spread_inverse
    rows = [cur_first, cur, first, mid, last, row(g, CELLS - 1)]
    write_z_message(zmsg_ref, rows, faces_of(jac), spread_inverse, jnp.sum(r), sizes)


def chain_kernel(sizes, fresh, zrec_ref, loc_ref, alpha_ref, *refs):
    if fresh:
        xmsg_ref, own_ref, zhalo_ref, chain_ref, final_ref, sol_ref = refs
    else:
        chain_ref, final_ref, xmsg_ref, own_ref, zhalo_ref, sol_ref = refs
    nx, ny, nz = sizes
    mx, my, mz = lax.axis_index("gx"), lax.axis_index("gy"), lax.axis_index("gz")
    used = iota((8, 128), 1) < LINES
    tiles = [jnp.where(used, zrec_ref[p], 1.0) for p in range(nz)]
    part = lambda p, i: tiles[p][i : i + 1, :]
    zero = jnp.zeros((1, 128), F32)

    if fresh:
        one = zero + 1.0
        cond, cond_own, hold, ginv = zero, zero, one, one
        for p in range(nz - 1):
            a, m, b, g = part(p, 2), part(p, 3), part(p, 4), part(p, 5)
            at_first = a + cond
            s = m + at_first
            n = b * s + m * at_first
            inv = 1.0 / (n + g * s)
            chain_ref[0, p : p + 1, :] = g * m * inv
            c2 = g * s * inv
            chain_ref[1, p : p + 1, :] = c2
            cond = g * n * inv
            here = mz == p + 1
            cond_own = jnp.where(here, cond, cond_own)
            hold = jnp.where(here, c2, hold)
            ginv = jnp.where(here, g, ginv)
        left_cond, left_hold, left_ginv = cond_own, hold, 1.0 / ginv
        cond = part(nz - 1, 5)
        cond_own, hold, ginv = cond, one, one
        for p in range(nz - 1, 0, -1):
            a, m, b, g = part(p, 2), part(p, 3), part(p, 4), part(p - 1, 5)
            at_last = b + cond
            s = m + at_last
            n = a * s + m * at_last
            inv = 1.0 / (n + g * s)
            chain_ref[2, p : p + 1, :] = g * m * inv
            c2 = g * s * inv
            chain_ref[3, p : p + 1, :] = c2
            cond = g * n * inv
            here = mz == p - 1
            cond_own = jnp.where(here, cond, cond_own)
            hold = jnp.where(here, c2, hold)
            ginv = jnp.where(here, g, ginv)
        right_cond, right_hold, right_ginv = cond_own, hold, 1.0 / ginv
        for c, p in ((0, nz - 1), (1, nz - 1), (2, 0), (3, 0)):
            chain_ref[c, p : p + 1, :] = zero
        mine = jnp.where(used, zrec_ref[mz], 1.0)
        big_a = mine[2:3, :] + left_cond
        big_b = mine[4:5, :] + right_cond
        m = mine[3:4, :]
        det_inv = 1.0 / (big_a * m + big_b * m + big_a * big_b)
        f1, f2, f3 = (big_b + m) * det_inv, m * det_inv, (big_a + m) * det_inv
        final_ref[...] = jnp.concatenate(
            [f1, f2, f3, left_ginv, left_hold, right_ginv, right_hold, zero], axis=0
        )
    else:
        mine = jnp.where(used, zrec_ref[mz], 0.0)
        f1, f2, f3, left_ginv, left_hold, right_ginv, right_hold = [
            final_ref[i : i + 1, :] for i in range(7)
        ]
    chain = lambda c, p: chain_ref[c, p : p + 1, :]
    cur, cur_left = zero, zero
    for p in range(nz - 1):
        cur = chain(0, p) * (part(p, 0) + cur) + chain(1, p) * part(p, 1)
        cur_left = jnp.where(mz == p + 1, cur, cur_left)
    cur, cur_right = zero, zero
    for p in range(nz - 1, 0, -1):
        cur = chain(2, p) * (part(p, 1) + cur) + chain(3, p) * part(p, 0)
        cur_right = jnp.where(mz == p - 1, cur, cur_right)
    cur_first = mine[0:1, :] + cur_left
    cur_last = mine[1:2, :] + cur_right
    sol_first = f1 * cur_first + f2 * cur_last
    sol_last = f2 * cur_first + f3 * cur_last
    below = cur_left * left_ginv + left_hold * sol_first
    above = cur_right * right_ginv + right_hold * sol_last
    sol_ref[0:1, :] = sol_first
    sol_ref[CELLS - 1 : CELLS, :] = sol_last
    value = sol_last
    for k in range(CELLS - 2, 0, -1):
        value = alpha_ref[k : k + 1, :] + loc_ref[0, k : k + 1, :] * sol_first + loc_ref[1, k : k + 1, :] * value
        sol_ref[k : k + 1, :] = value
    lanes16 = iota((CELLS, 128), 1) < LINES
    sol = jnp.where(lanes16, sol_ref[...], 0.0) * THETA

    line, lane = iota((128, 128), 0), iota((128, 128), 1)
    picks = [
        one_where(line == lane // 16),
        one_where(line == 8 + lane // 16),
        one_where((line == (lane // 16) * 8) & (lane < 32)),
        one_where((line == (lane // 16) * 8 + 7) & (lane < 32)),
    ]
    keep = iota((CELLS, 128), 1) % 16 == iota((CELLS, 128), 0)
    x_low, x_high, y_low, y_high = [
        jnp.sum(jnp.where(keep, dot(sol, pick), 0.0), axis=0, keepdims=True) for pick in picks
    ]
    own_ref[...] = jnp.concatenate([x_low, x_high] + [zero] * 6, axis=0)

    lane8, row8 = iota((8, 128), 1), iota((8, 128), 0)
    of_row = (lane8 // 8 == row8 // 4) & (lane8 < LINES)
    to_high = one_where((lane >= HIGH_AT) & ((lane - HIGH_AT) // 4 == line % 8) & (line < LINES))
    to_low = one_where(
        (lane >= LOW_AT) & (lane < HIGH_AT) & ((lane - LOW_AT) // 4 == line % 8) & (line < LINES)
    )
    lines_part = dot(jnp.where(of_row, below, 0.0), to_high) + dot(jnp.where(of_row, above, 0.0), to_low)
    from_below = zrec_ref[jnp.maximum(mz - 1, 0)]
    from_above = zrec_ref[jnp.minimum(mz + 1, nz - 1)]
    face = jnp.where(lane8 >= HIGH_AT, from_below, from_above)
    zhalo_ref[...] = jnp.where(lane8 >= LOW_AT, face + THETA * lines_part, 0.0)

    total = zrec_ref[0]
    for p in range(1, nz):
        total = total + zrec_ref[p]
    at = lambda lo: (lane8 >= lo) & (lane8 < lo + 8)
    x_less = pltpu.roll(pltpu.roll(total, 1, 0), 16, 1)
    x_more = pltpu.roll(pltpu.roll(total, 7, 0), 24, 1)
    sums = jnp.where((lane8 >= PART_AT) & (lane8 < PART_AT + 24), total, 0.0)
    sums = jnp.where(at(PART_AT + 24), x_less, sums)
    sums = jnp.where(at(PART_AT + 32), x_more, sums)
    second = iota((2, 128), 0) == 1
    for i in range(nx):
        both = jnp.where(second, sums[i : i + 1, :], 0.0)
        for j in range(ny):
            xmsg_ref[i * ny + j] = both
    here = mx * ny + my

    @pl.when(mx > 0)
    def _():
        xmsg_ref[here - ny, 0:1, :] = x_low

    @pl.when(mx < nx - 1)
    def _():
        xmsg_ref[here + ny, 0:1, :] = x_high

    @pl.when(my > 0)
    def _():
        xmsg_ref[here - 1, 0:1, :] = y_low

    @pl.when(my < ny - 1)
    def _():
        xmsg_ref[here + 1, 0:1, :] = y_high


def operator(sizes, base, sigma_ref, kappa_ref, xrec_ref, own_ref, zhalo_ref, halos, z_ref, w_ref):
    nx, ny, nz = sizes
    mx, my, mz = lax.axis_index("gx"), lax.axis_index("gy"), lax.axis_index("gz")
    here = mx * ny + my
    sums = xrec_ref[0, 1:2, :]
    for q in range(1, nx * ny):
        sums = sums + xrec_ref[q, 1:2, :]
    lane1 = iota((1, 128), 1)
    coarse = lambda at: jnp.sum(jnp.where(lane1 == at + my, sums, 0.0))
    c_own = coarse(PART_AT + 8)
    c_zlo, c_zhi = coarse(PART_AT), coarse(PART_AT + 16)
    c_ylo, c_yhi = coarse(PART_AT + 7), coarse(PART_AT + 9)
    c_xlo, c_xhi = coarse(PART_AT + 24), coarse(PART_AT + 32)

    lane32, row32 = iota((CY, 128), 1), iota((CY, 128), 0)
    lane8, row8 = iota((8, 128), 1), iota((8, 128), 0)
    wide = lambda row: jnp.where(lane32 // 16 == row32 // 4, row, 0.0)
    thin = lambda row: jnp.where(lane8 // 16 == row8 // 4, row, 0.0)
    left = xrec_ref[jnp.maximum(here - ny, 0), 0:1, :]
    right = xrec_ref[jnp.minimum(here + ny, nx * ny - 1), 0:1, :]
    front = xrec_ref[jnp.maximum(here - 1, 0), 0:1, :]
    back = xrec_ref[jnp.minimum(here + 1, nx * ny - 1), 0:1, :]
    rows = jnp.concatenate(
        [wide(own_ref[0:1, :]), wide(own_ref[1:2, :]), wide(left), wide(right), thin(front), thin(back)],
        axis=0,
    )
    to_cells = one_where(iota((128, 128), 0) % 16 == iota((128, 128), 1) // 8)
    lines = dot(rows, to_cells)
    xlo, xhi, ylo, yhi = halos
    xlo = jnp.where(mx > 0, xlo[...] + lines[64:96] + c_xlo, 0.0)
    xhi = jnp.where(mx < nx - 1, xhi[...] + lines[96:128] + c_xhi, 0.0)
    ylo = jnp.where(my > 0, ylo[...] + lines[128:136] + c_ylo, 0.0)
    yhi = jnp.where(my < ny - 1, yhi[...] + lines[136:144] + c_yhi, 0.0)
    face = zhalo_ref[...]
    high = jnp.where(mz > 0, face + c_zlo, 0.0)
    low = jnp.where(mz < nz - 1, face + c_zhi, 0.0)
    face = jnp.where(lane8 >= HIGH_AT, high, low)
    diagonal = (lane32 == row32 + HIGH_AT) | (lane32 == row32 + LOW_AT)
    spots = jnp.concatenate([jnp.where(diagonal, face[x : x + 1, :], 0.0) for x in range(CX)], axis=0)
    j, k = iota((128, 128), 0), iota((128, 128), 1)
    to_ends = one_where(((j >= HIGH_AT) & (k == 0)) | ((j >= LOW_AT) & (j < HIGH_AT) & (k == CZ - 1)))
    ends = dot(spots, to_ends)

    z = [base(x) + lines[(x // 4) * 32 : (x // 4) * 32 + 32] + c_own for x in range(CX)]
    w = []
    for x in range(CX):
        here_z = z[x]
        z_ref[x] = here_z
        before = z[x - 1] if x > 0 else xlo
        after = z[x + 1] if x < CX - 1 else xhi
        y_less = jnp.where(row32 == 0, ylo[x : x + 1, :], pltpu.roll(here_z, 1, 0))
        y_more = jnp.where(row32 == CY - 1, yhi[x : x + 1, :], pltpu.roll(here_z, CY - 1, 0))
        z_less = jnp.where(lane32 == 0, 0.0, pltpu.roll(here_z, 1, 1))
        z_more = jnp.where(lane32 == CZ - 1, 0.0, pltpu.roll(here_z, CZ - 1, 1))
        twice = 2.0 * here_z
        value = (
            sigma_ref[x] * here_z
            + kappa_ref[0, x] * (twice - before - after)
            + kappa_ref[1, x] * (twice - y_less - y_more)
            + kappa_ref[2, x] * (twice - z_less - z_more - ends[x * 32 : x * 32 + 32])
        )
        w_ref[x] = value
        w.append(value)
    return z, w


def first_kernel(
    sizes, jac_ref, dinv_ref, sigma_ref, kappa_ref, xrec_ref, own_ref, zhalo_ref, h0, h1, h2, h3,
    loc_ref, spread_ref, z_ref, w_ref, zmsg_ref, alpha_ref, *planes
):
    base = lambda x: jac_ref[x]
    operator(sizes, base, sigma_ref, kappa_ref, xrec_ref, own_ref, zhalo_ref, (h0, h1, h2, h3), z_ref, w_ref)
    field = w_ref[...]
    jac = dinv_ref[...] * field
    write_planes(jac, planes)
    rhs = lines_of(field)
    row = lambda a, k: a[k : k + 1, :]
    cur_first, cur = row(rhs, 0), row(rhs, 1)
    zero = jnp.zeros((1, 128), F32)
    for k in (0, CELLS - 1):
        alpha_ref[k : k + 1, :] = zero
    for k in range(1, CELLS - 1):
        alpha_ref[k : k + 1, :] = cur * loc_ref[2, k : k + 1, :]
        cur_first = cur_first + loc_ref[0, k : k + 1, :] * cur
        cur = row(rhs, k + 1) + loc_ref[1, k : k + 1, :] * cur
    write_z_message(
        zmsg_ref, [cur_first, cur], faces_of(jac), spread_ref[...], jnp.sum(field), sizes
    )


def second_kernel(
    sizes, r_ref, w1_ref, dinv_ref, sigma_ref, kappa_ref, xrec_ref, own_ref, zhalo_ref, h0, h1, h2, h3,
    z_ref, w_ref, sums_ref
):
    base = lambda x: dinv_ref[x] * w1_ref[x]
    operator(sizes, base, sigma_ref, kappa_ref, xrec_ref, own_ref, zhalo_ref, (h0, h1, h2, h3), z_ref, w_ref)
    w1, w2, r = w1_ref[...], w_ref[...], r_ref[...]
    lane = iota((1, 128), 1)
    out = jnp.zeros((1, 128), F32)
    for i, product in enumerate((w1 * w1, w1 * w2, w2 * w2, w1 * r, w2 * r)):
        out = jnp.where(lane == i, jnp.sum(product), out)
    sums_ref[...] = out


def end_kernel(all_ref, r_ref, z1_ref, w1_ref, z2_ref, w2_ref, field_ref, res_ref):
    sums = all_ref[0]
    for q in range(1, all_ref.shape[0]):
        sums = sums + all_ref[q]
    lane = iota((1, 128), 1)
    spread = lambda i: jnp.sum(jnp.where(lane == i, sums, 0.0), axis=1, keepdims=True)
    g11, g12, g22, h1, h2 = [spread(i) for i in range(5)]
    inv = 1.0 / (g11 * g22 - g12 * g12)
    y1 = (g22 * h1 - g12 * h2) * inv
    y2 = (g11 * h2 - g12 * h1) * inv
    for x in range(CX):
        field_ref[x] = y1 * z1_ref[x] + y2 * z2_ref[x]
        res_ref[x] = r_ref[x] - y1 * w1_ref[x] - y2 * w2_ref[x]


def call(kernel, out_shapes, scratch=(), name=None, **kw):
    vmem = pl.BlockSpec(memory_space=pltpu.VMEM)

    def run(*args):
        return pl.pallas_call(
            kernel,
            out_shape=[jax.ShapeDtypeStruct(s, F32) for s in out_shapes],
            in_specs=[vmem] * len(args),
            out_specs=[vmem] * len(out_shapes),
            scratch_shapes=[pltpu.VMEM(s, F32) for s in scratch],
            compiler_params=pltpu.CompilerParams(vmem_limit_bytes=24 * 1024 * 1024),
            name=name,
            **kw,
        )(*args)

    return run


def shards(sizes, r, sigma, kappa, inverse_rows):
    nx, ny, nz = sizes
    field, plane, tile, coarse = (CX, CY, CZ), (CY, CZ), (8, 128), (CELLS, 128)
    planes = [plane, plane, tile, tile]
    to_z, to_xy = (nz, 8, 128), (nx * ny, 2, 128)

    def halo(parts):
        xlo, xhi, ylo, yhi = parts
        up = lambda n: [(i, (i + 1) % n) for i in range(n)]
        down = lambda n: [((i + 1) % n, i) for i in range(n)]
        return (
            lax.ppermute(xhi, "gx", up(nx)),
            lax.ppermute(xlo, "gx", down(nx)),
            lax.ppermute(yhi, "gy", up(ny)),
            lax.ppermute(ylo, "gy", down(ny)),
        )

    def along_z(message):
        return lax.all_to_all(message, "gz", split_axis=0, concat_axis=0, tiled=True)

    def along_xy(message):
        return lax.all_to_all(message, ("gx", "gy"), split_axis=0, concat_axis=0, tiled=True)

    bind = lambda kernel, *a: functools.partial(kernel, sizes, *a)
    jac, dinv, zmsg, loc, alpha, spread, *sides = call(
        bind(begin_kernel), [field, field, to_z, (3, *coarse), coarse, tile, *planes], name="begin"
    )(r, sigma, kappa, inverse_rows)
    zrec = along_z(zmsg)
    halos = halo(sides)
    xmsg, own, zhalo, chain, final = call(
        bind(chain_kernel, True), [to_xy, tile, tile, (4, nz, 128), tile], [coarse], name="lines_first"
    )(zrec, loc, alpha)
    xrec = along_xy(xmsg)
    z1, w1, zmsg, alpha, *sides = call(
        bind(first_kernel), [field, field, to_z, coarse, *planes], name="operator_first"
    )(jac, dinv, sigma, kappa, xrec, own, zhalo, *halos, loc, spread)
    zrec = along_z(zmsg)
    halos = halo(sides)
    xmsg, own, zhalo = call(
        bind(chain_kernel, False), [to_xy, tile, tile], [coarse], name="lines_second"
    )(zrec, loc, alpha, chain, final)
    xrec = along_xy(xmsg)
    z2, w2, sums = call(bind(second_kernel), [field, field, (1, 128)], name="operator_second")(
        r, w1, dinv, sigma, kappa, xrec, own, zhalo, *halos
    )
    sums = jnp.sum(along_z(jnp.broadcast_to(sums[None], (nz, 1, 128))), axis=0)
    sums = along_xy(jnp.broadcast_to(sums[None], (nx * ny, 1, 128)))
    return tuple(call(end_kernel, [field, field], name="end")(sums, r, z1, w1, z2, w2))


def solution(mesh):
    sizes = (mesh.shape["gx"], mesh.shape["gy"], mesh.shape["gz"])
    spec = P("gx", "gy", "gz")

    def run(r, sigma, kappa, inverse):
        return shards(sizes, r, sigma, kappa, inverse.reshape(8, 128))

    return jax.shard_map(
        run,
        mesh=mesh,
        in_specs=(spec, spec, P(None, "gx", "gy", "gz"), P(("gx", "gy", "gz"), None)),
        out_specs=(spec, spec),
        check_vma=False,
    )
```

profile of v0, /device:TPU:1, one launch (start us, length us, event | category | flops | bytes accessed | tf_op | source)
XLA Modules:
  0.0 135.7 jit_solution(10850018944115461862)
XLA Ops:
  0.6 0.0 copy-start
  0.6 1.0 copy-done
  1.6 0.0 copy-start.2
  1.6 0.9 copy-done.2
  2.5 0.0 copy-start.4
  2.5 0.9 copy-done.4
  3.4 0.0 copy-start.6
  3.4 0.7 copy-done.6
  4.1 0.0 copy-start.1
  4.1 1.0 begin.1
  5.1 30.8 %all_to_all.30.zrec_ref = f32[16,8,128]{2,1,0:T(8,128)S(1)} all-to-all(f32[16,8,128]{2,1,0:T(8,128)S(1)} %get-tuple-element.33), channel_id=1, replica_groups=mesh['gx'=8,'gy'=8,'gz'=16] {'gz'}, dimensions={0} | all-to-all | bytes 131072 | tf_op jit(solution)/shard_map/all_to_all | solution.py:419
  35.9 0.0 copy-start.3
  35.9 1.3 lines_first.1
  37.2 12.2 %all-to-all-start.1 = ((f32[64,2,128]{2,1,0:T(2,128)}), f32[64,2,128]{2,1,0:T(2,128)S(1)}, u32[]{:S(2)}, u32[]{:S(2)}) async-start(f32[64,2,128]{2,1,0:T(2,128)} %get-tuple-element.36), calls=%async_computation.1 | async-start | bytes 131072 | tf_op jit(solution)/shard_map/all_to_all | solution.py:422
  49.5 1.6 %collective-permute-start = (f32[32,128]{1,0:T(8,128)S(1)}, f32[32,128]{1,0:T(8,128)S(1)}, u32[]{:S(2)}, u32[]{:S(2)}) collective-permute-start(f32[32,128]{1,0:T(8,128)S(1)} %get-tuple-element.39), channel_id=1, source_target_pairs={{0,128},{128,256},{256,384},{384,512},{512,640},{640,768},{768,896... | collective-permute-start | bytes 49160 | tf_op jit(solution)/shard_map/ppermute | solution.py:412
  51.1 0.0 collective-permute-start.1
  51.1 3.1 %collective-permute-start.2 = (f32[8,128]{1,0:T(8,128)S(1)}, f32[8,128]{1,0:T(8,128)S(1)}, u32[]{:S(2)}, u32[]{:S(2)}) collective-permute-start(f32[8,128]{1,0:T(8,128)S(1)} %get-tuple-element.41), channel_id=1, source_target_pairs={{0,16},{16,32},{32,48},{48,64},{64,80},{80,96},{96,112},{112,0},{1... | collective-permute-start | bytes 12296 | tf_op jit(solution)/shard_map/ppermute | solution.py:414
  54.2 3.4 %collective-permute-start.3 = (f32[8,128]{1,0:T(8,128)S(1)}, f32[8,128]{1,0:T(8,128)S(1)}, u32[]{:S(2)}, u32[]{:S(2)}) collective-permute-start(f32[8,128]{1,0:T(8,128)S(1)} %get-tuple-element.42), channel_id=1, source_target_pairs={{16,0},{32,16},{48,32},{64,48},{80,64},{96,80},{112,96},{0,112},{1... | collective-permute-start | bytes 12296 | tf_op jit(solution)/shard_map/ppermute | solution.py:415
  57.6 0.0 collective-permute-done.2.h2
  57.6 1.2 collective-permute-done.3.h3
  58.9 0.0 collective-permute-done.h0
  58.9 0.0 collective-permute-done.1.h1
  58.9 0.1 all-to-all-done.1.xrec_ref
  58.9 0.0 copy-done.1
  58.9 0.0 copy-done.3
  58.9 1.1 operator_first.1
  60.0 14.2 %all_to_all.31.zrec_ref = f32[16,8,128]{2,1,0:T(8,128)S(1)} all-to-all(f32[16,8,128]{2,1,0:T(8,128)S(1)} %get-tuple-element.45), channel_id=1, replica_groups=mesh['gx'=8,'gy'=8,'gz'=16] {'gz'}, dimensions={0} | all-to-all | bytes 131072 | tf_op jit(solution)/shard_map/all_to_all | solution.py:419
  74.2 0.0 copy-start.5
  74.2 1.1 lines_second.1
  75.4 13.3 %all-to-all-start.3 = ((f32[64,2,128]{2,1,0:T(2,128)}), f32[64,2,128]{2,1,0:T(2,128)S(1)}, u32[]{:S(2)}, u32[]{:S(2)}) async-start(f32[64,2,128]{2,1,0:T(2,128)} %get-tuple-element.49), calls=%async_computation.3 | async-start | bytes 131072 | tf_op jit(solution)/shard_map/all_to_all | solution.py:422
  88.7 1.6 %collective-permute-start.4 = (f32[32,128]{1,0:T(8,128)S(1)}, f32[32,128]{1,0:T(8,128)S(1)}, u32[]{:S(2)}, u32[]{:S(2)}) collective-permute-start(f32[32,128]{1,0:T(8,128)S(1)} %get-tuple-element.52), channel_id=1, source_target_pairs={{0,128},{128,256},{256,384},{384,512},{512,640},{640,768},{768,896... | collective-permute-start | bytes 49160 | tf_op jit(solution)/shard_map/ppermute | solution.py:412
  90.3 0.0 collective-permute-start.5
  90.3 3.1 %collective-permute-start.6 = (f32[8,128]{1,0:T(8,128)S(1)}, f32[8,128]{1,0:T(8,128)S(1)}, u32[]{:S(2)}, u32[]{:S(2)}) collective-permute-start(f32[8,128]{1,0:T(8,128)S(1)} %get-tuple-element.54), channel_id=1, source_target_pairs={{0,16},{16,32},{32,48},{48,64},{64,80},{80,96},{96,112},{112,0},{1... | collective-permute-start | bytes 12296 | tf_op jit(solution)/shard_map/ppermute | solution.py:414
  93.4 3.4 %collective-permute-start.7 = (f32[8,128]{1,0:T(8,128)S(1)}, f32[8,128]{1,0:T(8,128)S(1)}, u32[]{:S(2)}, u32[]{:S(2)}) collective-permute-start(f32[8,128]{1,0:T(8,128)S(1)} %get-tuple-element.55), channel_id=1, source_target_pairs={{16,0},{32,16},{48,32},{64,48},{80,64},{96,80},{112,96},{0,112},{1... | collective-permute-start | bytes 12296 | tf_op jit(solution)/shard_map/ppermute | solution.py:415
  96.8 0.0 collective-permute-done.6.h2
  96.8 1.2 collective-permute-done.7.h3
  98.1 0.0 collective-permute-done.4.h0
  98.1 0.0 collective-permute-done.5.h1
  98.1 0.1 all-to-all-done.3.xrec_ref
  98.1 0.0 copy-done.5
  98.1 0.7 operator_second.1
  98.8 13.8 %all_to_all.32 = f32[16,1,128]{2,1,0:T(1,128)S(1)} all-to-all(f32[16,1,128]{2,1,0:T(1,128)S(1)} %broadcast_in_dim.7), channel_id=1, replica_groups=mesh['gx'=8,'gy'=8,'gz'=16] {'gz'}, dimensions={0} | all-to-all | bytes 16384 | tf_op jit(solution)/shard_map/all_to_all | solution.py:419
  112.7 22.1 %all_to_all.33.all_ref = f32[64,1,128]{2,1,0:T(1,128)S(1)} all-to-all(f32[64,1,128]{2,1,0:T(1,128)S(1)} %broadcast_in_dim.16), channel_id=1, replica_groups=mesh['gx'=8,'gy'=8,'gz'=16] {'gx','gy'}, dimensions={0} | all-to-all | bytes 65536 | tf_op jit(solution)/shard_map/all_to_all | solution.py:422
  134.8 0.9 end.1
  (3 shorter events, 0.0 us)
Async XLA Ops:
  0.6 1.0 copy-start
  1.6 0.9 copy-start.2
  2.5 0.9 copy-start.4
  3.4 0.7 copy-start.6
  4.1 54.8 %copy-start.1 = (f32[3,8,32,128]{3,2,1,0:T(8,128)S(1)}, f32[3,8,32,128]{3,2,1,0:T(8,128)}, u32[]{:S(2)}) copy-start(f32[3,8,32,128]{3,2,1,0:T(8,128)} %kappa_ref.5) | copy-start | bytes 1179652
  35.9 23.0 %copy-start.3 = (f32[8,32,128]{2,1,0:T(8,128)S(1)}, f32[8,32,128]{2,1,0:T(8,128)}, u32[]{:S(2)}) copy-start(f32[8,32,128]{2,1,0:T(8,128)} %sigma_ref.5) | copy-start | bytes 393220
  37.2 21.7 %all-to-all-start.1 = ((f32[64,2,128]{2,1,0:T(2,128)}), f32[64,2,128]{2,1,0:T(2,128)S(1)}, u32[]{:S(2)}, u32[]{:S(2)}) async-start(f32[64,2,128]{2,1,0:T(2,128)} %get-tuple-element.36), calls=%async_computation.1 | async-start | bytes 131072 | tf_op jit(solution)/shard_map/all_to_all | solution.py:422
  49.5 9.4 %collective-permute-start = (f32[32,128]{1,0:T(8,128)S(1)}, f32[32,128]{1,0:T(8,128)S(1)}, u32[]{:S(2)}, u32[]{:S(2)}) collective-permute-start(f32[32,128]{1,0:T(8,128)S(1)} %get-tuple-element.39), channel_id=1, source_target_pairs={{0,128},{128,256},{256,384},{384,512},{512,640},{640,768},{768,896... | collective-permute-start | bytes 49160 | tf_op jit(solution)/shard_map/ppermute | solution.py:412
  51.1 7.7 %collective-permute-start.1 = (f32[32,128]{1,0:T(8,128)S(1)}, f32[32,128]{1,0:T(8,128)S(1)}, u32[]{:S(2)}, u32[]{:S(2)}) collective-permute-start(f32[32,128]{1,0:T(8,128)S(1)} %get-tuple-element.40), channel_id=1, source_target_pairs={{128,0},{256,128},{384,256},{512,384},{640,512},{768,640},{896,768... | collective-permute-start | bytes 49160 | tf_op jit(solution)/shard_map/ppermute | solution.py:413
  51.1 6.5 %collective-permute-start.2 = (f32[8,128]{1,0:T(8,128)S(1)}, f32[8,128]{1,0:T(8,128)S(1)}, u32[]{:S(2)}, u32[]{:S(2)}) collective-permute-start(f32[8,128]{1,0:T(8,128)S(1)} %get-tuple-element.41), channel_id=1, source_target_pairs={{0,16},{16,32},{32,48},{48,64},{64,80},{80,96},{96,112},{112,0},{1... | collective-permute-start | bytes 12296 | tf_op jit(solution)/shard_map/ppermute | solution.py:414
  54.2 4.6 %collective-permute-start.3 = (f32[8,128]{1,0:T(8,128)S(1)}, f32[8,128]{1,0:T(8,128)S(1)}, u32[]{:S(2)}, u32[]{:S(2)}) collective-permute-start(f32[8,128]{1,0:T(8,128)S(1)} %get-tuple-element.42), channel_id=1, source_target_pairs={{16,0},{32,16},{48,32},{64,48},{80,64},{96,80},{112,96},{0,112},{1... | collective-permute-start | bytes 12296 | tf_op jit(solution)/shard_map/ppermute | solution.py:415
  74.2 23.9 %copy-start.5 = (f32[8,32,128]{2,1,0:T(8,128)S(1)}, f32[8,32,128]{2,1,0:T(8,128)}, u32[]{:S(2)}) copy-start(f32[8,32,128]{2,1,0:T(8,128)} %r_ref.5) | copy-start | bytes 393220
  75.4 22.8 %all-to-all-start.3 = ((f32[64,2,128]{2,1,0:T(2,128)}), f32[64,2,128]{2,1,0:T(2,128)S(1)}, u32[]{:S(2)}, u32[]{:S(2)}) async-start(f32[64,2,128]{2,1,0:T(2,128)} %get-tuple-element.49), calls=%async_computation.3 | async-start | bytes 131072 | tf_op jit(solution)/shard_map/all_to_all | solution.py:422
  88.7 9.4 %collective-permute-start.4 = (f32[32,128]{1,0:T(8,128)S(1)}, f32[32,128]{1,0:T(8,128)S(1)}, u32[]{:S(2)}, u32[]{:S(2)}) collective-permute-start(f32[32,128]{1,0:T(8,128)S(1)} %get-tuple-element.52), channel_id=1, source_target_pairs={{0,128},{128,256},{256,384},{384,512},{512,640},{640,768},{768,896... | collective-permute-start | bytes 49160 | tf_op jit(solution)/shard_map/ppermute | solution.py:412
  90.3 7.7 %collective-permute-start.5 = (f32[32,128]{1,0:T(8,128)S(1)}, f32[32,128]{1,0:T(8,128)S(1)}, u32[]{:S(2)}, u32[]{:S(2)}) collective-permute-start(f32[32,128]{1,0:T(8,128)S(1)} %get-tuple-element.53), channel_id=1, source_target_pairs={{128,0},{256,128},{384,256},{512,384},{640,512},{768,640},{896,768... | collective-permute-start | bytes 49160 | tf_op jit(solution)/shard_map/ppermute | solution.py:413
  90.3 6.5 %collective-permute-start.6 = (f32[8,128]{1,0:T(8,128)S(1)}, f32[8,128]{1,0:T(8,128)S(1)}, u32[]{:S(2)}, u32[]{:S(2)}) collective-permute-start(f32[8,128]{1,0:T(8,128)S(1)} %get-tuple-element.54), channel_id=1, source_target_pairs={{0,16},{16,32},{32,48},{48,64},{64,80},{80,96},{96,112},{112,0},{1... | collective-permute-start | bytes 12296 | tf_op jit(solution)/shard_map/ppermute | solution.py:414
  93.4 4.6 %collective-permute-start.7 = (f32[8,128]{1,0:T(8,128)S(1)}, f32[8,128]{1,0:T(8,128)S(1)}, u32[]{:S(2)}, u32[]{:S(2)}) collective-permute-start(f32[8,128]{1,0:T(8,128)S(1)} %get-tuple-element.55), channel_id=1, source_target_pairs={{16,0},{32,16},{48,32},{64,48},{80,64},{96,80},{112,96},{0,112},{1... | collective-permute-start | bytes 12296 | tf_op jit(solution)/shard_map/ppermute | solution.py:415
where the time goes:
time: 136 us
  blocking collectives  80.9 us (59%)
  starting transfers between devices  41.8 us (31%)
  Pallas kernels  6.1 us (4%)
  local copies, waits for them, and re-layouts  3.52 us (3%)
  waiting for transfers between devices  2.58 us (2%)
    all_to_all x3, blocking collectives, along_z(): lax.all_to_all(message, 'gz', split_axis=0, concat_axis=0, tiled=True)  58.8 us
    all_to_all x2, starting transfers between devices, along_xy(): lax.all_to_all(message, ('gx', 'gy'), split_axis=0, concat_axis=0, tiled=...  25.6 us
    all_to_all x1, blocking collectives, along_xy(): lax.all_to_all(message, ('gx', 'gy'), split_axis=0, concat_axis=0, tiled=...  22.1 us
    ppermute x2, starting transfers between devices, halo(): lax.ppermute(ylo, 'gy', down(ny))  6.8 us
    ppermute x2, starting transfers between devices, halo(): lax.ppermute(yhi, 'gy', up(ny))  6.16 us
    pallas_call x6, Pallas kernels, run(): pl.pallas_call(kernel, out_shape=[jax.ShapeDtypeStruct(s, F32) for s in o...  6.1 us
    unnamed x14, local copies, waits for them, and re-layouts  3.49 us
    ppermute x2, starting transfers between devices, halo(): lax.ppermute(xhi, 'gx', up(nx))  3.29 us
  transfers between devices with their start and end apart: 10, of which 4 were waited for; matrix products, arithmetic and copies ran while one was open for 0% of the time, Pallas kernels for 0%

commit v1 on v0

--- a/solution.py
+++ b/solution.py
@@ -74,9 +74,17 @@
 
 
 def begin_kernel(
-    sizes, r_ref, sigma_ref, kappa_ref, inv_ref,
-    jac_ref, dinv_ref, zmsg_ref, loc_ref, alpha_ref, spread_ref, *planes
+    sizes, r_hbm, sigma_hbm, kappa_hbm, inv_hbm,
+    jac_ref, dinv_ref, zmsg_ref, loc_ref, alpha_ref, spread_ref, xlo, xhi, ylo, yhi,
+    r_ref, sigma_ref, kappa_ref, inv_ref, sems
 ):
+    planes = (xlo, xhi, ylo, yhi)
+    pairs = ((kappa_hbm, kappa_ref), (sigma_hbm, sigma_ref), (r_hbm, r_ref), (inv_hbm, inv_ref))
+    copies = [pltpu.make_async_copy(a, b, sems.at[i]) for i, (a, b) in enumerate(pairs)]
+    for copy in copies:
+        copy.start()
+    for copy in copies:
+        copy.wait()
     r, sigma = r_ref[...], sigma_ref[...]
     kx, ky, kz = kappa_ref[0], kappa_ref[1], kappa_ref[2]
     dinv = WEIGHT / (sigma + 2.0 * (kx + ky + kz))
@@ -116,7 +124,7 @@
     write_z_message(zmsg_ref, rows, faces_of(jac), spread_inverse, jnp.sum(r), sizes)
 
 
-def chain_kernel(sizes, fresh, zrec_ref, loc_ref, alpha_ref, *refs):
+def chain_kernel(sizes, fresh, zrec_ref, loc_ref, alpha_ref, _, __, *refs):
     if fresh:
         xmsg_ref, own_ref, zhalo_ref, chain_ref, final_ref, sol_ref = refs
     else:
@@ -380,19 +388,18 @@
         res_ref[x] = r_ref[x] - y1 * w1_ref[x] - y2 * w2_ref[x]
 
 
-def call(kernel, out_shapes, scratch=(), name=None, **kw):
+def call(kernel, out_shapes, scratch=(), name=None, inputs=pltpu.VMEM, semaphores=(), limit=24 << 20):
     vmem = pl.BlockSpec(memory_space=pltpu.VMEM)
 
     def run(*args):
         return pl.pallas_call(
             kernel,
             out_shape=[jax.ShapeDtypeStruct(s, F32) for s in out_shapes],
-            in_specs=[vmem] * len(args),
+            in_specs=[pl.BlockSpec(memory_space=inputs)] * len(args),
             out_specs=[vmem] * len(out_shapes),
-            scratch_shapes=[pltpu.VMEM(s, F32) for s in scratch],
-            compiler_params=pltpu.CompilerParams(vmem_limit_bytes=24 * 1024 * 1024),
+            scratch_shapes=[pltpu.VMEM(s, F32) for s in scratch] + list(semaphores),
+            compiler_params=pltpu.CompilerParams(vmem_limit_bytes=limit),
             name=name,
-            **kw,
         )(*args)
 
     return run
@@ -423,13 +430,14 @@
 
     bind = lambda kernel, *a: functools.partial(kernel, sizes, *a)
     jac, dinv, zmsg, loc, alpha, spread, *sides = call(
-        bind(begin_kernel), [field, field, to_z, (3, *coarse), coarse, tile, *planes], name="begin"
+        bind(begin_kernel), [field, field, to_z, (3, *coarse), coarse, tile, *planes],
+        [field, field, (3, *field), tile], "begin", pltpu.HBM, [pltpu.SemaphoreType.DMA((4,))], 54875 << 10,
     )(r, sigma, kappa, inverse_rows)
     zrec = along_z(zmsg)
     halos = halo(sides)
     xmsg, own, zhalo, chain, final = call(
-        bind(chain_kernel, True), [to_xy, tile, tile, (4, nz, 128), tile], [coarse], name="lines_first"
-    )(zrec, loc, alpha)
+        bind(chain_kernel, True), [to_xy, tile, tile, (4, nz, 128), tile], [coarse], "lines_first"
+    )(zrec, loc, alpha, *halos[2:])
     xrec = along_xy(xmsg)
     z1, w1, zmsg, alpha, *sides = call(
         bind(first_kernel), [field, field, to_z, coarse, *planes], name="operator_first"
@@ -437,8 +445,8 @@
     zrec = along_z(zmsg)
     halos = halo(sides)
     xmsg, own, zhalo = call(
-        bind(chain_kernel, False), [to_xy, tile, tile], [coarse], name="lines_second"
-    )(zrec, loc, alpha, chain, final)
+        bind(chain_kernel, False), [to_xy, tile, tile], [coarse], "lines_second"
+    )(zrec, loc, alpha, *halos[2:], chain, final)
     xrec = along_xy(xmsg)
     z2, w2, sums = call(bind(second_kernel), [field, field, (1, 128)], name="operator_second")(
         r, w1, dinv, sigma, kappa, xrec, own, zhalo, *halos

time: 136 us -> 135 us (level)
  blocking collectives: 80.9 us -> 35.5 us
  waiting for transfers between devices: 2.58 us -> 25.1 us
  starting transfers between devices: 41.8 us -> 63.6 us
  local copies, waits for them, and re-layouts: 3.52 us -> 0.73 us
  Pallas kernels: 6.1 us -> 8.54 us
    all_to_all x3 -> x1, blocking collectives: 58.8 us -> 20.6 us  [along_z(): lax.all_to_all(message, 'gz', split_axis=0, concat_axis=0, tiled=True)]
    all_to_all x0 -> x2, starting transfers between devices: none -> 27.9 us  [along_z(): lax.all_to_all(message, 'gz', split_axis=0, concat_axis=0, tiled=True)]
    all_to_all x2, waiting for transfers between devices: 0.11 us -> 8.63 us  [along_xy(): lax.all_to_all(message, ('gx', 'gy'), split_axis=0, concat_axis=0, tiled=...]
    all_to_all x0 -> x2, waiting for transfers between devices: none -> 7.92 us  [along_z(): lax.all_to_all(message, 'gz', split_axis=0, concat_axis=0, tiled=True)]
    all_to_all x1, blocking collectives: 22.1 us -> 14.9 us  [along_xy(): lax.all_to_all(message, ('gx', 'gy'), split_axis=0, concat_axis=0, tiled=...]
    all_to_all x2, starting transfers between devices: 25.6 us -> 18.7 us  [along_xy(): lax.all_to_all(message, ('gx', 'gy'), split_axis=0, concat_axis=0, tiled=...]
    ppermute x2, waiting for transfers between devices: 0.01 us -> 5.25 us  [halo(): lax.ppermute(xlo, 'gx', down(nx))]
    unnamed x14 -> x10, local copies, waits for them, and re-layouts: 3.49 us -> 0.7 us
  transfers between devices with their start and end apart: 10 -> 12, of which waited for: 4 -> 10; matrix products, arithmetic and copies ran while one was open for 0% -> 0% of each run, Pallas kernels for 0% -> 0%
where the time goes in v1:
time: 135 us; the launch traced here: 134 us
  starting transfers between devices  63.6 us (47%)
  blocking collectives  35.5 us (26%)
  waiting for transfers between devices  25.1 us (19%)
  Pallas kernels  8.54 us (6%)
    all_to_all x2, starting transfers between devices, along_z(): lax.all_to_all(message, 'gz', split_axis=0, concat_axis=0, tiled=True)  27.9 us
    all_to_all x1, blocking collectives, along_z(): lax.all_to_all(message, 'gz', split_axis=0, concat_axis=0, tiled=True)  20.6 us
    all_to_all x2, starting transfers between devices, along_xy(): lax.all_to_all(message, ('gx', 'gy'), split_axis=0, concat_axis=0, tiled=...  18.7 us
    all_to_all x1, blocking collectives, along_xy(): lax.all_to_all(message, ('gx', 'gy'), split_axis=0, concat_axis=0, tiled=...  14.9 us
    all_to_all x2, waiting for transfers between devices, along_xy(): lax.all_to_all(message, ('gx', 'gy'), split_axis=0, concat_axis=0, tiled=...  8.63 us
    pallas_call x6, Pallas kernels, run(): pl.pallas_call(kernel, out_shape=[jax.ShapeDtypeStruct(s, F32) for s in o...  8.54 us
    all_to_all x2, waiting for transfers between devices, along_z(): lax.all_to_all(message, 'gz', split_axis=0, concat_axis=0, tiled=True)  7.92 us
    ppermute x2, starting transfers between devices, halo(): lax.ppermute(ylo, 'gy', down(ny))  7.72 us
  transfers between devices with their start and end apart: 12, of which 10 were waited for; matrix products, arithmetic and copies ran while one was open for 0% of the time, Pallas kernels for 0%

profile of v1, /device:TPU:1, one launch (start us, length us, event | category | flops | bytes accessed | tf_op | source)
XLA Modules:
  0.0 134.3 jit_solution(14512919168798500117)
XLA Ops:
  0.6 0.0 copy-start.4
  0.6 0.7 copy-done.4
  1.3 0.0 copy-start
  1.3 2.8 %begin.1 = (f32[8,32,128]{2,1,0:T(8,128)S(1)}, f32[8,32,128]{2,1,0:T(8,128)}, f32[16,8,128]{2,1,0:T(8,128)}, f32[3,16,128]{2,1,0:T(8,128)S(1)}, f32[16,128]{1,0:...) custom-call(f32[8,32,128]{2,1,0:T(8,128)} %r_ref.3, ...), custom_call_target="tpu_custom_call" | custom-call | tf_op jit(solution)/shard_map/begin/pallas_call | solution.py:395
  4.1 0.0 copy-start.3
  4.1 19.6 %all-to-all-start = ((f32[16,8,128]{2,1,0:T(8,128)}), f32[16,8,128]{2,1,0:T(8,128)S(1)}, u32[]{:S(2)}, u32[]{:S(2)}) async-start(f32[16,8,128]{2,1,0:T(8,128)} %get-tuple-element.33), calls=%async_computation | async-start | bytes 131072 | tf_op jit(solution)/shard_map/all_to_all | solution.py:426
  23.7 0.0 copy-start.1
  23.7 3.3 %collective-permute-start = (f32[8,128]{1,0:T(8,128)S(1)}, f32[8,128]{1,0:T(8,128)S(1)}, u32[]{:S(2)}, u32[]{:S(2)}) collective-permute-start(f32[8,128]{1,0:T(8,128)S(1)} %get-tuple-element.36), channel_id=1, source_target_pairs={{0,16},{16,32},{32,48},{48,64},{64,80},{80,96},{96,112},{112,0},{1... | collective-permute-start | bytes 12296 | tf_op jit(solution)/shard_map/ppermute | solution.py:421
  27.1 3.8 %collective-permute-start.1 = (f32[8,128]{1,0:T(8,128)S(1)}, f32[8,128]{1,0:T(8,128)S(1)}, u32[]{:S(2)}, u32[]{:S(2)}) collective-permute-start(f32[8,128]{1,0:T(8,128)S(1)} %get-tuple-element.37), channel_id=1, source_target_pairs={{16,0},{32,16},{48,32},{64,48},{80,64},{96,80},{112,96},{0,112},{1... | collective-permute-start | bytes 12296 | tf_op jit(solution)/shard_map/ppermute | solution.py:422
  30.9 0.0 collective-permute-done._.h2
  30.9 0.8 collective-permute-done.1.__.h3
  31.7 3.6 %all-to-all-done.zrec_ref = f32[16,8,128]{2,1,0:T(8,128)S(1)} async-done(((f32[16,8,128]{2,1,0:T(8,128)}), f32[16,8,128]{2,1,0:T(8,128)S(1)}, u32[]{:S(2)}, u32[]{:S(2)}) %all-to-all-start) | async-done | bytes 65568 | tf_op jit(solution)/shard_map/all_to_all | solution.py:426
  35.3 1.3 lines_first.1
  36.6 12.2 %all-to-all-start.1 = ((f32[64,2,128]{2,1,0:T(2,128)}), f32[64,2,128]{2,1,0:T(2,128)S(1)}, u32[]{:S(2)}, u32[]{:S(2)}) async-start(f32[64,2,128]{2,1,0:T(2,128)} %get-tuple-element.38), calls=%async_computation.1 | async-start | bytes 131072 | tf_op jit(solution)/shard_map/all_to_all | solution.py:429
  48.8 1.6 %collective-permute-start.2 = (f32[32,128]{1,0:T(8,128)S(1)}, f32[32,128]{1,0:T(8,128)S(1)}, u32[]{:S(2)}, u32[]{:S(2)}) collective-permute-start(f32[32,128]{1,0:T(8,128)S(1)} %get-tuple-element.41), channel_id=1, source_target_pairs={{0,128},{128,256},{256,384},{384,512},{512,640},{640,768},{768,896... | collective-permute-start | bytes 49160 | tf_op jit(solution)/shard_map/ppermute | solution.py:419
  50.5 0.0 collective-permute-start.3
  50.5 0.9 collective-permute-done.2.h0
  51.3 2.6 %collective-permute-done.3.h1 = f32[32,128]{1,0:T(8,128)S(1)} collective-permute-done((f32[32,128]{1,0:T(8,128)S(1)}, f32[32,128]{1,0:T(8,128)S(1)}, u32[]{:S(2)}, u32[]{:S(2)}) %collective-permute-start.3) | collective-permute-done | bytes 16416 | tf_op jit(solution)/shard_map/ppermute | solution.py:420
  54.0 4.3 %all-to-all-done.1.xrec_ref = f32[64,2,128]{2,1,0:T(2,128)S(1)} async-done(((f32[64,2,128]{2,1,0:T(2,128)}), f32[64,2,128]{2,1,0:T(2,128)S(1)}, u32[]{:S(2)}, u32[]{:S(2)}) %all-to-all-start.1) | async-done | bytes 65568 | tf_op jit(solution)/shard_map/all_to_all | solution.py:429
  58.3 0.0 copy-done
  58.3 0.0 copy-done.3
  58.3 0.0 copy-done.1
  58.3 1.7 %operator_first.1 = (f32[8,32,128]{2,1,0:T(8,128)S(1)}, f32[8,32,128]{2,1,0:T(8,128)S(1)}, f32[16,8,128]{2,1,0:T(8,128)}, f32[16,128]{1,0:T(8,128)S(1)}, f32[32,...) custom-call(f32[8,32,128]{2,1,0:T(8,128)S(1)} %get-tuple-element.31.jac_ref, ...), custom_call_target="tpu_custom_call" | custom-call | tf_op jit(solution)/shard_map/operator_first/pallas_call | solution.py:395
  60.0 8.4 %all-to-all-start.2 = ((f32[16,8,128]{2,1,0:T(8,128)}), f32[16,8,128]{2,1,0:T(8,128)S(1)}, u32[]{:S(2)}, u32[]{:S(2)}) async-start(f32[16,8,128]{2,1,0:T(8,128)} %get-tuple-element.45), calls=%async_computation.2 | async-start | bytes 131072 | tf_op jit(solution)/shard_map/all_to_all | solution.py:426
  68.4 2.6 %collective-permute-start.4 = (f32[8,128]{1,0:T(8,128)S(1)}, f32[8,128]{1,0:T(8,128)S(1)}, u32[]{:S(2)}, u32[]{:S(2)}) collective-permute-start(f32[8,128]{1,0:T(8,128)S(1)} %get-tuple-element.47), channel_id=1, source_target_pairs={{0,16},{16,32},{32,48},{48,64},{64,80},{80,96},{96,112},{112,0},{1... | collective-permute-start | bytes 12296 | tf_op jit(solution)/shard_map/ppermute | solution.py:421
  71.0 3.9 %collective-permute-start.5 = (f32[8,128]{1,0:T(8,128)S(1)}, f32[8,128]{1,0:T(8,128)S(1)}, u32[]{:S(2)}, u32[]{:S(2)}) collective-permute-start(f32[8,128]{1,0:T(8,128)S(1)} %get-tuple-element.48), channel_id=1, source_target_pairs={{16,0},{32,16},{48,32},{64,48},{80,64},{96,80},{112,96},{0,112},{1... | collective-permute-start | bytes 12296 | tf_op jit(solution)/shard_map/ppermute | solution.py:422
  74.9 0.0 collective-permute-done.4._.h2
  74.9 0.7 collective-permute-done.5.__.h3
  75.6 4.4 %all-to-all-done.2.zrec_ref = f32[16,8,128]{2,1,0:T(8,128)S(1)} async-done(((f32[16,8,128]{2,1,0:T(8,128)}), f32[16,8,128]{2,1,0:T(8,128)S(1)}, u32[]{:S(2)}, u32[]{:S(2)}) %all-to-all-start.2) | async-done | bytes 65568 | tf_op jit(solution)/shard_map/all_to_all | solution.py:426
  80.0 0.0 copy-start.2
  80.0 1.1 lines_second.1
  81.1 6.5 %all-to-all-start.3 = ((f32[64,2,128]{2,1,0:T(2,128)}), f32[64,2,128]{2,1,0:T(2,128)S(1)}, u32[]{:S(2)}, u32[]{:S(2)}) async-start(f32[64,2,128]{2,1,0:T(2,128)} %get-tuple-element.51), calls=%async_computation.3 | async-start | bytes 131072 | tf_op jit(solution)/shard_map/all_to_all | solution.py:429
  87.6 1.7 %collective-permute-start.6 = (f32[32,128]{1,0:T(8,128)S(1)}, f32[32,128]{1,0:T(8,128)S(1)}, u32[]{:S(2)}, u32[]{:S(2)}) collective-permute-start(f32[32,128]{1,0:T(8,128)S(1)} %get-tuple-element.54), channel_id=1, source_target_pairs={{0,128},{128,256},{256,384},{384,512},{512,640},{640,768},{768,896... | collective-permute-start | bytes 49160 | tf_op jit(solution)/shard_map/ppermute | solution.py:419
  89.3 0.0 collective-permute-start.7
  89.3 0.9 collective-permute-done.6.h0
  90.2 2.6 %collective-permute-done.7.h1 = f32[32,128]{1,0:T(8,128)S(1)} collective-permute-done((f32[32,128]{1,0:T(8,128)S(1)}, f32[32,128]{1,0:T(8,128)S(1)}, u32[]{:S(2)}, u32[]{:S(2)}) %collective-permute-start.7) | collective-permute-done | bytes 16416 | tf_op jit(solution)/shard_map/ppermute | solution.py:420
  92.8 4.3 %all-to-all-done.3.xrec_ref = f32[64,2,128]{2,1,0:T(2,128)S(1)} async-done(((f32[64,2,128]{2,1,0:T(2,128)}), f32[64,2,128]{2,1,0:T(2,128)S(1)}, u32[]{:S(2)}, u32[]{:S(2)}) %all-to-all-start.3) | async-done | bytes 65568 | tf_op jit(solution)/shard_map/all_to_all | solution.py:429
  97.1 0.0 copy-done.2
  97.1 0.7 operator_second.1
  97.8 20.6 %all_to_all.30 = f32[16,1,128]{2,1,0:T(1,128)S(1)} all-to-all(f32[16,1,128]{2,1,0:T(1,128)S(1)} %broadcast_in_dim.7), channel_id=1, replica_groups=mesh['gx'=8,'gy'=8,'gz'=16] {'gz'}, dimensions={0} | all-to-all | bytes 16384 | tf_op jit(solution)/shard_map/all_to_all | solution.py:426
  118.5 14.9 %all_to_all.31.all_ref = f32[64,1,128]{2,1,0:T(1,128)S(1)} all-to-all(f32[64,1,128]{2,1,0:T(1,128)S(1)} %broadcast_in_dim.16), channel_id=1, replica_groups=mesh['gx'=8,'gy'=8,'gz'=16] {'gx','gy'}, dimensions={0} | all-to-all | bytes 65536 | tf_op jit(solution)/shard_map/all_to_all | solution.py:429
  133.4 0.9 end.1
  (3 shorter events, 0.0 us)
Async XLA Ops:
  0.6 0.7 copy-start.4
  1.3 57.0 %copy-start = (f32[3,8,32,128]{3,2,1,0:T(8,128)S(1)}, f32[3,8,32,128]{3,2,1,0:T(8,128)}, u32[]{:S(2)}) copy-start(f32[3,8,32,128]{3,2,1,0:T(8,128)} %kappa_ref.3) | copy-start | bytes 1179652
  4.1 54.1 %copy-start.3 = (f32[8,32,128]{2,1,0:T(8,128)S(1)}, f32[8,32,128]{2,1,0:T(8,128)}, u32[]{:S(2)}) copy-start(f32[8,32,128]{2,1,0:T(8,128)} %get-tuple-element.32.dinv_ref) | copy-start | bytes 393220
  4.1 31.1 %all-to-all-start = ((f32[16,8,128]{2,1,0:T(8,128)}), f32[16,8,128]{2,1,0:T(8,128)S(1)}, u32[]{:S(2)}, u32[]{:S(2)}) async-start(f32[16,8,128]{2,1,0:T(8,128)} %get-tuple-element.33), calls=%async_computation | async-start | bytes 131072 | tf_op jit(solution)/shard_map/all_to_all | solution.py:426
  23.7 34.6 %copy-start.1 = (f32[8,32,128]{2,1,0:T(8,128)S(1)}, f32[8,32,128]{2,1,0:T(8,128)}, u32[]{:S(2)}) copy-start(f32[8,32,128]{2,1,0:T(8,128)} %sigma_ref.3) | copy-start | bytes 393220
  23.7 7.2 %collective-permute-start = (f32[8,128]{1,0:T(8,128)S(1)}, f32[8,128]{1,0:T(8,128)S(1)}, u32[]{:S(2)}, u32[]{:S(2)}) collective-permute-start(f32[8,128]{1,0:T(8,128)S(1)} %get-tuple-element.36), channel_id=1, source_target_pairs={{0,16},{16,32},{32,48},{48,64},{64,80},{80,96},{96,112},{112,0},{1... | collective-permute-start | bytes 12296 | tf_op jit(solution)/shard_map/ppermute | solution.py:421
  27.1 4.6 %collective-permute-start.1 = (f32[8,128]{1,0:T(8,128)S(1)}, f32[8,128]{1,0:T(8,128)S(1)}, u32[]{:S(2)}, u32[]{:S(2)}) collective-permute-start(f32[8,128]{1,0:T(8,128)S(1)} %get-tuple-element.37), channel_id=1, source_target_pairs={{16,0},{32,16},{48,32},{64,48},{80,64},{96,80},{112,96},{0,112},{1... | collective-permute-start | bytes 12296 | tf_op jit(solution)/shard_map/ppermute | solution.py:422
  36.6 21.7 %all-to-all-start.1 = ((f32[64,2,128]{2,1,0:T(2,128)}), f32[64,2,128]{2,1,0:T(2,128)S(1)}, u32[]{:S(2)}, u32[]{:S(2)}) async-start(f32[64,2,128]{2,1,0:T(2,128)} %get-tuple-element.38), calls=%async_computation.1 | async-start | bytes 131072 | tf_op jit(solution)/shard_map/all_to_all | solution.py:429
  48.8 2.5 %collective-permute-start.2 = (f32[32,128]{1,0:T(8,128)S(1)}, f32[32,128]{1,0:T(8,128)S(1)}, u32[]{:S(2)}, u32[]{:S(2)}) collective-permute-start(f32[32,128]{1,0:T(8,128)S(1)} %get-tuple-element.41), channel_id=1, source_target_pairs={{0,128},{128,256},{256,384},{384,512},{512,640},{640,768},{768,896... | collective-permute-start | bytes 49160 | tf_op jit(solution)/shard_map/ppermute | solution.py:419
  50.5 3.5 %collective-permute-start.3 = (f32[32,128]{1,0:T(8,128)S(1)}, f32[32,128]{1,0:T(8,128)S(1)}, u32[]{:S(2)}, u32[]{:S(2)}) collective-permute-start(f32[32,128]{1,0:T(8,128)S(1)} %get-tuple-element.42), channel_id=1, source_target_pairs={{128,0},{256,128},{384,256},{512,384},{640,512},{768,640},{896,768... | collective-permute-start | bytes 49160 | tf_op jit(solution)/shard_map/ppermute | solution.py:420
  60.0 20.0 %all-to-all-start.2 = ((f32[16,8,128]{2,1,0:T(8,128)}), f32[16,8,128]{2,1,0:T(8,128)S(1)}, u32[]{:S(2)}, u32[]{:S(2)}) async-start(f32[16,8,128]{2,1,0:T(8,128)} %get-tuple-element.45), calls=%async_computation.2 | async-start | bytes 131072 | tf_op jit(solution)/shard_map/all_to_all | solution.py:426
  68.4 6.5 %collective-permute-start.4 = (f32[8,128]{1,0:T(8,128)S(1)}, f32[8,128]{1,0:T(8,128)S(1)}, u32[]{:S(2)}, u32[]{:S(2)}) collective-permute-start(f32[8,128]{1,0:T(8,128)S(1)} %get-tuple-element.47), channel_id=1, source_target_pairs={{0,16},{16,32},{32,48},{48,64},{64,80},{80,96},{96,112},{112,0},{1... | collective-permute-start | bytes 12296 | tf_op jit(solution)/shard_map/ppermute | solution.py:421
  71.0 4.6 %collective-permute-start.5 = (f32[8,128]{1,0:T(8,128)S(1)}, f32[8,128]{1,0:T(8,128)S(1)}, u32[]{:S(2)}, u32[]{:S(2)}) collective-permute-start(f32[8,128]{1,0:T(8,128)S(1)} %get-tuple-element.48), channel_id=1, source_target_pairs={{16,0},{32,16},{48,32},{64,48},{80,64},{96,80},{112,96},{0,112},{1... | collective-permute-start | bytes 12296 | tf_op jit(solution)/shard_map/ppermute | solution.py:422
  80.0 17.1 %copy-start.2 = (f32[8,32,128]{2,1,0:T(8,128)S(1)}, f32[8,32,128]{2,1,0:T(8,128)}, u32[]{:S(2)}) copy-start(f32[8,32,128]{2,1,0:T(8,128)} %r_ref.3) | copy-start | bytes 393220
  81.1 16.0 %all-to-all-start.3 = ((f32[64,2,128]{2,1,0:T(2,128)}), f32[64,2,128]{2,1,0:T(2,128)S(1)}, u32[]{:S(2)}, u32[]{:S(2)}) async-start(f32[64,2,128]{2,1,0:T(2,128)} %get-tuple-element.51), calls=%async_computation.3 | async-start | bytes 131072 | tf_op jit(solution)/shard_map/all_to_all | solution.py:429
  87.6 2.6 %collective-permute-start.6 = (f32[32,128]{1,0:T(8,128)S(1)}, f32[32,128]{1,0:T(8,128)S(1)}, u32[]{:S(2)}, u32[]{:S(2)}) collective-permute-start(f32[32,128]{1,0:T(8,128)S(1)} %get-tuple-element.54), channel_id=1, source_target_pairs={{0,128},{128,256},{256,384},{384,512},{512,640},{640,768},{768,896... | collective-permute-start | bytes 49160 | tf_op jit(solution)/shard_map/ppermute | solution.py:419
  89.3 3.5 %collective-permute-start.7 = (f32[32,128]{1,0:T(8,128)S(1)}, f32[32,128]{1,0:T(8,128)S(1)}, u32[]{:S(2)}, u32[]{:S(2)}) collective-permute-start(f32[32,128]{1,0:T(8,128)S(1)} %get-tuple-element.55), channel_id=1, source_target_pairs={{128,0},{256,128},{384,256},{512,384},{640,512},{768,640},{896,768... | collective-permute-start | bytes 49160 | tf_op jit(solution)/shard_map/ppermute | solution.py:420

commit v2 on v1

--- a/solution.py
+++ b/solution.py
@@ -66,19 +66,21 @@
 
 
 def write_planes(field, planes):
-    xlo, xhi, ylo, yhi = planes
-    xlo[...] = field[0]
-    xhi[...] = field[CX - 1]
-    ylo[...] = field[:, 0, :]
-    yhi[...] = field[:, CY - 1, :]
+    x_in, x_out, y_in, y_out = planes
+    even_x, even_y = lax.axis_index("gx") % 2 == 0, lax.axis_index("gy") % 2 == 0
+    low, high = field[0], field[CX - 1]
+    x_in[...] = jnp.where(even_x, high, low)
+    x_out[...] = jnp.where(even_x, low, high)
+    low, high = field[:, 0, :], field[:, CY - 1, :]
+    y_in[...] = jnp.where(even_y, high, low)
+    y_out[...] = jnp.where(even_y, low, high)
 
 
 def begin_kernel(
     sizes, r_hbm, sigma_hbm, kappa_hbm, inv_hbm,
-    jac_ref, dinv_ref, zmsg_ref, loc_ref, alpha_ref, spread_ref, xlo, xhi, ylo, yhi,
+    zmsg_ref, loc_ref, alpha_ref, spread_ref, x_in, x_out, y_in, y_out,
     r_ref, sigma_ref, kappa_ref, inv_ref, sems
 ):
-    planes = (xlo, xhi, ylo, yhi)
     pairs = ((kappa_hbm, kappa_ref), (sigma_hbm, sigma_ref), (r_hbm, r_ref), (inv_hbm, inv_ref))
     copies = [pltpu.make_async_copy(a, b, sems.at[i]) for i, (a, b) in enumerate(pairs)]
     for copy in copies:
@@ -87,11 +89,8 @@
         copy.wait()
     r, sigma = r_ref[...], sigma_ref[...]
     kx, ky, kz = kappa_ref[0], kappa_ref[1], kappa_ref[2]
-    dinv = WEIGHT / (sigma + 2.0 * (kx + ky + kz))
-    jac = dinv * r
-    dinv_ref[...] = dinv
-    jac_ref[...] = jac
-    write_planes(jac, planes)
+    jac = r * (WEIGHT / (sigma + 2.0 * (kx + ky + kz)))
+    write_planes(jac, (x_in, x_out, y_in, y_out))
     unused = iota((CELLS, 128), 1) >= LINES
     e = jnp.where(unused, 1.0, lines_of(sigma))
     g = jnp.where(unused, 1.0, lines_of(kz) * 0.125)
@@ -124,7 +123,7 @@
     write_z_message(zmsg_ref, rows, faces_of(jac), spread_inverse, jnp.sum(r), sizes)
 
 
-def chain_kernel(sizes, fresh, zrec_ref, loc_ref, alpha_ref, _, __, *refs):
+def chain_kernel(sizes, fresh, zrec_ref, loc_ref, alpha_ref, h0, h1, h2, h3, *refs):
     if fresh:
         xmsg_ref, own_ref, zhalo_ref, chain_ref, final_ref, sol_ref = refs
     else:
@@ -269,6 +268,10 @@
         xmsg_ref[here + 1, 0:1, :] = y_high
 
 
+def scale(sigma_ref, kappa_ref, x):
+    return WEIGHT / (sigma_ref[x] + 2.0 * (kappa_ref[0, x] + kappa_ref[1, x] + kappa_ref[2, x]))
+
+
 def operator(sizes, base, sigma_ref, kappa_ref, xrec_ref, own_ref, zhalo_ref, halos, z_ref, w_ref):
     nx, ny, nz = sizes
     mx, my, mz = lax.axis_index("gx"), lax.axis_index("gy"), lax.axis_index("gz")
@@ -297,11 +300,14 @@
     )
     to_cells = one_where(iota((128, 128), 0) % 16 == iota((128, 128), 1) // 8)
     lines = dot(rows, to_cells)
-    xlo, xhi, ylo, yhi = halos
-    xlo = jnp.where(mx > 0, xlo[...] + lines[64:96] + c_xlo, 0.0)
-    xhi = jnp.where(mx < nx - 1, xhi[...] + lines[96:128] + c_xhi, 0.0)
-    ylo = jnp.where(my > 0, ylo[...] + lines[128:136] + c_ylo, 0.0)
-    yhi = jnp.where(my < ny - 1, yhi[...] + lines[136:144] + c_yhi, 0.0)
+    x_in, x_out, y_in, y_out = [h[...] for h in halos]
+    even_x, even_y = mx % 2 == 0, my % 2 == 0
+    xlo, xhi = jnp.where(even_x, x_out, x_in), jnp.where(even_x, x_in, x_out)
+    ylo, yhi = jnp.where(even_y, y_out, y_in), jnp.where(even_y, y_in, y_out)
+    xlo = jnp.where(mx > 0, xlo + lines[64:96] + c_xlo, 0.0)
+    xhi = jnp.where(mx < nx - 1, xhi + lines[96:128] + c_xhi, 0.0)
+    ylo = jnp.where(my > 0, ylo + lines[128:136] + c_ylo, 0.0)
+    yhi = jnp.where(my < ny - 1, yhi + lines[136:144] + c_yhi, 0.0)
     face = zhalo_ref[...]
     high = jnp.where(mz > 0, face + c_zlo, 0.0)
     low = jnp.where(mz < nz - 1, face + c_zhi, 0.0)
@@ -336,13 +342,14 @@
 
 
 def first_kernel(
-    sizes, jac_ref, dinv_ref, sigma_ref, kappa_ref, xrec_ref, own_ref, zhalo_ref, h0, h1, h2, h3,
+    sizes, r_ref, sigma_ref, kappa_ref, xrec_ref, own_ref, zhalo_ref, h0, h1, h2, h3,
     loc_ref, spread_ref, z_ref, w_ref, zmsg_ref, alpha_ref, *planes
 ):
-    base = lambda x: jac_ref[x]
+    scales = [scale(sigma_ref, kappa_ref, x) for x in range(CX)]
+    base = lambda x: scales[x] * r_ref[x]
     operator(sizes, base, sigma_ref, kappa_ref, xrec_ref, own_ref, zhalo_ref, (h0, h1, h2, h3), z_ref, w_ref)
     field = w_ref[...]
-    jac = dinv_ref[...] * field
+    jac = jnp.stack([scales[x] * w_ref[x] for x in range(CX)], axis=0)
     write_planes(jac, planes)
     rhs = lines_of(field)
     row = lambda a, k: a[k : k + 1, :]
@@ -360,10 +367,10 @@
 
 
 def second_kernel(
-    sizes, r_ref, w1_ref, dinv_ref, sigma_ref, kappa_ref, xrec_ref, own_ref, zhalo_ref, h0, h1, h2, h3,
+    sizes, r_ref, w1_ref, sigma_ref, kappa_ref, xrec_ref, own_ref, zhalo_ref, h0, h1, h2, h3,
     z_ref, w_ref, sums_ref
 ):
-    base = lambda x: dinv_ref[x] * w1_ref[x]
+    base = lambda x: scale(sigma_ref, kappa_ref, x) * w1_ref[x]
     operator(sizes, base, sigma_ref, kappa_ref, xrec_ref, own_ref, zhalo_ref, (h0, h1, h2, h3), z_ref, w_ref)
     w1, w2, r = w1_ref[...], w_ref[...], r_ref[...]
     lane = iota((1, 128), 1)
@@ -411,15 +418,17 @@
     planes = [plane, plane, tile, tile]
     to_z, to_xy = (nz, 8, 128), (nx * ny, 2, 128)
 
+    def swaps(n, first):
+        pairs = [(i, i + 1) for i in range(first, n - 1, 2)]
+        return pairs + [(b, a) for a, b in pairs]
+
     def halo(parts):
-        xlo, xhi, ylo, yhi = parts
-        up = lambda n: [(i, (i + 1) % n) for i in range(n)]
-        down = lambda n: [((i + 1) % n, i) for i in range(n)]
+        x_in, x_out, y_in, y_out = parts
         return (
-            lax.ppermute(xhi, "gx", up(nx)),
-            lax.ppermute(xlo, "gx", down(nx)),
-            lax.ppermute(yhi, "gy", up(ny)),
-            lax.ppermute(ylo, "gy", down(ny)),
+            lax.ppermute(x_in, "gx", swaps(nx, 0)),
+            lax.ppermute(x_out, "gx", swaps(nx, 1)),
+            lax.ppermute(y_in, "gy", swaps(ny, 0)),
+            lax.ppermute(y_out, "gy", swaps(ny, 1)),
         )
 
     def along_z(message):
@@ -429,27 +438,27 @@
         return lax.all_to_all(message, ("gx", "gy"), split_axis=0, concat_axis=0, tiled=True)
 
     bind = lambda kernel, *a: functools.partial(kernel, sizes, *a)
-    jac, dinv, zmsg, loc, alpha, spread, *sides = call(
-        bind(begin_kernel), [field, field, to_z, (3, *coarse), coarse, tile, *planes],
-        [field, field, (3, *field), tile], "begin", pltpu.HBM, [pltpu.SemaphoreType.DMA((4,))], 54875 << 10,
+    zmsg, loc, alpha, spread, *sides = call(
+        bind(begin_kernel), [to_z, (3, *coarse), coarse, tile, *planes],
+        [field, field, (3, *field), tile], "begin", pltpu.HBM, [pltpu.SemaphoreType.DMA((4,))], 55100 << 10,
     )(r, sigma, kappa, inverse_rows)
     zrec = along_z(zmsg)
     halos = halo(sides)
     xmsg, own, zhalo, chain, final = call(
         bind(chain_kernel, True), [to_xy, tile, tile, (4, nz, 128), tile], [coarse], "lines_first"
-    )(zrec, loc, alpha, *halos[2:])
+    )(zrec, loc, alpha, *halos)
     xrec = along_xy(xmsg)
     z1, w1, zmsg, alpha, *sides = call(
         bind(first_kernel), [field, field, to_z, coarse, *planes], name="operator_first"
-    )(jac, dinv, sigma, kappa, xrec, own, zhalo, *halos, loc, spread)
+    )(r, sigma, kappa, xrec, own, zhalo, *halos, loc, spread)
     zrec = along_z(zmsg)
     halos = halo(sides)
     xmsg, own, zhalo = call(
         bind(chain_kernel, False), [to_xy, tile, tile], [coarse], "lines_second"
-    )(zrec, loc, alpha, *halos[2:], chain, final)
+    )(zrec, loc, alpha, *halos, chain, final)
     xrec = along_xy(xmsg)
     z2, w2, sums = call(bind(second_kernel), [field, field, (1, 128)], name="operator_second")(
-        r, w1, dinv, sigma, kappa, xrec, own, zhalo, *halos
+        r, w1, sigma, kappa, xrec, own, zhalo, *halos
     )
     sums = jnp.sum(along_z(jnp.broadcast_to(sums[None], (nz, 1, 128))), axis=0)
     sums = along_xy(jnp.broadcast_to(sums[None], (nx * ny, 1, 128)))

time: 135 us -> 142 us (1.052)
  blocking collectives: 35.5 us -> 78.1 us
  waiting for transfers between devices: 25.1 us -> 4.91 us
  starting transfers between devices: 63.6 us -> 49.3 us
    all_to_all x1 -> x3, blocking collectives: 14.9 us -> 55.3 us  [along_xy(): lax.all_to_all(message, ('gx', 'gy'), split_axis=0, concat_axis=0, tiled=...]
    all_to_all x2 -> x0, starting transfers between devices: 18.7 us -> none  [along_xy(): lax.all_to_all(message, ('gx', 'gy'), split_axis=0, concat_axis=0, tiled=...]
    all_to_all x2 -> x0, waiting for transfers between devices: 8.63 us -> none  [along_xy(): lax.all_to_all(message, ('gx', 'gy'), split_axis=0, concat_axis=0, tiled=...]
    ppermute x8, waiting for transfers between devices: 8.52 us -> 2.32 us  [the longest x2 2.3 us: halo(): lax.ppermute(y_in, 'gy', swaps(ny, 0))]
    all_to_all x2, waiting for transfers between devices: 7.92 us -> 2.59 us  [along_z(): lax.all_to_all(message, 'gz', split_axis=0, concat_axis=0, tiled=True)]
    all_to_all x2, starting transfers between devices: 27.9 us -> 31.2 us  [along_z(): lax.all_to_all(message, 'gz', split_axis=0, concat_axis=0, tiled=True)]
    all_to_all x1, blocking collectives: 20.6 us -> 22.8 us  [along_z(): lax.all_to_all(message, 'gz', split_axis=0, concat_axis=0, tiled=True)]
  transfers between devices with their start and end apart: 12 -> 10, of which waited for: 10 -> 4; matrix products, arithmetic and copies ran while one was open for 0% -> 0% of each run, Pallas kernels for 0% -> 0%
where the time goes in v2:
time: 142 us; the launch traced here: 141 us
  blocking collectives  78.1 us (55%)
  starting transfers between devices  49.3 us (35%)
  Pallas kernels  7.33 us (5%)
  waiting for transfers between devices  4.91 us (3%)
    all_to_all x3, blocking collectives, along_xy(): lax.all_to_all(message, ('gx', 'gy'), split_axis=0, concat_axis=0, tiled=...  55.3 us
    all_to_all x2, starting transfers between devices, along_z(): lax.all_to_all(message, 'gz', split_axis=0, concat_axis=0, tiled=True)  31.2 us
    all_to_all x1, blocking collectives, along_z(): lax.all_to_all(message, 'gz', split_axis=0, concat_axis=0, tiled=True)  22.8 us
    pallas_call x6, Pallas kernels, run(): pl.pallas_call(kernel, out_shape=[jax.ShapeDtypeStruct(s, F32) for s in o...  7.33 us
    ppermute x2, starting transfers between devices, halo(): lax.ppermute(x_in, 'gx', swaps(nx, 0))  6 us
    ppermute x2, starting transfers between devices, halo(): lax.ppermute(y_in, 'gy', swaps(ny, 0))  5.63 us
    ppermute x2, starting transfers between devices, halo(): lax.ppermute(x_out, 'gx', swaps(nx, 1))  5.22 us
  transfers between devices with their start and end apart: 10, of which 4 were waited for; matrix products, arithmetic and copies ran while one was open for 0% of the time, Pallas kernels for 0%

profile of v2, /device:TPU:1, one launch (start us, length us, event | category | flops | bytes accessed | tf_op | source)
XLA Modules:
  0.0 141.2 jit_solution(870072475626707623)
XLA Ops:
  0.6 0.0 copy-start.3
  0.6 0.7 copy-done.3
  1.3 0.0 copy-start
  1.3 2.8 %begin.1 = (f32[16,8,128]{2,1,0:T(8,128)}, f32[3,16,128]{2,1,0:T(8,128)S(1)}, f32[16,128]{1,0:T(8,128)S(1)}, f32[8,128]{1,0:T(8,128)S(1)}, f32[32,128]{1,0:T(8,1...) custom-call(f32[8,32,128]{2,1,0:T(8,128)} %r_ref.5, f32[8,32,128]{2,1,0:T(8,128)} %sigma_ref.3, ...), custom_call_target="tpu_custom_call" | custom-call | tf_op jit(solution)/shard_map/begin/pallas_call | solution.py:402
  4.1 19.4 %all-to-all-start = ((f32[16,8,128]{2,1,0:T(8,128)}), f32[16,8,128]{2,1,0:T(8,128)S(1)}, u32[]{:S(2)}, u32[]{:S(2)}) async-start(f32[16,8,128]{2,1,0:T(8,128)} %get-tuple-element.29), calls=%async_computation | async-start | bytes 131072 | tf_op jit(solution)/shard_map/all_to_all | solution.py:435
  23.6 2.9 %collective-permute-start = (f32[32,128]{1,0:T(8,128)S(1)}, f32[32,128]{1,0:T(8,128)S(1)}, u32[]{:S(2)}, u32[]{:S(2)}) collective-permute-start(f32[32,128]{1,0:T(8,128)S(1)} %get-tuple-element.32), channel_id=1, source_target_pairs={{0,128},{256,384},{512,640},{768,896},{128,0},{384,256},{640,512},... | collective-permute-start | bytes 49160 | tf_op jit(solution)/shard_map/ppermute | solution.py:428
  26.4 3.0 %collective-permute-start.1 = (f32[32,128]{1,0:T(8,128)S(1)}, f32[32,128]{1,0:T(8,128)S(1)}, u32[]{:S(2)}, u32[]{:S(2)}) collective-permute-start(f32[32,128]{1,0:T(8,128)S(1)} %get-tuple-element.33), channel_id=1, source_target_pairs={{128,256},{384,512},{640,768},{256,128},{512,384},{768,640},{129,2... | collective-permute-start | bytes 49160 | tf_op jit(solution)/shard_map/ppermute | solution.py:429
  29.5 3.2 %collective-permute-start.2 = (f32[8,128]{1,0:T(8,128)S(1)}, f32[8,128]{1,0:T(8,128)S(1)}, u32[]{:S(2)}, u32[]{:S(2)}) collective-permute-start(f32[8,128]{1,0:T(8,128)S(1)} %get-tuple-element.34), channel_id=1, source_target_pairs={{0,16},{32,48},{64,80},{96,112},{16,0},{48,32},{80,64},{112,96},{1... | collective-permute-start | bytes 12296 | tf_op jit(solution)/shard_map/ppermute | solution.py:430
  32.7 0.7 collective-permute-start.3
  33.4 0.8 collective-permute-done.2.h2
  34.1 0.0 collective-permute-done.3.h3
  34.1 0.0 collective-permute-done.h0
  34.1 0.0 collective-permute-done.1.h1
  34.1 1.0 all-to-all-done.zrec_ref
  35.1 0.0 copy-start.1
  35.1 0.0 copy-start.2
  35.1 0.7 lines_first.1
  35.8 22.6 %all_to_all.30.xrec_ref = f32[64,2,128]{2,1,0:T(2,128)S(1)} all-to-all(f32[64,2,128]{2,1,0:T(2,128)S(1)} %get-tuple-element.36), channel_id=1, replica_groups=mesh['gx'=8,'gy'=8,'gz'=16] {'gx','gy'}, dimensions={0} | all-to-all | bytes 131072 | tf_op jit(solution)/shard_map/all_to_all | solution.py:438
  58.4 0.0 copy-done
  58.4 0.0 copy-done.1
  58.4 0.0 copy-done.2
  58.4 1.8 %operator_first.1 = (f32[8,32,128]{2,1,0:T(8,128)S(1)}, f32[8,32,128]{2,1,0:T(8,128)S(1)}, f32[16,8,128]{2,1,0:T(8,128)}, f32[16,128]{1,0:T(8,128)S(1)}, f32[32,...) custom-call(f32[8,32,128]{2,1,0:T(8,128)S(1)} %copy-done.1, ...), custom_call_target="tpu_custom_call" | custom-call | tf_op jit(solution)/shard_map/operator_first/pallas_call | solution.py:402
  60.2 11.7 %all-to-all-start.2 = ((f32[16,8,128]{2,1,0:T(8,128)}), f32[16,8,128]{2,1,0:T(8,128)S(1)}, u32[]{:S(2)}, u32[]{:S(2)}) async-start(f32[16,8,128]{2,1,0:T(8,128)} %get-tuple-element.41), calls=%async_computation.2 | async-start | bytes 131072 | tf_op jit(solution)/shard_map/all_to_all | solution.py:435
  71.9 3.1 %collective-permute-start.4 = (f32[32,128]{1,0:T(8,128)S(1)}, f32[32,128]{1,0:T(8,128)S(1)}, u32[]{:S(2)}, u32[]{:S(2)}) collective-permute-start(f32[32,128]{1,0:T(8,128)S(1)} %get-tuple-element.43), channel_id=1, source_target_pairs={{0,128},{256,384},{512,640},{768,896},{128,0},{384,256},{640,512},... | collective-permute-start | bytes 49160 | tf_op jit(solution)/shard_map/ppermute | solution.py:428
  75.1 2.2 %collective-permute-start.5 = (f32[32,128]{1,0:T(8,128)S(1)}, f32[32,128]{1,0:T(8,128)S(1)}, u32[]{:S(2)}, u32[]{:S(2)}) collective-permute-start(f32[32,128]{1,0:T(8,128)S(1)} %get-tuple-element.44), channel_id=1, source_target_pairs={{128,256},{384,512},{640,768},{256,128},{512,384},{768,640},{129,2... | collective-permute-start | bytes 49160 | tf_op jit(solution)/shard_map/ppermute | solution.py:429
  77.3 2.4 %collective-permute-start.6 = (f32[8,128]{1,0:T(8,128)S(1)}, f32[8,128]{1,0:T(8,128)S(1)}, u32[]{:S(2)}, u32[]{:S(2)}) collective-permute-start(f32[8,128]{1,0:T(8,128)S(1)} %get-tuple-element.45), channel_id=1, source_target_pairs={{0,16},{32,48},{64,80},{96,112},{16,0},{48,32},{80,64},{112,96},{1... | collective-permute-start | bytes 12296 | tf_op jit(solution)/shard_map/ppermute | solution.py:430
  79.7 0.7 collective-permute-start.7
  80.4 1.5 %collective-permute-done.6.h2 = f32[8,128]{1,0:T(8,128)S(1)} collective-permute-done((f32[8,128]{1,0:T(8,128)S(1)}, f32[8,128]{1,0:T(8,128)S(1)}, u32[]{:S(2)}, u32[]{:S(2)}) %collective-permute-start.6) | collective-permute-done | bytes 4128 | tf_op jit(solution)/shard_map/ppermute | solution.py:430
  81.9 0.0 collective-permute-done.7.h3
  81.9 0.0 collective-permute-done.4.h0
  81.9 0.0 collective-permute-done.5.h1
  82.0 1.6 %all-to-all-done.2.zrec_ref = f32[16,8,128]{2,1,0:T(8,128)S(1)} async-done(((f32[16,8,128]{2,1,0:T(8,128)}), f32[16,8,128]{2,1,0:T(8,128)S(1)}, u32[]{:S(2)}, u32[]{:S(2)}) %all-to-all-start.2) | async-done | bytes 65568 | tf_op jit(solution)/shard_map/all_to_all | solution.py:435
  83.5 0.5 lines_second.1
  84.0 17.8 %all_to_all.31.xrec_ref = f32[64,2,128]{2,1,0:T(2,128)S(1)} all-to-all(f32[64,2,128]{2,1,0:T(2,128)S(1)} %get-tuple-element.49), channel_id=1, replica_groups=mesh['gx'=8,'gy'=8,'gz'=16] {'gx','gy'}, dimensions={0} | all-to-all | bytes 131072 | tf_op jit(solution)/shard_map/all_to_all | solution.py:438
  101.8 0.7 operator_second.1
  102.5 22.8 %all_to_all.32 = f32[16,1,128]{2,1,0:T(1,128)S(1)} all-to-all(f32[16,1,128]{2,1,0:T(1,128)S(1)} %broadcast_in_dim.7), channel_id=1, replica_groups=mesh['gx'=8,'gy'=8,'gz'=16] {'gz'}, dimensions={0} | all-to-all | bytes 16384 | tf_op jit(solution)/shard_map/all_to_all | solution.py:435
  125.4 14.9 %all_to_all.33.all_ref = f32[64,1,128]{2,1,0:T(1,128)S(1)} all-to-all(f32[64,1,128]{2,1,0:T(1,128)S(1)} %broadcast_in_dim.16), channel_id=1, replica_groups=mesh['gx'=8,'gy'=8,'gz'=16] {'gx','gy'}, dimensions={0} | all-to-all | bytes 65536 | tf_op jit(solution)/shard_map/all_to_all | solution.py:438
  140.3 0.9 end.1
  (3 shorter events, 0.0 us)
Async XLA Ops:
  0.6 0.7 copy-start.3
  1.3 57.1 %copy-start = (f32[3,8,32,128]{3,2,1,0:T(8,128)S(1)}, f32[3,8,32,128]{3,2,1,0:T(8,128)}, u32[]{:S(2)}) copy-start(f32[3,8,32,128]{3,2,1,0:T(8,128)} %kappa_ref.3) | copy-start | bytes 1179652
  4.1 31.0 %all-to-all-start = ((f32[16,8,128]{2,1,0:T(8,128)}), f32[16,8,128]{2,1,0:T(8,128)S(1)}, u32[]{:S(2)}, u32[]{:S(2)}) async-start(f32[16,8,128]{2,1,0:T(8,128)} %get-tuple-element.29), calls=%async_computation | async-start | bytes 131072 | tf_op jit(solution)/shard_map/all_to_all | solution.py:435
  23.6 10.5 %collective-permute-start = (f32[32,128]{1,0:T(8,128)S(1)}, f32[32,128]{1,0:T(8,128)S(1)}, u32[]{:S(2)}, u32[]{:S(2)}) collective-permute-start(f32[32,128]{1,0:T(8,128)S(1)} %get-tuple-element.32), channel_id=1, source_target_pairs={{0,128},{256,384},{512,640},{768,896},{128,0},{384,256},{640,512},... | collective-permute-start | bytes 49160 | tf_op jit(solution)/shard_map/ppermute | solution.py:428
  26.4 7.7 %collective-permute-start.1 = (f32[32,128]{1,0:T(8,128)S(1)}, f32[32,128]{1,0:T(8,128)S(1)}, u32[]{:S(2)}, u32[]{:S(2)}) collective-permute-start(f32[32,128]{1,0:T(8,128)S(1)} %get-tuple-element.33), channel_id=1, source_target_pairs={{128,256},{384,512},{640,768},{256,128},{512,384},{768,640},{129,2... | collective-permute-start | bytes 49160 | tf_op jit(solution)/shard_map/ppermute | solution.py:429
  29.5 4.6 %collective-permute-start.2 = (f32[8,128]{1,0:T(8,128)S(1)}, f32[8,128]{1,0:T(8,128)S(1)}, u32[]{:S(2)}, u32[]{:S(2)}) collective-permute-start(f32[8,128]{1,0:T(8,128)S(1)} %get-tuple-element.34), channel_id=1, source_target_pairs={{0,16},{32,48},{64,80},{96,112},{16,0},{48,32},{80,64},{112,96},{1... | collective-permute-start | bytes 12296 | tf_op jit(solution)/shard_map/ppermute | solution.py:430
  32.7 1.4 %collective-permute-start.3 = (f32[8,128]{1,0:T(8,128)S(1)}, f32[8,128]{1,0:T(8,128)S(1)}, u32[]{:S(2)}, u32[]{:S(2)}) collective-permute-start(f32[8,128]{1,0:T(8,128)S(1)} %get-tuple-element.35), channel_id=1, source_target_pairs={{16,32},{48,64},{80,96},{32,16},{64,48},{96,80},{17,33},{49,65},{8... | collective-permute-start | bytes 12296 | tf_op jit(solution)/shard_map/ppermute | solution.py:431
  35.1 23.3 %copy-start.1 = (f32[8,32,128]{2,1,0:T(8,128)S(1)}, f32[8,32,128]{2,1,0:T(8,128)}, u32[]{:S(2)}) copy-start(f32[8,32,128]{2,1,0:T(8,128)} %r_ref.5) | copy-start | bytes 393220
  35.1 23.3 %copy-start.2 = (f32[8,32,128]{2,1,0:T(8,128)S(1)}, f32[8,32,128]{2,1,0:T(8,128)}, u32[]{:S(2)}) copy-start(f32[8,32,128]{2,1,0:T(8,128)} %sigma_ref.3) | copy-start | bytes 393220
  60.2 23.3 %all-to-all-start.2 = ((f32[16,8,128]{2,1,0:T(8,128)}), f32[16,8,128]{2,1,0:T(8,128)S(1)}, u32[]{:S(2)}, u32[]{:S(2)}) async-start(f32[16,8,128]{2,1,0:T(8,128)} %get-tuple-element.41), calls=%async_computation.2 | async-start | bytes 131072 | tf_op jit(solution)/shard_map/all_to_all | solution.py:435
  71.9 10.0 %collective-permute-start.4 = (f32[32,128]{1,0:T(8,128)S(1)}, f32[32,128]{1,0:T(8,128)S(1)}, u32[]{:S(2)}, u32[]{:S(2)}) collective-permute-start(f32[32,128]{1,0:T(8,128)S(1)} %get-tuple-element.43), channel_id=1, source_target_pairs={{0,128},{256,384},{512,640},{768,896},{128,0},{384,256},{640,512},... | collective-permute-start | bytes 49160 | tf_op jit(solution)/shard_map/ppermute | solution.py:428
  75.1 6.9 %collective-permute-start.5 = (f32[32,128]{1,0:T(8,128)S(1)}, f32[32,128]{1,0:T(8,128)S(1)}, u32[]{:S(2)}, u32[]{:S(2)}) collective-permute-start(f32[32,128]{1,0:T(8,128)S(1)} %get-tuple-element.44), channel_id=1, source_target_pairs={{128,256},{384,512},{640,768},{256,128},{512,384},{768,640},{129,2... | collective-permute-start | bytes 49160 | tf_op jit(solution)/shard_map/ppermute | solution.py:429
  77.3 4.6 %collective-permute-start.6 = (f32[8,128]{1,0:T(8,128)S(1)}, f32[8,128]{1,0:T(8,128)S(1)}, u32[]{:S(2)}, u32[]{:S(2)}) collective-permute-start(f32[8,128]{1,0:T(8,128)S(1)} %get-tuple-element.45), channel_id=1, source_target_pairs={{0,16},{32,48},{64,80},{96,112},{16,0},{48,32},{80,64},{112,96},{1... | collective-permute-start | bytes 12296 | tf_op jit(solution)/shard_map/ppermute | solution.py:430
  79.7 2.2 %collective-permute-start.7 = (f32[8,128]{1,0:T(8,128)S(1)}, f32[8,128]{1,0:T(8,128)S(1)}, u32[]{:S(2)}, u32[]{:S(2)}) collective-permute-start(f32[8,128]{1,0:T(8,128)S(1)} %get-tuple-element.46), channel_id=1, source_target_pairs={{16,32},{48,64},{80,96},{32,16},{64,48},{96,80},{17,33},{49,65},{8... | collective-permute-start | bytes 12296 | tf_op jit(solution)/shard_map/ppermute | solution.py:431

commit v3 on v1

--- a/solution.py
+++ b/solution.py
@@ -75,10 +75,9 @@
 
 def begin_kernel(
     sizes, r_hbm, sigma_hbm, kappa_hbm, inv_hbm,
-    jac_ref, dinv_ref, zmsg_ref, loc_ref, alpha_ref, spread_ref, xlo, xhi, ylo, yhi,
+    zmsg_ref, loc_ref, alpha_ref, spread_ref, xlo, xhi, ylo, yhi,
     r_ref, sigma_ref, kappa_ref, inv_ref, sems
 ):
-    planes = (xlo, xhi, ylo, yhi)
     pairs = ((kappa_hbm, kappa_ref), (sigma_hbm, sigma_ref), (r_hbm, r_ref), (inv_hbm, inv_ref))
     copies = [pltpu.make_async_copy(a, b, sems.at[i]) for i, (a, b) in enumerate(pairs)]
     for copy in copies:
@@ -87,11 +86,8 @@
         copy.wait()
     r, sigma = r_ref[...], sigma_ref[...]
     kx, ky, kz = kappa_ref[0], kappa_ref[1], kappa_ref[2]
-    dinv = WEIGHT / (sigma + 2.0 * (kx + ky + kz))
-    jac = dinv * r
-    dinv_ref[...] = dinv
-    jac_ref[...] = jac
-    write_planes(jac, planes)
+    jac = r * (WEIGHT / (sigma + 2.0 * (kx + ky + kz)))
+    write_planes(jac, (xlo, xhi, ylo, yhi))
     unused = iota((CELLS, 128), 1) >= LINES
     e = jnp.where(unused, 1.0, lines_of(sigma))
     g = jnp.where(unused, 1.0, lines_of(kz) * 0.125)
@@ -124,13 +120,9 @@
     write_z_message(zmsg_ref, rows, faces_of(jac), spread_inverse, jnp.sum(r), sizes)
 
 
-def chain_kernel(sizes, fresh, zrec_ref, loc_ref, alpha_ref, _, __, *refs):
-    if fresh:
-        xmsg_ref, own_ref, zhalo_ref, chain_ref, final_ref, sol_ref = refs
-    else:
-        chain_ref, final_ref, xmsg_ref, own_ref, zhalo_ref, sol_ref = refs
-    nx, ny, nz = sizes
-    mx, my, mz = lax.axis_index("gx"), lax.axis_index("gy"), lax.axis_index("gz")
+def solve_chain(sizes, fresh, zrec_ref, loc_ref, alpha_ref, chain_ref, final_ref, sol_ref):
+    nz = sizes[2]
+    mz = lax.axis_index("gz")
     used = iota((8, 128), 1) < LINES
     tiles = [jnp.where(used, zrec_ref[p], 1.0) for p in range(nz)]
     part = lambda p, i: tiles[p][i : i + 1, :]
@@ -222,7 +214,6 @@
     x_low, x_high, y_low, y_high = [
         jnp.sum(jnp.where(keep, dot(sol, pick), 0.0), axis=0, keepdims=True) for pick in picks
     ]
-    own_ref[...] = jnp.concatenate([x_low, x_high] + [zero] * 6, axis=0)
 
     lane8, row8 = iota((8, 128), 1), iota((8, 128), 0)
     of_row = (lane8 // 8 == row8 // 4) & (lane8 < LINES)
@@ -234,7 +225,22 @@
     from_below = zrec_ref[jnp.maximum(mz - 1, 0)]
     from_above = zrec_ref[jnp.minimum(mz + 1, nz - 1)]
     face = jnp.where(lane8 >= HIGH_AT, from_below, from_above)
-    zhalo_ref[...] = jnp.where(lane8 >= LOW_AT, face + THETA * lines_part, 0.0)
+    zhalo = jnp.where(lane8 >= LOW_AT, face + THETA * lines_part, 0.0)
+    return x_low, x_high, y_low, y_high, zhalo
+
+
+def first_lines_kernel(
+    sizes, zrec_ref, loc_ref, alpha_ref, h2, h3, xmsg_ref, own_ref, zhalo_ref, chain_ref, final_ref, sol_ref
+):
+    nx, ny, nz = sizes
+    mx, my = lax.axis_index("gx"), lax.axis_index("gy")
+    x_low, x_high, y_low, y_high, zhalo = solve_chain(
+        sizes, True, zrec_ref, loc_ref, alpha_ref, chain_ref, final_ref, sol_ref
+    )
+    zero = jnp.zeros((1, 128), F32)
+    lane8 = iota((8, 128), 1)
+    own_ref[...] = jnp.concatenate([x_low, x_high] + [zero] * 6, axis=0)
+    zhalo_ref[...] = zhalo
 
     total = zrec_ref[0]
     for p in range(1, nz):
@@ -269,7 +275,51 @@
         xmsg_ref[here + 1, 0:1, :] = y_high
 
 
-def operator(sizes, base, sigma_ref, kappa_ref, xrec_ref, own_ref, zhalo_ref, halos, z_ref, w_ref):
+def scale(sigma_ref, kappa_ref, x):
+    return WEIGHT / (sigma_ref[x] + 2.0 * (kappa_ref[0, x] + kappa_ref[1, x] + kappa_ref[2, x]))
+
+
+def ends_of(face):
+    lane32, row32 = iota((CY, 128), 1), iota((CY, 128), 0)
+    diagonal = (lane32 == row32 + HIGH_AT) | (lane32 == row32 + LOW_AT)
+    spots = jnp.concatenate([jnp.where(diagonal, face[x : x + 1, :], 0.0) for x in range(CX)], axis=0)
+    j, k = iota((128, 128), 0), iota((128, 128), 1)
+    to_ends = one_where(((j >= HIGH_AT) & (k == 0)) | ((j >= LOW_AT) & (j < HIGH_AT) & (k == CZ - 1)))
+    return dot(spots, to_ends)
+
+
+def apply_operator(z, xlo, xhi, ylo, yhi, ends, sigma_ref, kappa_ref, w_ref):
+    lane32, row32 = iota((CY, 128), 1), iota((CY, 128), 0)
+    for x in range(CX):
+        here_z = z[x]
+        before = z[x - 1] if x > 0 else xlo
+        after = z[x + 1] if x < CX - 1 else xhi
+        y_less = jnp.where(row32 == 0, ylo[x : x + 1, :], pltpu.roll(here_z, 1, 0))
+        y_more = jnp.where(row32 == CY - 1, yhi[x : x + 1, :], pltpu.roll(here_z, CY - 1, 0))
+        z_less = jnp.where(lane32 == 0, 0.0, pltpu.roll(here_z, 1, 1))
+        z_more = jnp.where(lane32 == CZ - 1, 0.0, pltpu.roll(here_z, CZ - 1, 1))
+        twice = 2.0 * here_z
+        w_ref[x] = (
+            sigma_ref[x] * here_z
+            + kappa_ref[0, x] * (twice - before - after)
+            + kappa_ref[1, x] * (twice - y_less - y_more)
+            + kappa_ref[2, x] * (twice - z_less - z_more - ends[x * 32 : x * 32 + 32])
+        )
+
+
+def wide(row):
+    return jnp.where(iota((CY, 128), 1) // 16 == iota((CY, 128), 0) // 4, row, 0.0)
+
+
+def thin(row):
+    return jnp.where(iota((CX, 128), 1) // 16 == iota((CX, 128), 0) // 4, row, 0.0)
+
+
+def to_cells():
+    return one_where(iota((128, 128), 0) % 16 == iota((128, 128), 1) // 8)
+
+
+def full_direction(sizes, base, xrec_ref, own_ref, zhalo_ref, halos, z_ref):
     nx, ny, nz = sizes
     mx, my, mz = lax.axis_index("gx"), lax.axis_index("gy"), lax.axis_index("gz")
     here = mx * ny + my
@@ -283,10 +333,6 @@
     c_ylo, c_yhi = coarse(PART_AT + 7), coarse(PART_AT + 9)
     c_xlo, c_xhi = coarse(PART_AT + 24), coarse(PART_AT + 32)
 
-    lane32, row32 = iota((CY, 128), 1), iota((CY, 128), 0)
-    lane8, row8 = iota((8, 128), 1), iota((8, 128), 0)
-    wide = lambda row: jnp.where(lane32 // 16 == row32 // 4, row, 0.0)
-    thin = lambda row: jnp.where(lane8 // 16 == row8 // 4, row, 0.0)
     left = xrec_ref[jnp.maximum(here - ny, 0), 0:1, :]
     right = xrec_ref[jnp.minimum(here + ny, nx * ny - 1), 0:1, :]
     front = xrec_ref[jnp.maximum(here - 1, 0), 0:1, :]
@@ -295,55 +341,33 @@
         [wide(own_ref[0:1, :]), wide(own_ref[1:2, :]), wide(left), wide(right), thin(front), thin(back)],
         axis=0,
     )
-    to_cells = one_where(iota((128, 128), 0) % 16 == iota((128, 128), 1) // 8)
-    lines = dot(rows, to_cells)
-    xlo, xhi, ylo, yhi = halos
-    xlo = jnp.where(mx > 0, xlo[...] + lines[64:96] + c_xlo, 0.0)
-    xhi = jnp.where(mx < nx - 1, xhi[...] + lines[96:128] + c_xhi, 0.0)
-    ylo = jnp.where(my > 0, ylo[...] + lines[128:136] + c_ylo, 0.0)
-    yhi = jnp.where(my < ny - 1, yhi[...] + lines[136:144] + c_yhi, 0.0)
+    lines = dot(rows, to_cells())
+    xlo, xhi, ylo, yhi = [h[...] for h in halos]
+    xlo = jnp.where(mx > 0, xlo + lines[64:96] + c_xlo, 0.0)
+    xhi = jnp.where(mx < nx - 1, xhi + lines[96:128] + c_xhi, 0.0)
+    ylo = jnp.where(my > 0, ylo + lines[128:136] + c_ylo, 0.0)
+    yhi = jnp.where(my < ny - 1, yhi + lines[136:144] + c_yhi, 0.0)
     face = zhalo_ref[...]
     high = jnp.where(mz > 0, face + c_zlo, 0.0)
     low = jnp.where(mz < nz - 1, face + c_zhi, 0.0)
-    face = jnp.where(lane8 >= HIGH_AT, high, low)
-    diagonal = (lane32 == row32 + HIGH_AT) | (lane32 == row32 + LOW_AT)
-    spots = jnp.concatenate([jnp.where(diagonal, face[x : x + 1, :], 0.0) for x in range(CX)], axis=0)
-    j, k = iota((128, 128), 0), iota((128, 128), 1)
-    to_ends = one_where(((j >= HIGH_AT) & (k == 0)) | ((j >= LOW_AT) & (j < HIGH_AT) & (k == CZ - 1)))
-    ends = dot(spots, to_ends)
-
+    ends = ends_of(jnp.where(iota((8, 128), 1) >= HIGH_AT, high, low))
     z = [base(x) + lines[(x // 4) * 32 : (x // 4) * 32 + 32] + c_own for x in range(CX)]
-    w = []
     for x in range(CX):
-        here_z = z[x]
-        z_ref[x] = here_z
-        before = z[x - 1] if x > 0 else xlo
-        after = z[x + 1] if x < CX - 1 else xhi
-        y_less = jnp.where(row32 == 0, ylo[x : x + 1, :], pltpu.roll(here_z, 1, 0))
-        y_more = jnp.where(row32 == CY - 1, yhi[x : x + 1, :], pltpu.roll(here_z, CY - 1, 0))
-        z_less = jnp.where(lane32 == 0, 0.0, pltpu.roll(here_z, 1, 1))
-        z_more = jnp.where(lane32 == CZ - 1, 0.0, pltpu.roll(here_z, CZ - 1, 1))
-        twice = 2.0 * here_z
-        value = (
-            sigma_ref[x] * here_z
-            + kappa_ref[0, x] * (twice - before - after)
-            + kappa_ref[1, x] * (twice - y_less - y_more)
-            + kappa_ref[2, x] * (twice - z_less - z_more - ends[x * 32 : x * 32 + 32])
-        )
-        w_ref[x] = value
-        w.append(value)
-    return z, w
+        z_ref[x] = z[x]
+    return z, xlo, xhi, ylo, yhi, ends
 
 
 def first_kernel(
-    sizes, jac_ref, dinv_ref, sigma_ref, kappa_ref, xrec_ref, own_ref, zhalo_ref, h0, h1, h2, h3,
-    loc_ref, spread_ref, z_ref, w_ref, zmsg_ref, alpha_ref, *planes
+    sizes, r_ref, sigma_ref, kappa_ref, xrec_ref, own_ref, zhalo_ref, h0, h1, h2, h3,
+    loc_ref, spread_ref, z_ref, w_ref, jac_ref, zmsg_ref, alpha_ref
 ):
-    base = lambda x: jac_ref[x]
-    operator(sizes, base, sigma_ref, kappa_ref, xrec_ref, own_ref, zhalo_ref, (h0, h1, h2, h3), z_ref, w_ref)
+    scales = [scale(sigma_ref, kappa_ref, x) for x in range(CX)]
+    base = lambda x: scales[x] * r_ref[x]
+    parts = full_direction(sizes, base, xrec_ref, own_ref, zhalo_ref, (h0, h1, h2, h3), z_ref)
+    apply_operator(*parts, sigma_ref, kappa_ref, w_ref)
     field = w_ref[...]
-    jac = dinv_ref[...] * field
-    write_planes(jac, planes)
+    for x in range(CX):
+        jac_ref[x] = scales[x] * w_ref[x]
     rhs = lines_of(field)
     row = lambda a, k: a[k : k + 1, :]
     cur_first, cur = row(rhs, 0), row(rhs, 1)
@@ -355,25 +379,178 @@
         cur_first = cur_first + loc_ref[0, k : k + 1, :] * cur
         cur = row(rhs, k + 1) + loc_ref[1, k : k + 1, :] * cur
     write_z_message(
-        zmsg_ref, [cur_first, cur], faces_of(jac), spread_ref[...], jnp.sum(field), sizes
-    )
+        zmsg_ref, [cur_first, cur], faces_of(jac_ref[...]), spread_ref[...], jnp.sum(field), sizes
+    )
+
+
+def second_lines_kernel(
+    sizes, zrec_ref, loc_ref, alpha_ref, chain_ref, final_ref, jac_ref,
+    part_ref, zhalo_ref, z_ref, xlo, xhi, ylo, yhi, sol_ref
+):
+    x_low, x_high, _, _, zhalo = solve_chain(
+        sizes, False, zrec_ref, loc_ref, alpha_ref, chain_ref, final_ref, sol_ref
+    )
+    zhalo_ref[...] = zhalo
+    lines = dot(jnp.concatenate([wide(x_low), wide(x_high)], axis=0), to_cells())
+    for x in range(CX):
+        z_ref[x] = jac_ref[x] + lines[(x // 4) * 32 : (x // 4) * 32 + 32]
+    write_planes(z_ref[...], (xlo, xhi, ylo, yhi))
+    total = zrec_ref[0]
+    for p in range(1, sizes[2]):
+        total = total + zrec_ref[p]
+    part_ref[...] = total
+
+
+FACES = range(1, 7)
+TERMS = (
+    [("g11", -1, -1), ("g12", -1, -1), ("g22", -1, -1), ("h1", -1, -1), ("h2", -1, -1)]
+    + [(name, j, -1) for name in ("h2", "g12", "g22") for j in range(7)]
+    + [("g22", 0, j) for j in range(7)]
+    + [("g22", j, j) for j in FACES]
+    + [("g22", j, k) for j in FACES for k in FACES if j < k and (j - 1) // 2 != (k - 1) // 2]
+)
+NAMES = ("g11", "g12", "g22", "h1", "h2")
+TERMS_AT = 72
 
 
 def second_kernel(
-    sizes, r_ref, w1_ref, dinv_ref, sigma_ref, kappa_ref, xrec_ref, own_ref, zhalo_ref, h0, h1, h2, h3,
-    z_ref, w_ref, sums_ref
+    sizes, r_ref, w1_ref, sigma_ref, kappa_ref, z_ref, zhalo_ref, part_ref, h0, h1, h2, h3,
+    w_ref, xmsg_ref, terms_ref
 ):
-    base = lambda x: dinv_ref[x] * w1_ref[x]
-    operator(sizes, base, sigma_ref, kappa_ref, xrec_ref, own_ref, zhalo_ref, (h0, h1, h2, h3), z_ref, w_ref)
-    w1, w2, r = w1_ref[...], w_ref[...], r_ref[...]
-    lane = iota((1, 128), 1)
+    nx, ny, nz = sizes
+    mx, my, mz = lax.axis_index("gx"), lax.axis_index("gy"), lax.axis_index("gz")
+    xlo = jnp.where(mx > 0, h0[...], 0.0)
+    xhi = jnp.where(mx < nx - 1, h1[...], 0.0)
+    ylo = jnp.where(my > 0, h2[...], 0.0)
+    yhi = jnp.where(my < ny - 1, h3[...], 0.0)
+    face = zhalo_ref[...]
+    high, low = jnp.where(mz > 0, face, 0.0), jnp.where(mz < nz - 1, face, 0.0)
+    ends = ends_of(jnp.where(iota((8, 128), 1) >= HIGH_AT, high, low))
+    apply_operator([z_ref[x] for x in range(CX)], xlo, xhi, ylo, yhi, ends, sigma_ref, kappa_ref, w_ref)
+
+    r, w1, w2, sigma = r_ref[...], w1_ref[...], w_ref[...], sigma_ref[...]
+    kz = kappa_ref[2]
+    rows = lambda a: jnp.sum(jnp.sum(a, axis=0), axis=0, keepdims=True)
+    lane1 = iota((1, 128), 1)
+    pick = lambda profile, face: jnp.where(lane1 == (0 if face == 5 else CZ - 1), profile, 0.0)
+    low_row = lambda a: jnp.sum(a, axis=0, keepdims=True)
+    partner = {"h2": r, "g12": w1, "g22": w2}
+    partner_ref = {"h2": r_ref, "g12": w1_ref, "g22": w_ref}
+    z_profiles = {name: rows(kz * f) for name, f in partner.items()}
+    z_sigma, z_self = rows(kz * sigma), rows(kz * kz)
+
+    def plane(ref, f):
+        if f < 3:
+            return ref[0 if f == 1 else CX - 1]
+        return ref[:, 0 if f == 3 else CY - 1, :]
+
+    face_weight = {f: plane(kappa_ref.at[(f - 1) // 2], f) for f in range(1, 5)}
+
+    def on_face(f, other):
+        return low_row(face_weight[f] * plane(other, f))
+
+    def term(name, j, k):
+        if j == -1:
+            a, b = {"g11": (w1, w1), "g12": (w1, w2), "g22": (w2, w2), "h1": (w1, r), "h2": (w2, r)}[name]
+            return rows(a * b)
+        if k == -1:
+            twice = 2.0 if name == "g22" else 1.0
+            if j == 0:
+                return twice * rows(sigma * partner[name])
+            if j > 4:
+                return twice * pick(z_profiles[name], j)
+            return twice * on_face(j, partner_ref[name])
+        if j == 0:
+            if k == 0:
+                return rows(sigma * sigma)
+            return 2.0 * (pick(z_sigma, k) if k > 4 else on_face(k, sigma_ref))
+        if j == k:
+            return pick(z_self, j) if j > 4 else on_face(j, kappa_ref.at[(j - 1) // 2])
+        if k > 4:
+            return 2.0 * pick(on_face(j, kappa_ref.at[2]), k)
+        x, y = 0 if j == 1 else CX - 1, 0 if k == 3 else CY - 1
+        return 2.0 * kappa_ref[0, x, y : y + 1, :] * kappa_ref[1, x, y : y + 1, :]
+
+    for i, (name, j, k) in enumerate(TERMS):
+        terms_ref[i : i + 1, :] = term(name, j, k)
+    for i in range(len(TERMS), 128):
+        if i % 8 == 0:
+            terms_ref[i : i + 8, :] = jnp.zeros((8, 128), F32)
+        elif i == len(TERMS):
+            stop = -(-i // 8) * 8
+            terms_ref[i:stop, :] = jnp.zeros((stop - i, 128), F32)
+    poly = dot_t(jnp.full((8, 128), 1.0, F32), terms_ref[...])[0:1, :]
+    part = part_ref[...]
+    lane8 = iota((8, 128), 1)
+    part = jnp.where((lane8 >= PART_AT) & (lane8 < PART_AT + 24), part, 0.0)
+    at = lambda i, lane: pltpu.roll(part, (lane - PART_AT) % 128, 1)[i : i + 1, :]
+    upper = at(0, 0) + at(1, 24) + at(2, 48) + at(3, 72) + at(4, 96)
+    lower = at(5, 0) + at(6, 24) + at(7, 48) + pltpu.roll(poly, TERMS_AT, 1)
+    both = jnp.concatenate([upper, lower], axis=0)
+    for q in range(nx * ny):
+        xmsg_ref[q] = both
+
+
+def plane_kernel(sizes, xrec_ref, sums_ref, own_ref, flat_ref):
+    nx, ny, nz = sizes
+    mx, my, mz = lax.axis_index("gx"), lax.axis_index("gy"), lax.axis_index("gz")
+    count = nx * ny
+    total = xrec_ref[0]
+    for q in range(count):
+        flat_ref[q : q + 1, :] = xrec_ref[q, 1:2, :]
+        if q > 0:
+            total = total + xrec_ref[q]
+    lane, row = iota((count, 128), 1), iota((count, 128), 0)
+    tx, ty = row // ny, row % ny
+
+    def value(qx, qy, dz, valid):
+        at = jnp.where(qx < 5, qx * 24, (qx - 5) * 24) + 8 + 8 * dz + qy
+        chosen = jnp.where(qx < 5, total[0:1, :], total[1:2, :])
+        return jnp.sum(jnp.where((lane == at) & valid, chosen, 0.0), axis=1, keepdims=True)
+
+    always = row >= 0
+    c = value(tx, ty, 0, always)
+    near = [
+        value(tx - 1, ty, 0, tx > 0),
+        value(tx + 1, ty, 0, tx < nx - 1),
+        value(tx, ty - 1, 0, ty > 0),
+        value(tx, ty + 1, 0, ty < ny - 1),
+        value(tx, ty, -1, always & (mz > 0)),
+        value(tx, ty, 1, always & (mz < nz - 1)),
+    ]
+    v = [c] + [c - n for n in near]
+    first = jnp.where(lane < 0, 1.0, 0.0)
+    second = first
+    for j in range(-1, 7):
+        amount = 1.0 if j == -1 else v[j]
+        is_first = lane < 0
+        is_second = is_first
+        for i, (_, a, b) in enumerate(TERMS):
+            if a == j:
+                is_first = is_first | (lane == TERMS_AT + i)
+            if b == j:
+                is_second = is_second | (lane == TERMS_AT + i)
+        first = jnp.where(is_first, amount, first)
+        second = jnp.where(is_second, amount, second)
+    terms = jnp.where(lane >= TERMS_AT, flat_ref[...], 0.0)
+    added = jnp.sum(terms * first * second, axis=0, keepdims=True)
+    lane1 = iota((1, 128), 1)
     out = jnp.zeros((1, 128), F32)
-    for i, product in enumerate((w1 * w1, w1 * w2, w2 * w2, w1 * r, w2 * r)):
-        out = jnp.where(lane == i, jnp.sum(product), out)
+    for n, name in enumerate(NAMES):
+        mask = lane1 < 0
+        for i, (of, _, _) in enumerate(TERMS):
+            if of == name:
+                mask = mask | (lane1 == TERMS_AT + i)
+        out = jnp.where(lane1 == n, jnp.sum(jnp.where(mask, added, 0.0), axis=1, keepdims=True), out)
     sums_ref[...] = out
-
-
-def end_kernel(all_ref, r_ref, z1_ref, w1_ref, z2_ref, w2_ref, field_ref, res_ref):
+    mine = row == mx * ny + my
+    for j in range(7):
+        own = jnp.sum(jnp.where(mine & (lane == 0), v[j], 0.0))
+        own_ref[j : j + 1, :] = jnp.full((1, 128), own, F32)
+    own_ref[7:8, :] = jnp.zeros((1, 128), F32)
+
+
+def end_kernel(all_ref, own_ref, r_ref, sigma_ref, kappa_ref, z1_ref, w1_ref, z2_ref, w2_ref, field_ref, res_ref):
     sums = all_ref[0]
     for q in range(1, all_ref.shape[0]):
         sums = sums + all_ref[q]
@@ -383,9 +560,18 @@
     inv = 1.0 / (g11 * g22 - g12 * g12)
     y1 = (g22 * h1 - g12 * h2) * inv
     y2 = (g11 * h2 - g12 * h1) * inv
+    c, xlo, xhi, ylo, yhi, zlo, zhi = [own_ref[j : j + 1, :] for j in range(7)]
+    lane32, row32 = iota((CY, 128), 1), iota((CY, 128), 0)
+    on_y = jnp.where(row32 == 0, ylo, jnp.where(row32 == CY - 1, yhi, 0.0))
+    on_z = jnp.where(lane32 == 0, zlo, jnp.where(lane32 == CZ - 1, zhi, 0.0))
     for x in range(CX):
-        field_ref[x] = y1 * z1_ref[x] + y2 * z2_ref[x]
-        res_ref[x] = r_ref[x] - y1 * w1_ref[x] - y2 * w2_ref[x]
+        w2 = w2_ref[x] + sigma_ref[x] * c + kappa_ref[1, x] * on_y + kappa_ref[2, x] * on_z
+        if x == 0:
+            w2 = w2 + kappa_ref[0, x] * xlo
+        if x == CX - 1:
+            w2 = w2 + kappa_ref[0, x] * xhi
+        field_ref[x] = y1 * z1_ref[x] + y2 * (z2_ref[x] + c)
+        res_ref[x] = r_ref[x] - y1 * w1_ref[x] - y2 * w2
 
 
 def call(kernel, out_shapes, scratch=(), name=None, inputs=pltpu.VMEM, semaphores=(), limit=24 << 20):
@@ -429,31 +615,33 @@
         return lax.all_to_all(message, ("gx", "gy"), split_axis=0, concat_axis=0, tiled=True)
 
     bind = lambda kernel, *a: functools.partial(kernel, sizes, *a)
-    jac, dinv, zmsg, loc, alpha, spread, *sides = call(
-        bind(begin_kernel), [field, field, to_z, (3, *coarse), coarse, tile, *planes],
-        [field, field, (3, *field), tile], "begin", pltpu.HBM, [pltpu.SemaphoreType.DMA((4,))], 54875 << 10,
+    zmsg, loc, alpha, spread, *sides = call(
+        bind(begin_kernel), [to_z, (3, *coarse), coarse, tile, *planes],
+        [field, field, (3, *field), tile], "begin", pltpu.HBM, [pltpu.SemaphoreType.DMA((4,))], 55100 << 10,
     )(r, sigma, kappa, inverse_rows)
     zrec = along_z(zmsg)
     halos = halo(sides)
     xmsg, own, zhalo, chain, final = call(
-        bind(chain_kernel, True), [to_xy, tile, tile, (4, nz, 128), tile], [coarse], "lines_first"
+        bind(first_lines_kernel), [to_xy, tile, tile, (4, nz, 128), tile], [coarse], "lines_first"
     )(zrec, loc, alpha, *halos[2:])
     xrec = along_xy(xmsg)
-    z1, w1, zmsg, alpha, *sides = call(
-        bind(first_kernel), [field, field, to_z, coarse, *planes], name="operator_first"
-    )(jac, dinv, sigma, kappa, xrec, own, zhalo, *halos, loc, spread)
+    z1, w1, jac, zmsg, alpha = call(
+        bind(first_kernel), [field, field, field, to_z, coarse], name="operator_first"
+    )(r, sigma, kappa, xrec, own, zhalo, *halos, loc, spread)
     zrec = along_z(zmsg)
+    part, zhalo, z2, *sides = call(
+        bind(second_lines_kernel), [tile, tile, field, *planes], [coarse], "lines_second"
+    )(zrec, loc, alpha, chain, final, jac)
     halos = halo(sides)
-    xmsg, own, zhalo = call(
-        bind(chain_kernel, False), [to_xy, tile, tile], [coarse], "lines_second"
-    )(zrec, loc, alpha, *halos[2:], chain, final)
+    w2, xmsg = call(bind(second_kernel), [field, to_xy], [(128, 128)], "operator_second")(
+        r, w1, sigma, kappa, z2, zhalo, part, *halos
+    )
     xrec = along_xy(xmsg)
-    z2, w2, sums = call(bind(second_kernel), [field, field, (1, 128)], name="operator_second")(
-        r, w1, dinv, sigma, kappa, xrec, own, zhalo, *halos
-    )
-    sums = jnp.sum(along_z(jnp.broadcast_to(sums[None], (nz, 1, 128))), axis=0)
-    sums = along_xy(jnp.broadcast_to(sums[None], (nx * ny, 1, 128)))
-    return tuple(call(end_kernel, [field, field], name="end")(sums, r, z1, w1, z2, w2))
+    sums, values = call(bind(plane_kernel), [(1, 128), tile], [(nx * ny, 128)], "plane")(xrec)
+    sums = along_z(jnp.broadcast_to(sums[None], (nz, 1, 128)))
+    return tuple(
+        call(end_kernel, [field, field], name="end")(sums, values, r, sigma, kappa, z1, w1, z2, w2)
+    )
 
 
 def solution(mesh):

time: 135 us -> 125 us (0.926)
  blocking collectives: 35.5 us -> 51.9 us
  starting transfers between devices: 63.6 us -> 49.7 us
  waiting for transfers between devices: 25.1 us -> 12.9 us
    all_to_all x1 -> x2, blocking collectives: 20.6 us -> 33.6 us  [along_z(): lax.all_to_all(message, 'gz', split_axis=0, concat_axis=0, tiled=True)]
    all_to_all x2 -> x1, starting transfers between devices: 27.9 us -> 19.6 us  [along_z(): lax.all_to_all(message, 'gz', split_axis=0, concat_axis=0, tiled=True)]
    all_to_all x2 -> x1, starting transfers between devices: 18.7 us -> 12.2 us  [along_xy(): lax.all_to_all(message, ('gx', 'gy'), split_axis=0, concat_axis=0, tiled=...]
    all_to_all x2 -> x1, waiting for transfers between devices: 7.92 us -> 3.56 us  [along_z(): lax.all_to_all(message, 'gz', split_axis=0, concat_axis=0, tiled=True)]
    all_to_all x2 -> x1, waiting for transfers between devices: 8.63 us -> 4.31 us  [along_xy(): lax.all_to_all(message, ('gx', 'gy'), split_axis=0, concat_axis=0, tiled=...]
    all_to_all x1, blocking collectives: 14.9 us -> 18.4 us  [along_xy(): lax.all_to_all(message, ('gx', 'gy'), split_axis=0, concat_axis=0, tiled=...]
    ppermute x2, waiting for transfers between devices: 5.25 us -> 2.62 us  [halo(): lax.ppermute(xlo, 'gx', down(nx))]
    pallas_call x6 -> x7, Pallas kernels: 8.54 us -> 7.97 us  [run(): pl.pallas_call(kernel, out_shape=[jax.ShapeDtypeStruct(s, F32) for s in o...]
  transfers between devices with their start and end apart: 12 -> 10, of which waited for: 10 -> 6; matrix products, arithmetic and copies ran while one was open for 0% -> 0% of each run, Pallas kernels for 0% -> 0%
where the time goes in v3:
time: 125 us; the launch traced here: 124 us
  blocking collectives  51.9 us (42%)
  starting transfers between devices  49.7 us (40%)
  waiting for transfers between devices  12.9 us (10%)
  Pallas kernels  7.97 us (6%)
    all_to_all x2, blocking collectives, along_z(): lax.all_to_all(message, 'gz', split_axis=0, concat_axis=0, tiled=True)  33.6 us
    all_to_all x1, starting transfers between devices, along_z(): lax.all_to_all(message, 'gz', split_axis=0, concat_axis=0, tiled=True)  19.6 us
    all_to_all x1, blocking collectives, along_xy(): lax.all_to_all(message, ('gx', 'gy'), split_axis=0, concat_axis=0, tiled=...  18.4 us
    all_to_all x1, starting transfers between devices, along_xy(): lax.all_to_all(message, ('gx', 'gy'), split_axis=0, concat_axis=0, tiled=...  12.2 us
    pallas_call x7, Pallas kernels, run(): pl.pallas_call(kernel, out_shape=[jax.ShapeDtypeStruct(s, F32) for s in o...  7.97 us
    ppermute x2, starting transfers between devices, halo(): lax.ppermute(ylo, 'gy', down(ny))  7.89 us
    ppermute x2, starting transfers between devices, halo(): lax.ppermute(yhi, 'gy', up(ny))  5.74 us
    all_to_all x1, waiting for transfers between devices, along_xy(): lax.all_to_all(message, ('gx', 'gy'), split_axis=0, concat_axis=0, tiled=...  4.31 us
  transfers between devices with their start and end apart: 10, of which 6 were waited for; matrix products, arithmetic and copies ran while one was open for 0% of the time, Pallas kernels for 0%

profile of v3, /device:TPU:1, one launch (start us, length us, event | category | flops | bytes accessed | tf_op | source)
XLA Modules:
  0.0 124.0 jit_solution(1063968682082946202)
XLA Ops:
  0.6 0.0 copy-start.3
  0.6 0.7 copy-done.3
  1.3 0.0 copy-start
  1.3 2.8 %begin.1 = (f32[16,8,128]{2,1,0:T(8,128)}, f32[3,16,128]{2,1,0:T(8,128)S(1)}, f32[16,128]{1,0:T(8,128)S(1)}, f32[8,128]{1,0:T(8,128)S(1)}, f32[32,128]{1,0:T(8,1...) custom-call(f32[8,32,128]{2,1,0:T(8,128)} %r_ref.5, f32[8,32,128]{2,1,0:T(8,128)} %sigma_ref.5, ...), custom_call_target="tpu_custom_call" | custom-call | tf_op jit(solution)/shard_map/begin/pallas_call | solution.py:581
  4.1 0.0 copy-start.2
  4.1 19.6 %all-to-all-start = ((f32[16,8,128]{2,1,0:T(8,128)}), f32[16,8,128]{2,1,0:T(8,128)S(1)}, u32[]{:S(2)}, u32[]{:S(2)}) async-start(f32[16,8,128]{2,1,0:T(8,128)} %get-tuple-element.31), calls=%async_computation | async-start | bytes 131072 | tf_op jit(solution)/shard_map/all_to_all | solution.py:612
  23.7 0.0 copy-start.1
  23.7 3.3 %collective-permute-start = (f32[8,128]{1,0:T(8,128)S(1)}, f32[8,128]{1,0:T(8,128)S(1)}, u32[]{:S(2)}, u32[]{:S(2)}) collective-permute-start(f32[8,128]{1,0:T(8,128)S(1)} %get-tuple-element.34), channel_id=1, source_target_pairs={{0,16},{16,32},{32,48},{48,64},{64,80},{80,96},{96,112},{112,0},{1... | collective-permute-start | bytes 12296 | tf_op jit(solution)/shard_map/ppermute | solution.py:607
  27.1 3.8 %collective-permute-start.1 = (f32[8,128]{1,0:T(8,128)S(1)}, f32[8,128]{1,0:T(8,128)S(1)}, u32[]{:S(2)}, u32[]{:S(2)}) collective-permute-start(f32[8,128]{1,0:T(8,128)S(1)} %get-tuple-element.35), channel_id=1, source_target_pairs={{16,0},{32,16},{48,32},{64,48},{80,64},{96,80},{112,96},{0,112},{1... | collective-permute-start | bytes 12296 | tf_op jit(solution)/shard_map/ppermute | solution.py:608
  30.9 0.0 collective-permute-done.h2
  30.9 0.8 collective-permute-done.1.h3
  31.7 3.6 %all-to-all-done.zrec_ref = f32[16,8,128]{2,1,0:T(8,128)S(1)} async-done(((f32[16,8,128]{2,1,0:T(8,128)}), f32[16,8,128]{2,1,0:T(8,128)S(1)}, u32[]{:S(2)}, u32[]{:S(2)}) %all-to-all-start) | async-done | bytes 65568 | tf_op jit(solution)/shard_map/all_to_all | solution.py:612
  35.3 1.3 %lines_first.1 = (f32[64,2,128]{2,1,0:T(2,128)}, f32[8,128]{1,0:T(8,128)S(1)}, f32[8,128]{1,0:T(8,128)S(1)}, f32[4,16,128]{2,1,0:T(8,128)S(1)}, f32[8,128]{1,0:T(8,128)S(1)}) custom-call(f32[16,8,128]{2,1,0:T(8,128)S(1)} %all-to-all-done.zrec_ref, f32[3,16,128]{2,1,0:T(8,128)S(1)} %get-tuple-element.32.loc_ref, f32[16,128]{1,0:T(8,128)S(1)} %get-tuple-element.33.alpha_ref, ...), custom_call_target="tpu_custom_call" | custom-call | tf_op jit(solution)/shard_map/lines_first/pallas_call | solution.py:581
  36.6 12.2 %all-to-all-start.1 = ((f32[64,2,128]{2,1,0:T(2,128)}), f32[64,2,128]{2,1,0:T(2,128)S(1)}, u32[]{:S(2)}, u32[]{:S(2)}) async-start(f32[64,2,128]{2,1,0:T(2,128)} %get-tuple-element.36), calls=%async_computation.1 | async-start | bytes 131072 | tf_op jit(solution)/shard_map/all_to_all | solution.py:615
  48.8 1.6 %collective-permute-start.2 = (f32[32,128]{1,0:T(8,128)S(1)}, f32[32,128]{1,0:T(8,128)S(1)}, u32[]{:S(2)}, u32[]{:S(2)}) collective-permute-start(f32[32,128]{1,0:T(8,128)S(1)} %get-tuple-element.39), channel_id=1, source_target_pairs={{0,128},{128,256},{256,384},{384,512},{512,640},{640,768},{768,896... | collective-permute-start | bytes 49160 | tf_op jit(solution)/shard_map/ppermute | solution.py:605
  50.5 0.0 collective-permute-start.3
  50.5 0.9 collective-permute-done.2.h0
  51.3 2.6 %collective-permute-done.3.h1 = f32[32,128]{1,0:T(8,128)S(1)} collective-permute-done((f32[32,128]{1,0:T(8,128)S(1)}, f32[32,128]{1,0:T(8,128)S(1)}, u32[]{:S(2)}, u32[]{:S(2)}) %collective-permute-start.3) | collective-permute-done | bytes 16416 | tf_op jit(solution)/shard_map/ppermute | solution.py:606
  54.0 4.3 %all-to-all-done.1.xrec_ref = f32[64,2,128]{2,1,0:T(2,128)S(1)} async-done(((f32[64,2,128]{2,1,0:T(2,128)}), f32[64,2,128]{2,1,0:T(2,128)S(1)}, u32[]{:S(2)}, u32[]{:S(2)}) %all-to-all-start.1) | async-done | bytes 65568 | tf_op jit(solution)/shard_map/all_to_all | solution.py:615
  58.3 0.0 copy-done
  58.3 0.0 copy-done.2
  58.3 0.0 copy-done.1
  58.3 1.1 operator_first.1
  59.4 19.7 %all_to_all.25.zrec_ref = f32[16,8,128]{2,1,0:T(8,128)S(1)} all-to-all(f32[16,8,128]{2,1,0:T(8,128)S(1)} %get-tuple-element.43), channel_id=1, replica_groups=mesh['gx'=8,'gy'=8,'gz'=16] {'gz'}, dimensions={0} | all-to-all | bytes 131072 | tf_op jit(solution)/shard_map/all_to_all | solution.py:612
  79.2 0.6 lines_second.1
  79.7 2.7 %collective-permute-start.4 = (f32[32,128]{1,0:T(8,128)S(1)}, f32[32,128]{1,0:T(8,128)S(1)}, u32[]{:S(2)}, u32[]{:S(2)}) collective-permute-start(f32[32,128]{1,0:T(8,128)S(1)} %get-tuple-element.51), channel_id=1, source_target_pairs={{0,128},{128,256},{256,384},{384,512},{512,640},{640,768},{768,896... | collective-permute-start | bytes 49160 | tf_op jit(solution)/shard_map/ppermute | solution.py:605
  82.4 0.0 collective-permute-start.5
  82.4 2.4 %collective-permute-start.6 = (f32[8,128]{1,0:T(8,128)S(1)}, f32[8,128]{1,0:T(8,128)S(1)}, u32[]{:S(2)}, u32[]{:S(2)}) collective-permute-start(f32[8,128]{1,0:T(8,128)S(1)} %get-tuple-element.53), channel_id=1, source_target_pairs={{0,16},{16,32},{32,48},{48,64},{64,80},{80,96},{96,112},{112,0},{1... | collective-permute-start | bytes 12296 | tf_op jit(solution)/shard_map/ppermute | solution.py:607
  84.8 4.1 %collective-permute-start.7 = (f32[8,128]{1,0:T(8,128)S(1)}, f32[8,128]{1,0:T(8,128)S(1)}, u32[]{:S(2)}, u32[]{:S(2)}) collective-permute-start(f32[8,128]{1,0:T(8,128)S(1)} %get-tuple-element.54), channel_id=1, source_target_pairs={{16,0},{32,16},{48,32},{64,48},{80,64},{96,80},{112,96},{0,112},{1... | collective-permute-start | bytes 12296 | tf_op jit(solution)/shard_map/ppermute | solution.py:608
  88.9 0.0 collective-permute-done.6.h2
  88.9 0.7 collective-permute-done.7.h3
  89.6 0.0 collective-permute-done.4.h0
  89.6 0.0 collective-permute-done.5.h1
  89.6 1.0 operator_second.1
  90.6 18.4 %all_to_all.26.xrec_ref = f32[64,2,128]{2,1,0:T(2,128)S(1)} all-to-all(f32[64,2,128]{2,1,0:T(2,128)S(1)} %get-tuple-element.55), channel_id=1, replica_groups=mesh['gx'=8,'gy'=8,'gz'=16] {'gx','gy'}, dimensions={0} | all-to-all | bytes 131072 | tf_op jit(solution)/shard_map/all_to_all | solution.py:615
  109.0 0.3 plane.1
  109.4 13.8 %all_to_all.27.all_ref = f32[16,1,128]{2,1,0:T(1,128)S(1)} all-to-all(f32[16,1,128]{2,1,0:T(1,128)S(1)} %broadcast_in_dim.9), channel_id=1, replica_groups=mesh['gx'=8,'gy'=8,'gz'=16] {'gz'}, dimensions={0} | all-to-all | bytes 16384 | tf_op jit(solution)/shard_map/all_to_all | solution.py:612
  123.2 0.8 end.1
  (1 shorter events, 0.0 us)
Async XLA Ops:
  0.6 0.7 copy-start.3
  1.3 57.0 %copy-start = (f32[3,8,32,128]{3,2,1,0:T(8,128)S(1)}, f32[3,8,32,128]{3,2,1,0:T(8,128)}, u32[]{:S(2)}) copy-start(f32[3,8,32,128]{3,2,1,0:T(8,128)} %kappa_ref.5) | copy-start | bytes 1179652
  4.1 54.1 %copy-start.2 = (f32[8,32,128]{2,1,0:T(8,128)S(1)}, f32[8,32,128]{2,1,0:T(8,128)}, u32[]{:S(2)}) copy-start(f32[8,32,128]{2,1,0:T(8,128)} %sigma_ref.5) | copy-start | bytes 393220
  4.1 31.1 %all-to-all-start = ((f32[16,8,128]{2,1,0:T(8,128)}), f32[16,8,128]{2,1,0:T(8,128)S(1)}, u32[]{:S(2)}, u32[]{:S(2)}) async-start(f32[16,8,128]{2,1,0:T(8,128)} %get-tuple-element.31), calls=%async_computation | async-start | bytes 131072 | tf_op jit(solution)/shard_map/all_to_all | solution.py:612
  23.7 34.6 %copy-start.1 = (f32[8,32,128]{2,1,0:T(8,128)S(1)}, f32[8,32,128]{2,1,0:T(8,128)}, u32[]{:S(2)}) copy-start(f32[8,32,128]{2,1,0:T(8,128)} %r_ref.5) | copy-start | bytes 393220
  23.7 7.2 %collective-permute-start = (f32[8,128]{1,0:T(8,128)S(1)}, f32[8,128]{1,0:T(8,128)S(1)}, u32[]{:S(2)}, u32[]{:S(2)}) collective-permute-start(f32[8,128]{1,0:T(8,128)S(1)} %get-tuple-element.34), channel_id=1, source_target_pairs={{0,16},{16,32},{32,48},{48,64},{64,80},{80,96},{96,112},{112,0},{1... | collective-permute-start | bytes 12296 | tf_op jit(solution)/shard_map/ppermute | solution.py:607
  27.1 4.6 %collective-permute-start.1 = (f32[8,128]{1,0:T(8,128)S(1)}, f32[8,128]{1,0:T(8,128)S(1)}, u32[]{:S(2)}, u32[]{:S(2)}) collective-permute-start(f32[8,128]{1,0:T(8,128)S(1)} %get-tuple-element.35), channel_id=1, source_target_pairs={{16,0},{32,16},{48,32},{64,48},{80,64},{96,80},{112,96},{0,112},{1... | collective-permute-start | bytes 12296 | tf_op jit(solution)/shard_map/ppermute | solution.py:608
  36.6 21.7 %all-to-all-start.1 = ((f32[64,2,128]{2,1,0:T(2,128)}), f32[64,2,128]{2,1,0:T(2,128)S(1)}, u32[]{:S(2)}, u32[]{:S(2)}) async-start(f32[64,2,128]{2,1,0:T(2,128)} %get-tuple-element.36), calls=%async_computation.1 | async-start | bytes 131072 | tf_op jit(solution)/shard_map/all_to_all | solution.py:615
  48.8 2.5 %collective-permute-start.2 = (f32[32,128]{1,0:T(8,128)S(1)}, f32[32,128]{1,0:T(8,128)S(1)}, u32[]{:S(2)}, u32[]{:S(2)}) collective-permute-start(f32[32,128]{1,0:T(8,128)S(1)} %get-tuple-element.39), channel_id=1, source_target_pairs={{0,128},{128,256},{256,384},{384,512},{512,640},{640,768},{768,896... | collective-permute-start | bytes 49160 | tf_op jit(solution)/shard_map/ppermute | solution.py:605
  50.5 3.5 %collective-permute-start.3 = (f32[32,128]{1,0:T(8,128)S(1)}, f32[32,128]{1,0:T(8,128)S(1)}, u32[]{:S(2)}, u32[]{:S(2)}) collective-permute-start(f32[32,128]{1,0:T(8,128)S(1)} %get-tuple-element.40), channel_id=1, source_target_pairs={{128,0},{256,128},{384,256},{512,384},{640,512},{768,640},{896,768... | collective-permute-start | bytes 49160 | tf_op jit(solution)/shard_map/ppermute | solution.py:606
  79.7 9.9 %collective-permute-start.4 = (f32[32,128]{1,0:T(8,128)S(1)}, f32[32,128]{1,0:T(8,128)S(1)}, u32[]{:S(2)}, u32[]{:S(2)}) collective-permute-start(f32[32,128]{1,0:T(8,128)S(1)} %get-tuple-element.51), channel_id=1, source_target_pairs={{0,128},{128,256},{256,384},{384,512},{512,640},{640,768},{768,896... | collective-permute-start | bytes 49160 | tf_op jit(solution)/shard_map/ppermute | solution.py:605
  82.4 7.2 %collective-permute-start.5 = (f32[32,128]{1,0:T(8,128)S(1)}, f32[32,128]{1,0:T(8,128)S(1)}, u32[]{:S(2)}, u32[]{:S(2)}) collective-permute-start(f32[32,128]{1,0:T(8,128)S(1)} %get-tuple-element.52), channel_id=1, source_target_pairs={{128,0},{256,128},{384,256},{512,384},{640,512},{768,640},{896,768... | collective-permute-start | bytes 49160 | tf_op jit(solution)/shard_map/ppermute | solution.py:606
  82.4 6.5 %collective-permute-start.6 = (f32[8,128]{1,0:T(8,128)S(1)}, f32[8,128]{1,0:T(8,128)S(1)}, u32[]{:S(2)}, u32[]{:S(2)}) collective-permute-start(f32[8,128]{1,0:T(8,128)S(1)} %get-tuple-element.53), channel_id=1, source_target_pairs={{0,16},{16,32},{32,48},{48,64},{64,80},{80,96},{96,112},{112,0},{1... | collective-permute-start | bytes 12296 | tf_op jit(solution)/shard_map/ppermute | solution.py:607
  84.8 4.8 %collective-permute-start.7 = (f32[8,128]{1,0:T(8,128)S(1)}, f32[8,128]{1,0:T(8,128)S(1)}, u32[]{:S(2)}, u32[]{:S(2)}) collective-permute-start(f32[8,128]{1,0:T(8,128)S(1)} %get-tuple-element.54), channel_id=1, source_target_pairs={{16,0},{32,16},{48,32},{64,48},{80,64},{96,80},{112,96},{0,112},{1... | collective-permute-start | bytes 12296 | tf_op jit(solution)/shard_map/ppermute | solution.py:608

commit v4 on v3

--- a/solution.py
+++ b/solution.py
@@ -47,22 +47,43 @@
 
 
 def faces_of(field):
-    lane, row = iota((CX, CY, 128), 2), iota((CX, CY, 128), 1)
-    low = jnp.where(lane == LOW_AT + row, field[:, :, 0:1], 0.0)
-    both = jnp.where(lane == HIGH_AT + row, field[:, :, CZ - 1 : CZ], low)
-    return jnp.sum(both, axis=1)
-
-
-def write_z_message(zmsg_ref, rows, faces, spread_inverse, total, sizes):
-    lane = iota((8, 128), 1)
+    shape = (CX, CY, 128)
+    here = iota(shape, 2) == (iota(shape, 0) % 4) * 32 + iota(shape, 1)
+
+    def packed(z):
+        rows = jnp.sum(jnp.where(here, field[:, :, z : z + 1], 0.0), axis=1)
+        halves = [jnp.sum(rows[i : i + 4], axis=0, keepdims=True) for i in (0, 4)]
+        return jnp.concatenate(halves, axis=0)
+
+    return packed(0), packed(CZ - 1)
+
+
+def write_z_message(zmsg_ref, pairs, faces, spread_inverse, total, sizes):
+    nz, count = sizes[2], 2 + len(pairs)
+    mz = lax.axis_index("gz")
+    lane1, lane8, row8 = iota((1, 128), 1), iota((8, 128), 1), iota((8, 128), 0)
+    only = lambda v: jnp.where(lane1 < LINES, v, 0.0)
+    tails = [pltpu.roll(only(a), 96, 1) + pltpu.roll(only(b), 112, 1) if a is not None else None for a, b in pairs]
+    mine = spread_inverse * total
+    inside = lane8 // 24 == row8 % 4
     zero = jnp.zeros((1, 128), F32)
-    head = jnp.concatenate(rows + [zero] * (8 - len(rows)), axis=0)
-    base = jnp.where(lane < LINES, head, faces)
-    mine = spread_inverse * total
-    inside = (lane >= PART_AT) & (lane < PART_AT + 24)
-    for p in range(sizes[2]):
-        moved = pltpu.roll(mine, (PART_AT + 8 - 8 * p) % 128, 1)
-        zmsg_ref[p] = jnp.where(inside, moved, base)
+    for p in range(nz):
+        moved = jnp.where(inside, pltpu.roll(mine, (8 - 8 * p) % 128, 1), 0.0)
+        zmsg_ref[p * count] = zero
+        zmsg_ref[p * count + 1] = zero
+        for h, tail in enumerate(tails):
+            row = jnp.sum(moved[4 * h : 4 * h + 4], axis=0, keepdims=True) if h < 2 else zero
+            zmsg_ref[p * count + 2 + h] = row if tail is None else row + tail
+
+    @pl.when(mz > 0)
+    def _():
+        zmsg_ref[(mz - 1) * count] = faces[0][0:1]
+        zmsg_ref[(mz - 1) * count + 1] = faces[0][1:2]
+
+    @pl.when(mz < nz - 1)
+    def _():
+        zmsg_ref[(mz + 1) * count] = faces[1][0:1]
+        zmsg_ref[(mz + 1) * count + 1] = faces[1][1:2]
 
 
 def write_planes(field, planes):
@@ -114,19 +135,32 @@
         cur_first = cur_first + mu * cur
         cur = row(rhs, k + 1) + gam * cur
     move = one_where((iota((128, 128), 0) % 16) * 8 + iota((128, 128), 0) // 16 == iota((128, 128), 1))
-    spread_inverse = dot(inv_ref[...], move)
+    plain = dot(inv_ref[...], move)
+    step = iota((8, 128), 0) % 4
+    spread_inverse = plain
+    for k in range(1, 4):
+        spread_inverse = jnp.where(step == k, pltpu.roll(plain, 24 * k, 1), spread_inverse)
     spread_ref[...] = spread_inverse
-    rows = [cur_first, cur, first, mid, last, row(g, CELLS - 1)]
-    write_z_message(zmsg_ref, rows, faces_of(jac), spread_inverse, jnp.sum(r), sizes)
+    pairs = [(cur_first, cur), (first, mid), (last, row(g, CELLS - 1))]
+    write_z_message(zmsg_ref, pairs, faces_of(jac), spread_inverse, jnp.sum(r), sizes)
 
 
 def solve_chain(sizes, fresh, zrec_ref, loc_ref, alpha_ref, chain_ref, final_ref, sol_ref):
     nz = sizes[2]
     mz = lax.axis_index("gz")
-    used = iota((8, 128), 1) < LINES
-    tiles = [jnp.where(used, zrec_ref[p], 1.0) for p in range(nz)]
-    part = lambda p, i: tiles[p][i : i + 1, :]
+    count = 5 if fresh else 4
     zero = jnp.zeros((1, 128), F32)
+    columns = []
+    for h in range(count - 2 if fresh else 1):
+        rows = jnp.concatenate([zrec_ref[p * count + 2 + h] for p in range(nz)], axis=0)
+        used = iota(rows.shape, 1) < LINES
+        for shift in (32, 16):
+            columns.append(jnp.where(used, pltpu.roll(rows, shift, 1), 1.0))
+    part = lambda p, i: columns[i][p : p + 1, :]
+
+    def mine(i):
+        row = pltpu.roll(zrec_ref[mz * count + 2 + i // 2], 32 - 16 * (i % 2), 1)
+        return jnp.where(iota((1, 128), 1) < LINES, row, 1.0)
 
     if fresh:
         one = zero + 1.0
@@ -165,17 +199,15 @@
         right_cond, right_hold, right_ginv = cond_own, hold, 1.0 / ginv
         for c, p in ((0, nz - 1), (1, nz - 1), (2, 0), (3, 0)):
             chain_ref[c, p : p + 1, :] = zero
-        mine = jnp.where(used, zrec_ref[mz], 1.0)
-        big_a = mine[2:3, :] + left_cond
-        big_b = mine[4:5, :] + right_cond
-        m = mine[3:4, :]
+        big_a = mine(2) + left_cond
+        big_b = mine(4) + right_cond
+        m = mine(3)
         det_inv = 1.0 / (big_a * m + big_b * m + big_a * big_b)
         f1, f2, f3 = (big_b + m) * det_inv, m * det_inv, (big_a + m) * det_inv
         final_ref[...] = jnp.concatenate(
             [f1, f2, f3, left_ginv, left_hold, right_ginv, right_hold, zero], axis=0
         )
     else:
-        mine = jnp.where(used, zrec_ref[mz], 0.0)
         f1, f2, f3, left_ginv, left_hold, right_ginv, right_hold = [
             final_ref[i : i + 1, :] for i in range(7)
         ]
@@ -188,8 +220,8 @@
     for p in range(nz - 1, 0, -1):
         cur = chain(2, p) * (part(p, 1) + cur) + chain(3, p) * part(p, 0)
         cur_right = jnp.where(mz == p - 1, cur, cur_right)
-    cur_first = mine[0:1, :] + cur_left
-    cur_last = mine[1:2, :] + cur_right
+    cur_first = mine(0) + cur_left
+    cur_last = mine(1) + cur_right
     sol_first = f1 * cur_first + f2 * cur_last
     sol_last = f2 * cur_first + f3 * cur_last
     below = cur_left * left_ginv + left_hold * sol_first
@@ -222,11 +254,22 @@
         (lane >= LOW_AT) & (lane < HIGH_AT) & ((lane - LOW_AT) // 4 == line % 8) & (line < LINES)
     )
     lines_part = dot(jnp.where(of_row, below, 0.0), to_high) + dot(jnp.where(of_row, above, 0.0), to_low)
-    from_below = zrec_ref[jnp.maximum(mz - 1, 0)]
-    from_above = zrec_ref[jnp.minimum(mz + 1, nz - 1)]
-    face = jnp.where(lane8 >= HIGH_AT, from_below, from_above)
+    face = jnp.zeros((8, 128), F32)
+    for peer, at in ((jnp.maximum(mz - 1, 0), HIGH_AT), (jnp.minimum(mz + 1, nz - 1), LOW_AT)):
+        packed = jnp.where(row8 < 4, zrec_ref[peer * count], zrec_ref[peer * count + 1])
+        for k in range(4):
+            here = (lane8 // 32 == at // 32) & (row8 % 4 == k)
+            face = jnp.where(here, pltpu.roll(packed, (at - 32 * k) % 128, 1), face)
     zhalo = jnp.where(lane8 >= LOW_AT, face + THETA * lines_part, 0.0)
     return x_low, x_high, y_low, y_high, zhalo
+
+
+def coarse_totals(zrec_ref, count, nz):
+    totals = [zrec_ref[2], zrec_ref[3]]
+    for p in range(1, nz):
+        for h in range(2):
+            totals[h] = totals[h] + zrec_ref[p * count + 2 + h]
+    return totals
 
 
 def first_lines_kernel(
@@ -238,22 +281,24 @@
         sizes, True, zrec_ref, loc_ref, alpha_ref, chain_ref, final_ref, sol_ref
     )
     zero = jnp.zeros((1, 128), F32)
-    lane8 = iota((8, 128), 1)
     own_ref[...] = jnp.concatenate([x_low, x_high] + [zero] * 6, axis=0)
     zhalo_ref[...] = zhalo
 
-    total = zrec_ref[0]
-    for p in range(1, nz):
-        total = total + zrec_ref[p]
-    at = lambda lo: (lane8 >= lo) & (lane8 < lo + 8)
-    x_less = pltpu.roll(pltpu.roll(total, 1, 0), 16, 1)
-    x_more = pltpu.roll(pltpu.roll(total, 7, 0), 24, 1)
-    sums = jnp.where((lane8 >= PART_AT) & (lane8 < PART_AT + 24), total, 0.0)
-    sums = jnp.where(at(PART_AT + 24), x_less, sums)
-    sums = jnp.where(at(PART_AT + 32), x_more, sums)
+    totals = coarse_totals(zrec_ref, 5, nz)
+    lane1 = iota((1, 128), 1)
+
+    def block(i, width, at, offset):
+        moved = pltpu.roll(totals[i // 4], (at - 24 * (i % 4) - offset) % 128, 1)
+        return jnp.where((lane1 >= at) & (lane1 < at + width), moved, 0.0)
+
     second = iota((2, 128), 0) == 1
     for i in range(nx):
-        both = jnp.where(second, sums[i : i + 1, :], 0.0)
+        sums = block(i, 24, PART_AT, 0)
+        if i > 0:
+            sums = sums + block(i - 1, 8, PART_AT + 24, 8)
+        if i < nx - 1:
+            sums = sums + block(i + 1, 8, PART_AT + 32, 8)
+        both = jnp.where(second, sums, 0.0)
         for j in range(ny):
             xmsg_ref[i * ny + j] = both
     here = mx * ny + my
@@ -379,7 +424,7 @@
         cur_first = cur_first + loc_ref[0, k : k + 1, :] * cur
         cur = row(rhs, k + 1) + loc_ref[1, k : k + 1, :] * cur
     write_z_message(
-        zmsg_ref, [cur_first, cur], faces_of(jac_ref[...]), spread_ref[...], jnp.sum(field), sizes
+        zmsg_ref, [(cur_first, cur), (None, None)], faces_of(jac_ref[...]), spread_ref[...], jnp.sum(field), sizes
     )
 
 
@@ -395,10 +440,8 @@
     for x in range(CX):
         z_ref[x] = jac_ref[x] + lines[(x // 4) * 32 : (x // 4) * 32 + 32]
     write_planes(z_ref[...], (xlo, xhi, ylo, yhi))
-    total = zrec_ref[0]
-    for p in range(1, sizes[2]):
-        total = total + zrec_ref[p]
-    part_ref[...] = total
+    zero = jnp.zeros((1, 128), F32)
+    part_ref[...] = jnp.concatenate(coarse_totals(zrec_ref, 4, sizes[2]) + [zero] * 6, axis=0)
 
 
 FACES = range(1, 7)
@@ -410,7 +453,7 @@
     + [("g22", j, k) for j in FACES for k in FACES if j < k and (j - 1) // 2 != (k - 1) // 2]
 )
 NAMES = ("g11", "g12", "g22", "h1", "h2")
-TERMS_AT = 72
+TERMS_AT, TERMS_ROW = 96, 32
 
 
 def second_kernel(
@@ -480,13 +523,11 @@
             stop = -(-i // 8) * 8
             terms_ref[i:stop, :] = jnp.zeros((stop - i, 128), F32)
     poly = dot_t(jnp.full((8, 128), 1.0, F32), terms_ref[...])[0:1, :]
-    part = part_ref[...]
-    lane8 = iota((8, 128), 1)
-    part = jnp.where((lane8 >= PART_AT) & (lane8 < PART_AT + 24), part, 0.0)
-    at = lambda i, lane: pltpu.roll(part, (lane - PART_AT) % 128, 1)[i : i + 1, :]
-    upper = at(0, 0) + at(1, 24) + at(2, 48) + at(3, 72) + at(4, 96)
-    lower = at(5, 0) + at(6, 24) + at(7, 48) + pltpu.roll(poly, TERMS_AT, 1)
-    both = jnp.concatenate([upper, lower], axis=0)
+    halves = [
+        jnp.where(lane1 < TERMS_AT, part_ref[h : h + 1, :], pltpu.roll(poly, TERMS_AT - TERMS_ROW * h, 1))
+        for h in range(2)
+    ]
+    both = jnp.concatenate(halves, axis=0)
     for q in range(nx * ny):
         xmsg_ref[q] = both
 
@@ -497,15 +538,16 @@
     count = nx * ny
     total = xrec_ref[0]
     for q in range(count):
-        flat_ref[q : q + 1, :] = xrec_ref[q, 1:2, :]
+        for h in range(2):
+            flat_ref[h, q : q + 1, :] = xrec_ref[q, h : h + 1, :]
         if q > 0:
             total = total + xrec_ref[q]
     lane, row = iota((count, 128), 1), iota((count, 128), 0)
     tx, ty = row // ny, row % ny
 
     def value(qx, qy, dz, valid):
-        at = jnp.where(qx < 5, qx * 24, (qx - 5) * 24) + 8 + 8 * dz + qy
-        chosen = jnp.where(qx < 5, total[0:1, :], total[1:2, :])
+        at = (qx & 3) * 24 + 8 + 8 * dz + qy
+        chosen = jnp.where(qx < 4, total[0:1, :], total[1:2, :])
         return jnp.sum(jnp.where((lane == at) & valid, chosen, 0.0), axis=1, keepdims=True)
 
     always = row >= 0
@@ -519,29 +561,32 @@
         value(tx, ty, 1, always & (mz < nz - 1)),
     ]
     v = [c] + [c - n for n in near]
-    first = jnp.where(lane < 0, 1.0, 0.0)
-    second = first
-    for j in range(-1, 7):
-        amount = 1.0 if j == -1 else v[j]
-        is_first = lane < 0
-        is_second = is_first
-        for i, (_, a, b) in enumerate(TERMS):
-            if a == j:
-                is_first = is_first | (lane == TERMS_AT + i)
-            if b == j:
-                is_second = is_second | (lane == TERMS_AT + i)
-        first = jnp.where(is_first, amount, first)
-        second = jnp.where(is_second, amount, second)
-    terms = jnp.where(lane >= TERMS_AT, flat_ref[...], 0.0)
-    added = jnp.sum(terms * first * second, axis=0, keepdims=True)
     lane1 = iota((1, 128), 1)
     out = jnp.zeros((1, 128), F32)
-    for n, name in enumerate(NAMES):
-        mask = lane1 < 0
-        for i, (of, _, _) in enumerate(TERMS):
-            if of == name:
-                mask = mask | (lane1 == TERMS_AT + i)
-        out = jnp.where(lane1 == n, jnp.sum(jnp.where(mask, added, 0.0), axis=1, keepdims=True), out)
+    for h in range(2):
+        terms = list(enumerate(TERMS[TERMS_ROW * h : TERMS_ROW * (h + 1)], TERMS_AT))
+        first = jnp.where(lane < 0, 1.0, 0.0)
+        second = first
+        for j in range(-1, 7):
+            amount = 1.0 if j == -1 else v[j]
+            is_first = lane < 0
+            is_second = is_first
+            for i, (_, a, b) in terms:
+                if a == j:
+                    is_first = is_first | (lane == i)
+                if b == j:
+                    is_second = is_second | (lane == i)
+            first = jnp.where(is_first, amount, first)
+            second = jnp.where(is_second, amount, second)
+        weights = jnp.where(lane >= TERMS_AT, flat_ref[h], 0.0)
+        added = jnp.sum(weights * first * second, axis=0, keepdims=True)
+        for n, name in enumerate(NAMES):
+            mask = lane1 < 0
+            for i, (of, _, _) in terms:
+                if of == name:
+                    mask = mask | (lane1 == i)
+            add = jnp.sum(jnp.where(mask, added, 0.0), axis=1, keepdims=True)
+            out = jnp.where(lane1 == n, out + add, out)
     sums_ref[...] = out
     mine = row == mx * ny + my
     for j in range(7):
@@ -595,7 +640,7 @@
     nx, ny, nz = sizes
     field, plane, tile, coarse = (CX, CY, CZ), (CY, CZ), (8, 128), (CELLS, 128)
     planes = [plane, plane, tile, tile]
-    to_z, to_xy = (nz, 8, 128), (nx * ny, 2, 128)
+    to_xy = (nx * ny, 2, 128)
 
     def halo(parts):
         xlo, xhi, ylo, yhi = parts
@@ -616,7 +661,7 @@
 
     bind = lambda kernel, *a: functools.partial(kernel, sizes, *a)
     zmsg, loc, alpha, spread, *sides = call(
-        bind(begin_kernel), [to_z, (3, *coarse), coarse, tile, *planes],
+        bind(begin_kernel), [(nz * 5, 1, 128), (3, *coarse), coarse, tile, *planes],
         [field, field, (3, *field), tile], "begin", pltpu.HBM, [pltpu.SemaphoreType.DMA((4,))], 55100 << 10,
     )(r, sigma, kappa, inverse_rows)
     zrec = along_z(zmsg)
@@ -626,7 +671,7 @@
     )(zrec, loc, alpha, *halos[2:])
     xrec = along_xy(xmsg)
     z1, w1, jac, zmsg, alpha = call(
-        bind(first_kernel), [field, field, field, to_z, coarse], name="operator_first"
+        bind(first_kernel), [field, field, field, (nz * 4, 1, 128), coarse], name="operator_first"
     )(r, sigma, kappa, xrec, own, zhalo, *halos, loc, spread)
     zrec = along_z(zmsg)
     part, zhalo, z2, *sides = call(
@@ -637,7 +682,7 @@
         r, w1, sigma, kappa, z2, zhalo, part, *halos
     )
     xrec = along_xy(xmsg)
-    sums, values = call(bind(plane_kernel), [(1, 128), tile], [(nx * ny, 128)], "plane")(xrec)
+    sums, values = call(bind(plane_kernel), [(1, 128), tile], [(2, nx * ny, 128)], "plane")(xrec)
     sums = along_z(jnp.broadcast_to(sums[None], (nz, 1, 128)))
     return tuple(
         call(end_kernel, [field, field], name="end")(sums, values, r, sigma, kappa, z1, w1, z2, w2)

time: 125 us -> 125 us (level)
  no operation moved by 1% of the time
where the time goes in v4:
time: 125 us; the launch traced here: 124 us
  blocking collectives  51.9 us (42%)
  starting transfers between devices  49.6 us (40%)
  waiting for transfers between devices  12.9 us (10%)
  Pallas kernels  8.21 us (7%)
    all_to_all x2, blocking collectives, along_z(): lax.all_to_all(message, 'gz', split_axis=0, concat_axis=0, tiled=True)  33.6 us
    all_to_all x1, starting transfers between devices, along_z(): lax.all_to_all(message, 'gz', split_axis=0, concat_axis=0, tiled=True)  19.6 us
    all_to_all x1, blocking collectives, along_xy(): lax.all_to_all(message, ('gx', 'gy'), split_axis=0, concat_axis=0, tiled=...  18.4 us
    all_to_all x1, starting transfers between devices, along_xy(): lax.all_to_all(message, ('gx', 'gy'), split_axis=0, concat_axis=0, tiled=...  12.2 us
    pallas_call x7, Pallas kernels, run(): pl.pallas_call(kernel, out_shape=[jax.ShapeDtypeStruct(s, F32) for s in o...  8.21 us
    ppermute x2, starting transfers between devices, halo(): lax.ppermute(ylo, 'gy', down(ny))  7.94 us
    ppermute x2, starting transfers between devices, halo(): lax.ppermute(yhi, 'gy', up(ny))  5.69 us
    all_to_all x1, waiting for transfers between devices, along_xy(): lax.all_to_all(message, ('gx', 'gy'), split_axis=0, concat_axis=0, tiled=...  4.31 us
  transfers between devices with their start and end apart: 10, of which 6 were waited for; matrix products, arithmetic and copies ran while one was open for 0% of the time, Pallas kernels for 0%

profile of v4, /device:TPU:1, one launch (start us, length us, event | category | flops | bytes accessed | tf_op | source)
XLA Modules:
  0.0 124.1 jit_solution(4521982575133564580)
XLA Ops:
  0.6 0.0 copy-start.3
  0.6 0.7 copy-done.3
  1.3 0.0 copy-start
  1.3 2.9 %begin.1 = (f32[80,1,128]{2,1,0:T(1,128)}, f32[3,16,128]{2,1,0:T(8,128)S(1)}, f32[16,128]{1,0:T(8,128)S(1)}, f32[8,128]{1,0:T(8,128)S(1)}, f32[32,128]{1,0:T(8,1...) custom-call(f32[8,32,128]{2,1,0:T(8,128)} %r_ref.5, f32[8,32,128]{2,1,0:T(8,128)} %sigma_ref.5, ...), custom_call_target="tpu_custom_call" | custom-call | tf_op jit(solution)/shard_map/begin/pallas_call | solution.py:626
  4.2 0.0 copy-start.2
  4.2 19.6 %all-to-all-start = ((f32[80,1,128]{2,1,0:T(1,128)}), f32[80,1,128]{2,1,0:T(1,128)S(1)}, u32[]{:S(2)}, u32[]{:S(2)}) async-start(f32[80,1,128]{2,1,0:T(1,128)} %get-tuple-element.31), calls=%async_computation | async-start | bytes 81920 | tf_op jit(solution)/shard_map/all_to_all | solution.py:657
  23.8 0.0 copy-start.1
  23.8 3.3 %collective-permute-start = (f32[8,128]{1,0:T(8,128)S(1)}, f32[8,128]{1,0:T(8,128)S(1)}, u32[]{:S(2)}, u32[]{:S(2)}) collective-permute-start(f32[8,128]{1,0:T(8,128)S(1)} %get-tuple-element.34), channel_id=1, source_target_pairs={{0,16},{16,32},{32,48},{48,64},{64,80},{80,96},{96,112},{112,0},{1... | collective-permute-start | bytes 12296 | tf_op jit(solution)/shard_map/ppermute | solution.py:652
  27.1 3.8 %collective-permute-start.1 = (f32[8,128]{1,0:T(8,128)S(1)}, f32[8,128]{1,0:T(8,128)S(1)}, u32[]{:S(2)}, u32[]{:S(2)}) collective-permute-start(f32[8,128]{1,0:T(8,128)S(1)} %get-tuple-element.35), channel_id=1, source_target_pairs={{16,0},{32,16},{48,32},{64,48},{80,64},{96,80},{112,96},{0,112},{1... | collective-permute-start | bytes 12296 | tf_op jit(solution)/shard_map/ppermute | solution.py:653
  31.0 0.0 collective-permute-done.h2
  31.0 0.8 collective-permute-done.1.h3
  31.8 3.5 %all-to-all-done.zrec_ref = f32[80,1,128]{2,1,0:T(1,128)S(1)} async-done(((f32[80,1,128]{2,1,0:T(1,128)}), f32[80,1,128]{2,1,0:T(1,128)S(1)}, u32[]{:S(2)}, u32[]{:S(2)}) %all-to-all-start) | async-done | bytes 40992 | tf_op jit(solution)/shard_map/all_to_all | solution.py:657
  35.3 1.3 %lines_first.1 = (f32[64,2,128]{2,1,0:T(2,128)}, f32[8,128]{1,0:T(8,128)S(1)}, f32[8,128]{1,0:T(8,128)S(1)}, f32[4,16,128]{2,1,0:T(8,128)S(1)}, f32[8,128]{1,0:T(8,128)S(1)}) custom-call(f32[80,1,128]{2,1,0:T(1,128)S(1)} %all-to-all-done.zrec_ref, f32[3,16,128]{2,1,0:T(8,128)S(1)} %get-tuple-element.32.loc_ref, f32[16,128]{1,0:T(8,128)S(1)} %get-tuple-element.33.alpha_ref, ...), custom_call_target="tpu_custom_call" | custom-call | tf_op jit(solution)/shard_map/lines_first/pallas_call | solution.py:626
  36.6 12.2 %all-to-all-start.1 = ((f32[64,2,128]{2,1,0:T(2,128)}), f32[64,2,128]{2,1,0:T(2,128)S(1)}, u32[]{:S(2)}, u32[]{:S(2)}) async-start(f32[64,2,128]{2,1,0:T(2,128)} %get-tuple-element.36), calls=%async_computation.1 | async-start | bytes 131072 | tf_op jit(solution)/shard_map/all_to_all | solution.py:660
  48.8 1.6 %collective-permute-start.2 = (f32[32,128]{1,0:T(8,128)S(1)}, f32[32,128]{1,0:T(8,128)S(1)}, u32[]{:S(2)}, u32[]{:S(2)}) collective-permute-start(f32[32,128]{1,0:T(8,128)S(1)} %get-tuple-element.39), channel_id=1, source_target_pairs={{0,128},{128,256},{256,384},{384,512},{512,640},{640,768},{768,896... | collective-permute-start | bytes 49160 | tf_op jit(solution)/shard_map/ppermute | solution.py:650
  50.5 0.0 collective-permute-start.3
  50.5 0.9 collective-permute-done.2.h0
  51.3 2.6 %collective-permute-done.3.h1 = f32[32,128]{1,0:T(8,128)S(1)} collective-permute-done((f32[32,128]{1,0:T(8,128)S(1)}, f32[32,128]{1,0:T(8,128)S(1)}, u32[]{:S(2)}, u32[]{:S(2)}) %collective-permute-start.3) | collective-permute-done | bytes 16416 | tf_op jit(solution)/shard_map/ppermute | solution.py:651
  53.9 4.3 %all-to-all-done.1.xrec_ref = f32[64,2,128]{2,1,0:T(2,128)S(1)} async-done(((f32[64,2,128]{2,1,0:T(2,128)}), f32[64,2,128]{2,1,0:T(2,128)S(1)}, u32[]{:S(2)}, u32[]{:S(2)}) %all-to-all-start.1) | async-done | bytes 65568 | tf_op jit(solution)/shard_map/all_to_all | solution.py:660
  58.3 0.0 copy-done
  58.3 0.0 copy-done.2
  58.3 0.0 copy-done.1
  58.3 1.2 operator_first.1
  59.5 19.7 %all_to_all.25.zrec_ref = f32[64,1,128]{2,1,0:T(1,128)S(1)} all-to-all(f32[64,1,128]{2,1,0:T(1,128)S(1)} %get-tuple-element.43), channel_id=1, replica_groups=mesh['gx'=8,'gy'=8,'gz'=16] {'gz'}, dimensions={0} | all-to-all | bytes 65536 | tf_op jit(solution)/shard_map/all_to_all | solution.py:657
  79.2 0.6 lines_second.1
  79.9 2.7 %collective-permute-start.4 = (f32[32,128]{1,0:T(8,128)S(1)}, f32[32,128]{1,0:T(8,128)S(1)}, u32[]{:S(2)}, u32[]{:S(2)}) collective-permute-start(f32[32,128]{1,0:T(8,128)S(1)} %get-tuple-element.51), channel_id=1, source_target_pairs={{0,128},{128,256},{256,384},{384,512},{512,640},{640,768},{768,896... | collective-permute-start | bytes 49160 | tf_op jit(solution)/shard_map/ppermute | solution.py:650
  82.5 0.0 collective-permute-start.5
  82.5 2.4 %collective-permute-start.6 = (f32[8,128]{1,0:T(8,128)S(1)}, f32[8,128]{1,0:T(8,128)S(1)}, u32[]{:S(2)}, u32[]{:S(2)}) collective-permute-start(f32[8,128]{1,0:T(8,128)S(1)} %get-tuple-element.53), channel_id=1, source_target_pairs={{0,16},{16,32},{32,48},{48,64},{64,80},{80,96},{96,112},{112,0},{1... | collective-permute-start | bytes 12296 | tf_op jit(solution)/shard_map/ppermute | solution.py:652
  84.9 4.1 %collective-permute-start.7 = (f32[8,128]{1,0:T(8,128)S(1)}, f32[8,128]{1,0:T(8,128)S(1)}, u32[]{:S(2)}, u32[]{:S(2)}) collective-permute-start(f32[8,128]{1,0:T(8,128)S(1)} %get-tuple-element.54), channel_id=1, source_target_pairs={{16,0},{32,16},{48,32},{64,48},{80,64},{96,80},{112,96},{0,112},{1... | collective-permute-start | bytes 12296 | tf_op jit(solution)/shard_map/ppermute | solution.py:653
  89.0 0.0 collective-permute-done.6.h2
  89.0 0.7 collective-permute-done.7.h3
  89.7 0.0 collective-permute-done.4.h0
  89.7 0.0 collective-permute-done.5.h1
  89.7 1.0 operator_second.1
  90.7 18.4 %all_to_all.26.xrec_ref = f32[64,2,128]{2,1,0:T(2,128)S(1)} all-to-all(f32[64,2,128]{2,1,0:T(2,128)S(1)} %get-tuple-element.55), channel_id=1, replica_groups=mesh['gx'=8,'gy'=8,'gz'=16] {'gx','gy'}, dimensions={0} | all-to-all | bytes 131072 | tf_op jit(solution)/shard_map/all_to_all | solution.py:660
  109.1 0.3 plane.1
  109.5 13.8 %all_to_all.27.all_ref = f32[16,1,128]{2,1,0:T(1,128)S(1)} all-to-all(f32[16,1,128]{2,1,0:T(1,128)S(1)} %broadcast_in_dim.9), channel_id=1, replica_groups=mesh['gx'=8,'gy'=8,'gz'=16] {'gz'}, dimensions={0} | all-to-all | bytes 16384 | tf_op jit(solution)/shard_map/all_to_all | solution.py:657
  123.3 0.8 end.1
  (1 shorter events, 0.0 us)
Async XLA Ops:
  0.6 0.7 copy-start.3
  1.3 56.9 %copy-start = (f32[3,8,32,128]{3,2,1,0:T(8,128)S(1)}, f32[3,8,32,128]{3,2,1,0:T(8,128)}, u32[]{:S(2)}) copy-start(f32[3,8,32,128]{3,2,1,0:T(8,128)} %kappa_ref.5) | copy-start | bytes 1179652
  4.2 54.1 %copy-start.2 = (f32[8,32,128]{2,1,0:T(8,128)S(1)}, f32[8,32,128]{2,1,0:T(8,128)}, u32[]{:S(2)}) copy-start(f32[8,32,128]{2,1,0:T(8,128)} %sigma_ref.5) | copy-start | bytes 393220
  4.2 31.1 %all-to-all-start = ((f32[80,1,128]{2,1,0:T(1,128)}), f32[80,1,128]{2,1,0:T(1,128)S(1)}, u32[]{:S(2)}, u32[]{:S(2)}) async-start(f32[80,1,128]{2,1,0:T(1,128)} %get-tuple-element.31), calls=%async_computation | async-start | bytes 81920 | tf_op jit(solution)/shard_map/all_to_all | solution.py:657
  23.8 34.5 %copy-start.1 = (f32[8,32,128]{2,1,0:T(8,128)S(1)}, f32[8,32,128]{2,1,0:T(8,128)}, u32[]{:S(2)}) copy-start(f32[8,32,128]{2,1,0:T(8,128)} %r_ref.5) | copy-start | bytes 393220
  23.8 7.2 %collective-permute-start = (f32[8,128]{1,0:T(8,128)S(1)}, f32[8,128]{1,0:T(8,128)S(1)}, u32[]{:S(2)}, u32[]{:S(2)}) collective-permute-start(f32[8,128]{1,0:T(8,128)S(1)} %get-tuple-element.34), channel_id=1, source_target_pairs={{0,16},{16,32},{32,48},{48,64},{64,80},{80,96},{96,112},{112,0},{1... | collective-permute-start | bytes 12296 | tf_op jit(solution)/shard_map/ppermute | solution.py:652
  27.1 4.6 %collective-permute-start.1 = (f32[8,128]{1,0:T(8,128)S(1)}, f32[8,128]{1,0:T(8,128)S(1)}, u32[]{:S(2)}, u32[]{:S(2)}) collective-permute-start(f32[8,128]{1,0:T(8,128)S(1)} %get-tuple-element.35), channel_id=1, source_target_pairs={{16,0},{32,16},{48,32},{64,48},{80,64},{96,80},{112,96},{0,112},{1... | collective-permute-start | bytes 12296 | tf_op jit(solution)/shard_map/ppermute | solution.py:653
  36.6 21.6 %all-to-all-start.1 = ((f32[64,2,128]{2,1,0:T(2,128)}), f32[64,2,128]{2,1,0:T(2,128)S(1)}, u32[]{:S(2)}, u32[]{:S(2)}) async-start(f32[64,2,128]{2,1,0:T(2,128)} %get-tuple-element.36), calls=%async_computation.1 | async-start | bytes 131072 | tf_op jit(solution)/shard_map/all_to_all | solution.py:660
  48.8 2.5 %collective-permute-start.2 = (f32[32,128]{1,0:T(8,128)S(1)}, f32[32,128]{1,0:T(8,128)S(1)}, u32[]{:S(2)}, u32[]{:S(2)}) collective-permute-start(f32[32,128]{1,0:T(8,128)S(1)} %get-tuple-element.39), channel_id=1, source_target_pairs={{0,128},{128,256},{256,384},{384,512},{512,640},{640,768},{768,896... | collective-permute-start | bytes 49160 | tf_op jit(solution)/shard_map/ppermute | solution.py:650
  50.5 3.5 %collective-permute-start.3 = (f32[32,128]{1,0:T(8,128)S(1)}, f32[32,128]{1,0:T(8,128)S(1)}, u32[]{:S(2)}, u32[]{:S(2)}) collective-permute-start(f32[32,128]{1,0:T(8,128)S(1)} %get-tuple-element.40), channel_id=1, source_target_pairs={{128,0},{256,128},{384,256},{512,384},{640,512},{768,640},{896,768... | collective-permute-start | bytes 49160 | tf_op jit(solution)/shard_map/ppermute | solution.py:651
  79.9 9.9 %collective-permute-start.4 = (f32[32,128]{1,0:T(8,128)S(1)}, f32[32,128]{1,0:T(8,128)S(1)}, u32[]{:S(2)}, u32[]{:S(2)}) collective-permute-start(f32[32,128]{1,0:T(8,128)S(1)} %get-tuple-element.51), channel_id=1, source_target_pairs={{0,128},{128,256},{256,384},{384,512},{512,640},{640,768},{768,896... | collective-permute-start | bytes 49160 | tf_op jit(solution)/shard_map/ppermute | solution.py:650
  82.5 7.2 %collective-permute-start.5 = (f32[32,128]{1,0:T(8,128)S(1)}, f32[32,128]{1,0:T(8,128)S(1)}, u32[]{:S(2)}, u32[]{:S(2)}) collective-permute-start(f32[32,128]{1,0:T(8,128)S(1)} %get-tuple-element.52), channel_id=1, source_target_pairs={{128,0},{256,128},{384,256},{512,384},{640,512},{768,640},{896,768... | collective-permute-start | bytes 49160 | tf_op jit(solution)/shard_map/ppermute | solution.py:651
  82.5 6.5 %collective-permute-start.6 = (f32[8,128]{1,0:T(8,128)S(1)}, f32[8,128]{1,0:T(8,128)S(1)}, u32[]{:S(2)}, u32[]{:S(2)}) collective-permute-start(f32[8,128]{1,0:T(8,128)S(1)} %get-tuple-element.53), channel_id=1, source_target_pairs={{0,16},{16,32},{32,48},{48,64},{64,80},{80,96},{96,112},{112,0},{1... | collective-permute-start | bytes 12296 | tf_op jit(solution)/shard_map/ppermute | solution.py:652
  84.9 4.9 %collective-permute-start.7 = (f32[8,128]{1,0:T(8,128)S(1)}, f32[8,128]{1,0:T(8,128)S(1)}, u32[]{:S(2)}, u32[]{:S(2)}) collective-permute-start(f32[8,128]{1,0:T(8,128)S(1)} %get-tuple-element.54), channel_id=1, source_target_pairs={{16,0},{32,16},{48,32},{64,48},{80,64},{96,80},{112,96},{0,112},{1... | collective-permute-start | bytes 12296 | tf_op jit(solution)/shard_map/ppermute | solution.py:653

commit v5 on v4

--- a/solution.py
+++ b/solution.py
@@ -101,18 +101,23 @@
 ):
     pairs = ((kappa_hbm, kappa_ref), (sigma_hbm, sigma_ref), (r_hbm, r_ref), (inv_hbm, inv_ref))
     copies = [pltpu.make_async_copy(a, b, sems.at[i]) for i, (a, b) in enumerate(pairs)]
-    for copy in copies:
-        copy.start()
-    for copy in copies:
-        copy.wait()
-    r, sigma = r_ref[...], sigma_ref[...]
+    for i in (2, 1, 3, 0):
+        copies[i].start()
+    unused = iota((CELLS, 128), 1) >= LINES
+    copies[2].wait()
+    r = r_ref[...]
+    rhs = lines_of(r)
+    copies[1].wait()
+    sigma = sigma_ref[...]
+    e = jnp.where(unused, 1.0, lines_of(sigma))
+    copies[3].wait()
+    move = one_where((iota((128, 128), 0) % 16) * 8 + iota((128, 128), 0) // 16 == iota((128, 128), 1))
+    plain = dot(inv_ref[...], move)
+    copies[0].wait()
     kx, ky, kz = kappa_ref[0], kappa_ref[1], kappa_ref[2]
     jac = r * (WEIGHT / (sigma + 2.0 * (kx + ky + kz)))
     write_planes(jac, (xlo, xhi, ylo, yhi))
-    unused = iota((CELLS, 128), 1) >= LINES
-    e = jnp.where(unused, 1.0, lines_of(sigma))
     g = jnp.where(unused, 1.0, lines_of(kz) * 0.125)
-    rhs = lines_of(r)
     row = lambda a, k: a[k : k + 1, :]
     first, mid, last = row(e, 0), row(g, 0), row(e, 1)
     cur_first, cur = row(rhs, 0), row(rhs, 1)
@@ -134,8 +139,6 @@
         last = row(e, k + 1) + gam * last
         cur_first = cur_first + mu * cur
         cur = row(rhs, k + 1) + gam * cur
-    move = one_where((iota((128, 128), 0) % 16) * 8 + iota((128, 128), 0) // 16 == iota((128, 128), 1))
-    plain = dot(inv_ref[...], move)
     step = iota((8, 128), 0) % 4
     spread_inverse = plain
     for k in range(1, 4):
@@ -644,8 +647,8 @@
 
     def halo(parts):
         xlo, xhi, ylo, yhi = parts
-        up = lambda n: [(i, (i + 1) % n) for i in range(n)]
-        down = lambda n: [((i + 1) % n, i) for i in range(n)]
+        up = lambda n: [(i, i + 1) for i in range(n - 1)]
+        down = lambda n: [(i + 1, i) for i in range(n - 1)]
         return (
             lax.ppermute(xhi, "gx", up(nx)),
             lax.ppermute(xlo, "gx", down(nx)),

time: 125 us -> 131 us (1.048)
  starting transfers between devices: 49.6 us -> 51.9 us
  blocking collectives: 51.9 us -> 53.8 us
    ppermute x2, starting transfers between devices: 7.94 us -> 2.58 us  [halo(): lax.ppermute(ylo, 'gy', down(ny))]
    ppermute x2, waiting for transfers between devices: 1.54 us -> 6.38 us  [halo(): lax.ppermute(ylo, 'gy', down(ny))]
    ppermute x2, starting transfers between devices: 0.01 us -> 3.84 us  [halo(): lax.ppermute(xlo, 'gx', down(nx))]
    all_to_all x1, waiting for transfers between devices: 4.31 us -> 0.54 us  [along_xy(): lax.all_to_all(message, ('gx', 'gy'), split_axis=0, concat_axis=0, tiled=...]
    ppermute x2, starting transfers between devices: 4.3 us -> 8.04 us  [halo(): lax.ppermute(xhi, 'gx', up(nx))]
    all_to_all x1, blocking collectives: 18.4 us -> 20.3 us  [along_xy(): lax.all_to_all(message, ('gx', 'gy'), split_axis=0, concat_axis=0, tiled=...]
  transfers between devices with their start and end apart: 10 -> 10, of which waited for: 6 -> 5; matrix products, arithmetic and copies ran while one was open for 0% -> 0% of each run, Pallas kernels for 0% -> 0%
where the time goes in v5:
time: 131 us; the launch traced here: 130 us
  blocking collectives  53.8 us (41%)
  starting transfers between devices  51.9 us (40%)
  waiting for transfers between devices  13.9 us (11%)
  Pallas kernels  8.96 us (7%)
    all_to_all x2, blocking collectives, along_z(): lax.all_to_all(message, 'gz', split_axis=0, concat_axis=0, tiled=True)  33.6 us
    all_to_all x1, blocking collectives, along_xy(): lax.all_to_all(message, ('gx', 'gy'), split_axis=0, concat_axis=0, tiled=...  20.3 us
    all_to_all x1, starting transfers between devices, along_z(): lax.all_to_all(message, 'gz', split_axis=0, concat_axis=0, tiled=True)  19.6 us
    all_to_all x1, starting transfers between devices, along_xy(): lax.all_to_all(message, ('gx', 'gy'), split_axis=0, concat_axis=0, tiled=...  12.2 us
    pallas_call x7, Pallas kernels, run(): pl.pallas_call(kernel, out_shape=[jax.ShapeDtypeStruct(s, F32) for s in o...  8.96 us
    ppermute x2, starting transfers between devices, halo(): lax.ppermute(xhi, 'gx', up(nx))  8.04 us
    ppermute x2, waiting for transfers between devices, halo(): lax.ppermute(ylo, 'gy', down(ny))  6.38 us
    ppermute x2, starting transfers between devices, halo(): lax.ppermute(yhi, 'gy', up(ny))  5.75 us
  transfers between devices with their start and end apart: 10, of which 5 were waited for; matrix products, arithmetic and copies ran while one was open for 0% of the time, Pallas kernels for 0%

profile of v5, /device:TPU:1, one launch (start us, length us, event | category | flops | bytes accessed | tf_op | source)
XLA Modules:
  0.0 130.1 jit_solution(10319536514140545011)
XLA Ops:
  0.6 0.0 copy-start.3
  0.6 0.7 copy-done.3
  1.3 0.0 copy-start
  1.3 3.6 %begin.1 = (f32[80,1,128]{2,1,0:T(1,128)}, f32[3,16,128]{2,1,0:T(8,128)S(1)}, f32[16,128]{1,0:T(8,128)S(1)}, f32[8,128]{1,0:T(8,128)S(1)}, f32[32,128]{1,0:T(8,1...) custom-call(f32[8,32,128]{2,1,0:T(8,128)} %r_ref.5, f32[8,32,128]{2,1,0:T(8,128)} %sigma_ref.5, ...), custom_call_target="tpu_custom_call" | custom-call | tf_op jit(solution)/shard_map/begin/pallas_call | solution.py:629
  5.0 0.0 copy-start.2
  5.0 19.6 %all-to-all-start = ((f32[80,1,128]{2,1,0:T(1,128)}), f32[80,1,128]{2,1,0:T(1,128)S(1)}, u32[]{:S(2)}, u32[]{:S(2)}) async-start(f32[80,1,128]{2,1,0:T(1,128)} %get-tuple-element.31), calls=%async_computation | async-start | bytes 81920 | tf_op jit(solution)/shard_map/all_to_all | solution.py:660
  24.5 0.0 copy-start.1
  24.5 3.3 %collective-permute-start = (f32[8,128]{1,0:T(8,128)S(1)}, f32[8,128]{1,0:T(8,128)S(1)}, u32[]{:S(2)}, u32[]{:S(2)}) collective-permute-start(f32[8,128]{1,0:T(8,128)S(1)} %get-tuple-element.34), channel_id=1, source_target_pairs={{0,16},{16,32},{32,48},{48,64},{64,80},{80,96},{96,112},{1,17},{17... | collective-permute-start | bytes 12296 | tf_op jit(solution)/shard_map/ppermute | solution.py:655
  27.9 1.3 collective-permute-start.1
  29.2 0.0 collective-permute-done.h2
  29.2 3.3 %collective-permute-done.1.h3 = f32[8,128]{1,0:T(8,128)S(1)} collective-permute-done((f32[8,128]{1,0:T(8,128)S(1)}, f32[8,128]{1,0:T(8,128)S(1)}, u32[]{:S(2)}, u32[]{:S(2)}) %collective-permute-start.1) | collective-permute-done | bytes 4128 | tf_op jit(solution)/shard_map/ppermute | solution.py:656
  32.5 3.5 %all-to-all-done.zrec_ref = f32[80,1,128]{2,1,0:T(1,128)S(1)} async-done(((f32[80,1,128]{2,1,0:T(1,128)}), f32[80,1,128]{2,1,0:T(1,128)S(1)}, u32[]{:S(2)}, u32[]{:S(2)}) %all-to-all-start) | async-done | bytes 40992 | tf_op jit(solution)/shard_map/all_to_all | solution.py:660
  36.0 1.3 %lines_first.1 = (f32[64,2,128]{2,1,0:T(2,128)}, f32[8,128]{1,0:T(8,128)S(1)}, f32[8,128]{1,0:T(8,128)S(1)}, f32[4,16,128]{2,1,0:T(8,128)S(1)}, f32[8,128]{1,0:T(8,128)S(1)}) custom-call(f32[80,1,128]{2,1,0:T(1,128)S(1)} %all-to-all-done.zrec_ref, f32[3,16,128]{2,1,0:T(8,128)S(1)} %get-tuple-element.32.loc_ref, f32[16,128]{1,0:T(8,128)S(1)} %get-tuple-element.33.alpha_ref, ...), custom_call_target="tpu_custom_call" | custom-call | tf_op jit(solution)/shard_map/lines_first/pallas_call | solution.py:629
  37.4 12.2 %all-to-all-start.1 = ((f32[64,2,128]{2,1,0:T(2,128)}), f32[64,2,128]{2,1,0:T(2,128)S(1)}, u32[]{:S(2)}, u32[]{:S(2)}) async-start(f32[64,2,128]{2,1,0:T(2,128)} %get-tuple-element.36), calls=%async_computation.1 | async-start | bytes 131072 | tf_op jit(solution)/shard_map/all_to_all | solution.py:663
  49.6 3.5 %collective-permute-start.2 = (f32[32,128]{1,0:T(8,128)S(1)}, f32[32,128]{1,0:T(8,128)S(1)}, u32[]{:S(2)}, u32[]{:S(2)}) collective-permute-start(f32[32,128]{1,0:T(8,128)S(1)} %get-tuple-element.39), channel_id=1, source_target_pairs={{0,128},{128,256},{256,384},{384,512},{512,640},{640,768},{768,896... | collective-permute-start | bytes 49160 | tf_op jit(solution)/shard_map/ppermute | solution.py:653
  53.1 1.9 %collective-permute-start.3 = (f32[32,128]{1,0:T(8,128)S(1)}, f32[32,128]{1,0:T(8,128)S(1)}, u32[]{:S(2)}, u32[]{:S(2)}) collective-permute-start(f32[32,128]{1,0:T(8,128)S(1)} %get-tuple-element.40), channel_id=1, source_target_pairs={{128,0},{256,128},{384,256},{512,384},{640,512},{768,640},{896,768... | collective-permute-start | bytes 49160 | tf_op jit(solution)/shard_map/ppermute | solution.py:654
  55.0 0.0 collective-permute-done.2.h0
  55.0 3.4 %collective-permute-done.3.h1 = f32[32,128]{1,0:T(8,128)S(1)} collective-permute-done((f32[32,128]{1,0:T(8,128)S(1)}, f32[32,128]{1,0:T(8,128)S(1)}, u32[]{:S(2)}, u32[]{:S(2)}) %collective-permute-start.3) | collective-permute-done | bytes 16416 | tf_op jit(solution)/shard_map/ppermute | solution.py:654
  58.5 0.5 all-to-all-done.1.xrec_ref
  59.0 0.0 copy-done
  59.0 0.0 copy-done.2
  59.0 0.0 copy-done.1
  59.0 1.2 operator_first.1
  60.2 19.8 %all_to_all.25.zrec_ref = f32[64,1,128]{2,1,0:T(1,128)S(1)} all-to-all(f32[64,1,128]{2,1,0:T(1,128)S(1)} %get-tuple-element.43), channel_id=1, replica_groups=mesh['gx'=8,'gy'=8,'gz'=16] {'gz'}, dimensions={0} | all-to-all | bytes 65536 | tf_op jit(solution)/shard_map/all_to_all | solution.py:660
  79.9 0.6 lines_second.1
  80.6 4.5 %collective-permute-start.4 = (f32[32,128]{1,0:T(8,128)S(1)}, f32[32,128]{1,0:T(8,128)S(1)}, u32[]{:S(2)}, u32[]{:S(2)}) collective-permute-start(f32[32,128]{1,0:T(8,128)S(1)} %get-tuple-element.51), channel_id=1, source_target_pairs={{0,128},{128,256},{256,384},{384,512},{512,640},{640,768},{768,896... | collective-permute-start | bytes 49160 | tf_op jit(solution)/shard_map/ppermute | solution.py:653
  85.1 1.9 %collective-permute-start.5 = (f32[32,128]{1,0:T(8,128)S(1)}, f32[32,128]{1,0:T(8,128)S(1)}, u32[]{:S(2)}, u32[]{:S(2)}) collective-permute-start(f32[32,128]{1,0:T(8,128)S(1)} %get-tuple-element.52), channel_id=1, source_target_pairs={{128,0},{256,128},{384,256},{512,384},{640,512},{768,640},{896,768... | collective-permute-start | bytes 49160 | tf_op jit(solution)/shard_map/ppermute | solution.py:654
  87.0 2.4 %collective-permute-start.6 = (f32[8,128]{1,0:T(8,128)S(1)}, f32[8,128]{1,0:T(8,128)S(1)}, u32[]{:S(2)}, u32[]{:S(2)}) collective-permute-start(f32[8,128]{1,0:T(8,128)S(1)} %get-tuple-element.53), channel_id=1, source_target_pairs={{0,16},{16,32},{32,48},{48,64},{64,80},{80,96},{96,112},{1,17},{17... | collective-permute-start | bytes 12296 | tf_op jit(solution)/shard_map/ppermute | solution.py:655
  89.5 1.3 collective-permute-start.7
  90.8 0.0 collective-permute-done.6.h2
  90.8 3.0 %collective-permute-done.7.h3 = f32[8,128]{1,0:T(8,128)S(1)} collective-permute-done((f32[8,128]{1,0:T(8,128)S(1)}, f32[8,128]{1,0:T(8,128)S(1)}, u32[]{:S(2)}, u32[]{:S(2)}) %collective-permute-start.7) | collective-permute-done | bytes 4128 | tf_op jit(solution)/shard_map/ppermute | solution.py:656
  93.8 0.0 collective-permute-done.4.h0
  93.8 0.0 collective-permute-done.5.h1
  93.8 1.0 operator_second.1
  94.8 20.3 %all_to_all.26.xrec_ref = f32[64,2,128]{2,1,0:T(2,128)S(1)} all-to-all(f32[64,2,128]{2,1,0:T(2,128)S(1)} %get-tuple-element.55), channel_id=1, replica_groups=mesh['gx'=8,'gy'=8,'gz'=16] {'gx','gy'}, dimensions={0} | all-to-all | bytes 131072 | tf_op jit(solution)/shard_map/all_to_all | solution.py:663
  115.1 0.3 plane.1
  115.4 13.8 %all_to_all.27.all_ref = f32[16,1,128]{2,1,0:T(1,128)S(1)} all-to-all(f32[16,1,128]{2,1,0:T(1,128)S(1)} %broadcast_in_dim.9), channel_id=1, replica_groups=mesh['gx'=8,'gy'=8,'gz'=16] {'gz'}, dimensions={0} | all-to-all | bytes 16384 | tf_op jit(solution)/shard_map/all_to_all | solution.py:660
  129.2 0.8 end.1
  (1 shorter events, 0.0 us)
Async XLA Ops:
  0.6 0.7 copy-start.3
  1.3 57.7 %copy-start = (f32[3,8,32,128]{3,2,1,0:T(8,128)S(1)}, f32[3,8,32,128]{3,2,1,0:T(8,128)}, u32[]{:S(2)}) copy-start(f32[3,8,32,128]{3,2,1,0:T(8,128)} %kappa_ref.5) | copy-start | bytes 1179652
  5.0 54.1 %copy-start.2 = (f32[8,32,128]{2,1,0:T(8,128)S(1)}, f32[8,32,128]{2,1,0:T(8,128)}, u32[]{:S(2)}) copy-start(f32[8,32,128]{2,1,0:T(8,128)} %sigma_ref.5) | copy-start | bytes 393220
  5.0 31.1 %all-to-all-start = ((f32[80,1,128]{2,1,0:T(1,128)}), f32[80,1,128]{2,1,0:T(1,128)S(1)}, u32[]{:S(2)}, u32[]{:S(2)}) async-start(f32[80,1,128]{2,1,0:T(1,128)} %get-tuple-element.31), calls=%async_computation | async-start | bytes 81920 | tf_op jit(solution)/shard_map/all_to_all | solution.py:660
  24.5 34.5 %copy-start.1 = (f32[8,32,128]{2,1,0:T(8,128)S(1)}, f32[8,32,128]{2,1,0:T(8,128)}, u32[]{:S(2)}) copy-start(f32[8,32,128]{2,1,0:T(8,128)} %r_ref.5) | copy-start | bytes 393220
  24.5 4.6 %collective-permute-start = (f32[8,128]{1,0:T(8,128)S(1)}, f32[8,128]{1,0:T(8,128)S(1)}, u32[]{:S(2)}, u32[]{:S(2)}) collective-permute-start(f32[8,128]{1,0:T(8,128)S(1)} %get-tuple-element.34), channel_id=1, source_target_pairs={{0,16},{16,32},{32,48},{48,64},{64,80},{80,96},{96,112},{1,17},{17... | collective-permute-start | bytes 12296 | tf_op jit(solution)/shard_map/ppermute | solution.py:655
  27.9 4.6 %collective-permute-start.1 = (f32[8,128]{1,0:T(8,128)S(1)}, f32[8,128]{1,0:T(8,128)S(1)}, u32[]{:S(2)}, u32[]{:S(2)}) collective-permute-start(f32[8,128]{1,0:T(8,128)S(1)} %get-tuple-element.35), channel_id=1, source_target_pairs={{16,0},{32,16},{48,32},{64,48},{80,64},{96,80},{112,96},{17,1},{33... | collective-permute-start | bytes 12296 | tf_op jit(solution)/shard_map/ppermute | solution.py:656
  37.4 21.6 %all-to-all-start.1 = ((f32[64,2,128]{2,1,0:T(2,128)}), f32[64,2,128]{2,1,0:T(2,128)S(1)}, u32[]{:S(2)}, u32[]{:S(2)}) async-start(f32[64,2,128]{2,1,0:T(2,128)} %get-tuple-element.36), calls=%async_computation.1 | async-start | bytes 131072 | tf_op jit(solution)/shard_map/all_to_all | solution.py:663
  49.6 5.5 %collective-permute-start.2 = (f32[32,128]{1,0:T(8,128)S(1)}, f32[32,128]{1,0:T(8,128)S(1)}, u32[]{:S(2)}, u32[]{:S(2)}) collective-permute-start(f32[32,128]{1,0:T(8,128)S(1)} %get-tuple-element.39), channel_id=1, source_target_pairs={{0,128},{128,256},{256,384},{384,512},{512,640},{640,768},{768,896... | collective-permute-start | bytes 49160 | tf_op jit(solution)/shard_map/ppermute | solution.py:653
  53.1 5.4 %collective-permute-start.3 = (f32[32,128]{1,0:T(8,128)S(1)}, f32[32,128]{1,0:T(8,128)S(1)}, u32[]{:S(2)}, u32[]{:S(2)}) collective-permute-start(f32[32,128]{1,0:T(8,128)S(1)} %get-tuple-element.40), channel_id=1, source_target_pairs={{128,0},{256,128},{384,256},{512,384},{640,512},{768,640},{896,768... | collective-permute-start | bytes 49160 | tf_op jit(solution)/shard_map/ppermute | solution.py:654
  80.6 13.2 %collective-permute-start.4 = (f32[32,128]{1,0:T(8,128)S(1)}, f32[32,128]{1,0:T(8,128)S(1)}, u32[]{:S(2)}, u32[]{:S(2)}) collective-permute-start(f32[32,128]{1,0:T(8,128)S(1)} %get-tuple-element.51), channel_id=1, source_target_pairs={{0,128},{128,256},{256,384},{384,512},{512,640},{640,768},{768,896... | collective-permute-start | bytes 49160 | tf_op jit(solution)/shard_map/ppermute | solution.py:653
  85.1 8.7 %collective-permute-start.5 = (f32[32,128]{1,0:T(8,128)S(1)}, f32[32,128]{1,0:T(8,128)S(1)}, u32[]{:S(2)}, u32[]{:S(2)}) collective-permute-start(f32[32,128]{1,0:T(8,128)S(1)} %get-tuple-element.52), channel_id=1, source_target_pairs={{128,0},{256,128},{384,256},{512,384},{640,512},{768,640},{896,768... | collective-permute-start | bytes 49160 | tf_op jit(solution)/shard_map/ppermute | solution.py:654
  87.0 3.7 %collective-permute-start.6 = (f32[8,128]{1,0:T(8,128)S(1)}, f32[8,128]{1,0:T(8,128)S(1)}, u32[]{:S(2)}, u32[]{:S(2)}) collective-permute-start(f32[8,128]{1,0:T(8,128)S(1)} %get-tuple-element.53), channel_id=1, source_target_pairs={{0,16},{16,32},{32,48},{48,64},{64,80},{80,96},{96,112},{1,17},{17... | collective-permute-start | bytes 12296 | tf_op jit(solution)/shard_map/ppermute | solution.py:655
  89.5 4.4 %collective-permute-start.7 = (f32[8,128]{1,0:T(8,128)S(1)}, f32[8,128]{1,0:T(8,128)S(1)}, u32[]{:S(2)}, u32[]{:S(2)}) collective-permute-start(f32[8,128]{1,0:T(8,128)S(1)} %get-tuple-element.54), channel_id=1, source_target_pairs={{16,0},{32,16},{48,32},{64,48},{80,64},{96,80},{112,96},{17,1},{33... | collective-permute-start | bytes 12296 | tf_op jit(solution)/shard_map/ppermute | solution.py:656

commit v6 on v4

--- a/solution.py
+++ b/solution.py
@@ -87,11 +87,18 @@
 
 
 def write_planes(field, planes):
-    xlo, xhi, ylo, yhi = planes
+    xlo, xhi, y_one, y_two = planes
     xlo[...] = field[0]
     xhi[...] = field[CX - 1]
-    ylo[...] = field[:, 0, :]
-    yhi[...] = field[:, CY - 1, :]
+    core = lax.axis_index("gx") % 2
+    low, high = field[:, 0, :], field[:, CY - 1, :]
+    y_one[...] = jnp.where(core == 0, high, low)
+    y_two[...] = jnp.where(core == 0, low, high)
+
+
+def y_halos(y_one, y_two):
+    core = lax.axis_index("gx") % 2
+    return jnp.where(core == 0, y_one, y_two), jnp.where(core == 0, y_two, y_one)
 
 
 def begin_kernel(
@@ -387,7 +394,8 @@
         axis=0,
     )
     lines = dot(rows, to_cells())
-    xlo, xhi, ylo, yhi = [h[...] for h in halos]
+    xlo, xhi = halos[0][...], halos[1][...]
+    ylo, yhi = y_halos(halos[2][...], halos[3][...])
     xlo = jnp.where(mx > 0, xlo + lines[64:96] + c_xlo, 0.0)
     xhi = jnp.where(mx < nx - 1, xhi + lines[96:128] + c_xhi, 0.0)
     ylo = jnp.where(my > 0, ylo + lines[128:136] + c_ylo, 0.0)
@@ -464,8 +472,9 @@
     mx, my, mz = lax.axis_index("gx"), lax.axis_index("gy"), lax.axis_index("gz")
     xlo = jnp.where(mx > 0, h0[...], 0.0)
     xhi = jnp.where(mx < nx - 1, h1[...], 0.0)
-    ylo = jnp.where(my > 0, h2[...], 0.0)
-    yhi = jnp.where(my < ny - 1, h3[...], 0.0)
+    ylo, yhi = y_halos(h2[...], h3[...])
+    ylo = jnp.where(my > 0, ylo, 0.0)
+    yhi = jnp.where(my < ny - 1, yhi, 0.0)
     face = zhalo_ref[...]
     high, low = jnp.where(mz > 0, face, 0.0), jnp.where(mz < nz - 1, face, 0.0)
     ends = ends_of(jnp.where(iota((8, 128), 1) >= HIGH_AT, high, low))
@@ -642,15 +651,19 @@
     planes = [plane, plane, tile, tile]
     to_xy = (nx * ny, 2, 128)
 
+    fold = []
+    for x in range(0, nx, 2):
+        ring = [x * ny + y for y in range(ny)] + [(x + 1) * ny + y for y in reversed(range(ny))]
+        fold += list(zip(ring, ring[1:] + ring[:1]))
+    unfold = [(b, a) for a, b in fold]
+
     def halo(parts):
-        xlo, xhi, ylo, yhi = parts
-        up = lambda n: [(i, (i + 1) % n) for i in range(n)]
-        down = lambda n: [((i + 1) % n, i) for i in range(n)]
+        xlo, xhi, y_one, y_two = parts
         return (
-            lax.ppermute(xhi, "gx", up(nx)),
-            lax.ppermute(xlo, "gx", down(nx)),
-            lax.ppermute(yhi, "gy", up(ny)),
-            lax.ppermute(ylo, "gy", down(ny)),
+            lax.ppermute(xhi, "gx", [(i, (i + 1) % nx) for i in range(nx)]),
+            lax.ppermute(xlo, "gx", [((i + 1) % nx, i) for i in range(nx)]),
+            lax.ppermute(y_one, ("gx", "gy"), fold),
+            lax.ppermute(y_two, ("gx", "gy"), unfold),
         )
 
     def along_z(message):

time: 125 us -> 115 us (0.920)
  starting transfers between devices: 49.6 us -> 40.2 us
  waiting for transfers between devices: 12.9 us -> 19.2 us
  blocking collectives: 51.9 us -> 45.6 us
    ppermute x8, starting transfers between devices: 17.9 us -> 8.46 us  [the longest x2 4.3 us: halo(): lax.ppermute(xhi, 'gx', [(i, (i + 1) % nx) for i in range(nx)])]
    all_to_all x1, waiting for transfers between devices: 3.51 us -> 8.3 us  [along_z(): lax.all_to_all(message, 'gz', split_axis=0, concat_axis=0, tiled=True)]
    all_to_all x2, blocking collectives: 33.6 us -> 29.6 us  [along_z(): lax.all_to_all(message, 'gz', split_axis=0, concat_axis=0, tiled=True)]
    all_to_all x1, blocking collectives: 18.4 us -> 16 us  [along_xy(): lax.all_to_all(message, ('gx', 'gy'), split_axis=0, concat_axis=0, tiled=...]
    ppermute x8, waiting for transfers between devices: 5.04 us -> 6.62 us  [the longest x2 2.62 us: halo(): lax.ppermute(xlo, 'gx', [((i + 1) % nx, i) for i in range(nx)])]
  transfers between devices with their start and end apart: 10 -> 10, of which waited for: 6 -> 8; matrix products, arithmetic and copies ran while one was open for 0% -> 0% of each run, Pallas kernels for 0% -> 0%
where the time goes in v6:
time: 115 us
  blocking collectives  45.6 us (40%)
  starting transfers between devices  40.2 us (35%)
  waiting for transfers between devices  19.2 us (17%)
  Pallas kernels  8.21 us (7%)
    all_to_all x2, blocking collectives, along_z(): lax.all_to_all(message, 'gz', split_axis=0, concat_axis=0, tiled=True)  29.6 us
    all_to_all x1, starting transfers between devices, along_z(): lax.all_to_all(message, 'gz', split_axis=0, concat_axis=0, tiled=True)  19.6 us
    all_to_all x1, blocking collectives, along_xy(): lax.all_to_all(message, ('gx', 'gy'), split_axis=0, concat_axis=0, tiled=...  16 us
    all_to_all x1, starting transfers between devices, along_xy(): lax.all_to_all(message, ('gx', 'gy'), split_axis=0, concat_axis=0, tiled=...  12.2 us
    all_to_all x1, waiting for transfers between devices, along_z(): lax.all_to_all(message, 'gz', split_axis=0, concat_axis=0, tiled=True)  8.3 us
    pallas_call x7, Pallas kernels, run(): pl.pallas_call(kernel, out_shape=[jax.ShapeDtypeStruct(s, F32) for s in o...  8.21 us
    all_to_all x1, waiting for transfers between devices, along_xy(): lax.all_to_all(message, ('gx', 'gy'), split_axis=0, concat_axis=0, tiled=...  4.31 us
    ppermute x2, starting transfers between devices, halo(): lax.ppermute(xhi, 'gx', [(i, (i + 1) % nx) for i in range(nx)])  4.3 us
  transfers between devices with their start and end apart: 10, of which 8 were waited for; matrix products, arithmetic and copies ran while one was open for 0% of the time, Pallas kernels for 0%

profile of v6, /device:TPU:1, one launch (start us, length us, event | category | flops | bytes accessed | tf_op | source)
XLA Modules:
  0.0 114.7 jit_solution(10131927249549339044)
XLA Ops:
  0.6 0.0 copy-start.3
  0.6 0.7 copy-done.3
  1.3 0.0 copy-start
  1.3 2.9 %begin.1 = (f32[80,1,128]{2,1,0:T(1,128)}, f32[3,16,128]{2,1,0:T(8,128)S(1)}, f32[16,128]{1,0:T(8,128)S(1)}, f32[8,128]{1,0:T(8,128)S(1)}, f32[32,128]{1,0:T(8,1...) custom-call(f32[8,32,128]{2,1,0:T(8,128)} %r_ref.5, f32[8,32,128]{2,1,0:T(8,128)} %sigma_ref.5, ...), custom_call_target="tpu_custom_call" | custom-call | tf_op jit(solution)/shard_map/begin/pallas_call | solution.py:635
  4.2 0.0 copy-start.2
  4.2 19.6 %all-to-all-start = ((f32[80,1,128]{2,1,0:T(1,128)}), f32[80,1,128]{2,1,0:T(1,128)S(1)}, u32[]{:S(2)}, u32[]{:S(2)}) async-start(f32[80,1,128]{2,1,0:T(1,128)} %get-tuple-element.31), calls=%async_computation | async-start | bytes 81920 | tf_op jit(solution)/shard_map/all_to_all | solution.py:670
  23.8 0.0 copy-start.1
  23.8 1.0 collective-permute-start
  24.8 0.5 collective-permute-start.1
  25.3 1.0 collective-permute-done.h2
  26.3 0.7 collective-permute-done.1.h3
  27.0 8.3 %all-to-all-done.zrec_ref = f32[80,1,128]{2,1,0:T(1,128)S(1)} async-done(((f32[80,1,128]{2,1,0:T(1,128)}), f32[80,1,128]{2,1,0:T(1,128)S(1)}, u32[]{:S(2)}, u32[]{:S(2)}) %all-to-all-start) | async-done | bytes 40992 | tf_op jit(solution)/shard_map/all_to_all | solution.py:670
  35.3 1.3 %lines_first.1 = (f32[64,2,128]{2,1,0:T(2,128)}, f32[8,128]{1,0:T(8,128)S(1)}, f32[8,128]{1,0:T(8,128)S(1)}, f32[4,16,128]{2,1,0:T(8,128)S(1)}, f32[8,128]{1,0:T(8,128)S(1)}) custom-call(f32[80,1,128]{2,1,0:T(1,128)S(1)} %all-to-all-done.zrec_ref, f32[3,16,128]{2,1,0:T(8,128)S(1)} %get-tuple-element.32.loc_ref, f32[16,128]{1,0:T(8,128)S(1)} %get-tuple-element.33.alpha_ref, ...), custom_call_target="tpu_custom_call" | custom-call | tf_op jit(solution)/shard_map/lines_first/pallas_call | solution.py:635
  36.6 12.2 %all-to-all-start.1 = ((f32[64,2,128]{2,1,0:T(2,128)}), f32[64,2,128]{2,1,0:T(2,128)S(1)}, u32[]{:S(2)}, u32[]{:S(2)}) async-start(f32[64,2,128]{2,1,0:T(2,128)} %get-tuple-element.36), calls=%async_computation.1 | async-start | bytes 131072 | tf_op jit(solution)/shard_map/all_to_all | solution.py:673
  48.8 1.6 %collective-permute-start.2 = (f32[32,128]{1,0:T(8,128)S(1)}, f32[32,128]{1,0:T(8,128)S(1)}, u32[]{:S(2)}, u32[]{:S(2)}) collective-permute-start(f32[32,128]{1,0:T(8,128)S(1)} %get-tuple-element.39), channel_id=1, source_target_pairs={{0,128},{128,256},{256,384},{384,512},{512,640},{640,768},{768,896... | collective-permute-start | bytes 49160 | tf_op jit(solution)/shard_map/ppermute | solution.py:663
  50.5 0.0 collective-permute-start.3
  50.5 0.9 collective-permute-done.2.h0
  51.3 2.6 %collective-permute-done.3.h1 = f32[32,128]{1,0:T(8,128)S(1)} collective-permute-done((f32[32,128]{1,0:T(8,128)S(1)}, f32[32,128]{1,0:T(8,128)S(1)}, u32[]{:S(2)}, u32[]{:S(2)}) %collective-permute-start.3) | collective-permute-done | bytes 16416 | tf_op jit(solution)/shard_map/ppermute | solution.py:664
  54.0 4.3 %all-to-all-done.1.xrec_ref = f32[64,2,128]{2,1,0:T(2,128)S(1)} async-done(((f32[64,2,128]{2,1,0:T(2,128)}), f32[64,2,128]{2,1,0:T(2,128)S(1)}, u32[]{:S(2)}, u32[]{:S(2)}) %all-to-all-start.1) | async-done | bytes 65568 | tf_op jit(solution)/shard_map/all_to_all | solution.py:673
  58.3 0.0 copy-done
  58.3 0.0 copy-done.2
  58.3 0.0 copy-done.1
  58.3 1.2 %operator_first.1 = (f32[8,32,128]{2,1,0:T(8,128)S(1)}, f32[8,32,128]{2,1,0:T(8,128)S(1)}, f32[8,32,128]{2,1,0:T(8,128)S(1)}, f32[64,1,128]{2,1,0:T(1,128)S(1)}, f32[16,128]{1,0:T(8,128)S(1)}) custom-call(f32[8,32,128]{2,1,0:T(8,128)S(1)} %copy-done.1, f32[8,32,128]{2,1,0:T(8,128)S(1)} %copy-done.2, f32[3,8,32,128]{3,2,1,0:T(8,128)S(1)} %copy-done, ...), custom_call_target="tpu_custom_call" | custom-call | tf_op jit(solution)/shard_map/operator_first/pallas_call | solution.py:635
  59.5 15.8 %all_to_all.25.zrec_ref = f32[64,1,128]{2,1,0:T(1,128)S(1)} all-to-all(f32[64,1,128]{2,1,0:T(1,128)S(1)} %get-tuple-element.43), channel_id=1, replica_groups=mesh['gx'=8,'gy'=8,'gz'=16] {'gz'}, dimensions={0} | all-to-all | bytes 65536 | tf_op jit(solution)/shard_map/all_to_all | solution.py:670
  75.3 0.7 lines_second.1
  75.9 2.7 %collective-permute-start.4 = (f32[32,128]{1,0:T(8,128)S(1)}, f32[32,128]{1,0:T(8,128)S(1)}, u32[]{:S(2)}, u32[]{:S(2)}) collective-permute-start(f32[32,128]{1,0:T(8,128)S(1)} %get-tuple-element.51), channel_id=1, source_target_pairs={{0,128},{128,256},{256,384},{384,512},{512,640},{640,768},{768,896... | collective-permute-start | bytes 49160 | tf_op jit(solution)/shard_map/ppermute | solution.py:663
  78.6 0.0 collective-permute-start.5
  78.6 2.7 %collective-permute-start.6 = (f32[8,128]{1,0:T(8,128)S(1)}, f32[8,128]{1,0:T(8,128)S(1)}, u32[]{:S(2)}, u32[]{:S(2)}) collective-permute-start(f32[8,128]{1,0:T(8,128)S(1)} %get-tuple-element.53), channel_id=1, source_target_pairs={{0,16},{16,32},{32,48},{48,64},{64,80},{80,96},{96,112},{112,240},... | collective-permute-start | bytes 12296 | tf_op jit(solution)/shard_map/ppermute | solution.py:665
  81.3 0.0 collective-permute-start.7
  81.3 0.8 collective-permute-done.6.h2
  82.1 0.6 collective-permute-done.7.h3
  82.7 0.0 collective-permute-done.4.h0
  82.7 0.0 collective-permute-done.5.h1
  82.7 1.0 operator_second.1
  83.7 16.0 %all_to_all.26.xrec_ref = f32[64,2,128]{2,1,0:T(2,128)S(1)} all-to-all(f32[64,2,128]{2,1,0:T(2,128)S(1)} %get-tuple-element.55), channel_id=1, replica_groups=mesh['gx'=8,'gy'=8,'gz'=16] {'gx','gy'}, dimensions={0} | all-to-all | bytes 131072 | tf_op jit(solution)/shard_map/all_to_all | solution.py:673
  99.6 0.3 plane.1
  100.0 13.8 %all_to_all.27.all_ref = f32[16,1,128]{2,1,0:T(1,128)S(1)} all-to-all(f32[16,1,128]{2,1,0:T(1,128)S(1)} %broadcast_in_dim.9), channel_id=1, replica_groups=mesh['gx'=8,'gy'=8,'gz'=16] {'gz'}, dimensions={0} | all-to-all | bytes 16384 | tf_op jit(solution)/shard_map/all_to_all | solution.py:670
  113.8 0.8 end.1
  (1 shorter events, 0.0 us)
Async XLA Ops:
  0.6 0.7 copy-start.3
  1.3 56.9 %copy-start = (f32[3,8,32,128]{3,2,1,0:T(8,128)S(1)}, f32[3,8,32,128]{3,2,1,0:T(8,128)}, u32[]{:S(2)}) copy-start(f32[3,8,32,128]{3,2,1,0:T(8,128)} %kappa_ref.5) | copy-start | bytes 1179652
  4.2 54.1 %copy-start.2 = (f32[8,32,128]{2,1,0:T(8,128)S(1)}, f32[8,32,128]{2,1,0:T(8,128)}, u32[]{:S(2)}) copy-start(f32[8,32,128]{2,1,0:T(8,128)} %sigma_ref.5) | copy-start | bytes 393220
  4.2 31.1 %all-to-all-start = ((f32[80,1,128]{2,1,0:T(1,128)}), f32[80,1,128]{2,1,0:T(1,128)S(1)}, u32[]{:S(2)}, u32[]{:S(2)}) async-start(f32[80,1,128]{2,1,0:T(1,128)} %get-tuple-element.31), calls=%async_computation | async-start | bytes 81920 | tf_op jit(solution)/shard_map/all_to_all | solution.py:670
  23.8 34.5 %copy-start.1 = (f32[8,32,128]{2,1,0:T(8,128)S(1)}, f32[8,32,128]{2,1,0:T(8,128)}, u32[]{:S(2)}) copy-start(f32[8,32,128]{2,1,0:T(8,128)} %r_ref.5) | copy-start | bytes 393220
  23.8 2.5 %collective-permute-start = (f32[8,128]{1,0:T(8,128)S(1)}, f32[8,128]{1,0:T(8,128)S(1)}, u32[]{:S(2)}, u32[]{:S(2)}) collective-permute-start(f32[8,128]{1,0:T(8,128)S(1)} %get-tuple-element.34), channel_id=1, source_target_pairs={{0,16},{16,32},{32,48},{48,64},{64,80},{80,96},{96,112},{112,240},... | collective-permute-start | bytes 12296 | tf_op jit(solution)/shard_map/ppermute | solution.py:665
  24.8 2.2 %collective-permute-start.1 = (f32[8,128]{1,0:T(8,128)S(1)}, f32[8,128]{1,0:T(8,128)S(1)}, u32[]{:S(2)}, u32[]{:S(2)}) collective-permute-start(f32[8,128]{1,0:T(8,128)S(1)} %get-tuple-element.35), channel_id=1, source_target_pairs={{16,0},{32,16},{48,32},{64,48},{80,64},{96,80},{112,96},{240,112},... | collective-permute-start | bytes 12296 | tf_op jit(solution)/shard_map/ppermute | solution.py:666
  36.6 21.6 %all-to-all-start.1 = ((f32[64,2,128]{2,1,0:T(2,128)}), f32[64,2,128]{2,1,0:T(2,128)S(1)}, u32[]{:S(2)}, u32[]{:S(2)}) async-start(f32[64,2,128]{2,1,0:T(2,128)} %get-tuple-element.36), calls=%async_computation.1 | async-start | bytes 131072 | tf_op jit(solution)/shard_map/all_to_all | solution.py:673
  48.8 2.5 %collective-permute-start.2 = (f32[32,128]{1,0:T(8,128)S(1)}, f32[32,128]{1,0:T(8,128)S(1)}, u32[]{:S(2)}, u32[]{:S(2)}) collective-permute-start(f32[32,128]{1,0:T(8,128)S(1)} %get-tuple-element.39), channel_id=1, source_target_pairs={{0,128},{128,256},{256,384},{384,512},{512,640},{640,768},{768,896... | collective-permute-start | bytes 49160 | tf_op jit(solution)/shard_map/ppermute | solution.py:663
  50.5 3.5 %collective-permute-start.3 = (f32[32,128]{1,0:T(8,128)S(1)}, f32[32,128]{1,0:T(8,128)S(1)}, u32[]{:S(2)}, u32[]{:S(2)}) collective-permute-start(f32[32,128]{1,0:T(8,128)S(1)} %get-tuple-element.40), channel_id=1, source_target_pairs={{128,0},{256,128},{384,256},{512,384},{640,512},{768,640},{896,768... | collective-permute-start | bytes 49160 | tf_op jit(solution)/shard_map/ppermute | solution.py:664
  75.9 6.7 %collective-permute-start.4 = (f32[32,128]{1,0:T(8,128)S(1)}, f32[32,128]{1,0:T(8,128)S(1)}, u32[]{:S(2)}, u32[]{:S(2)}) collective-permute-start(f32[32,128]{1,0:T(8,128)S(1)} %get-tuple-element.51), channel_id=1, source_target_pairs={{0,128},{128,256},{256,384},{384,512},{512,640},{640,768},{768,896... | collective-permute-start | bytes 49160 | tf_op jit(solution)/shard_map/ppermute | solution.py:663
  78.6 4.1 %collective-permute-start.5 = (f32[32,128]{1,0:T(8,128)S(1)}, f32[32,128]{1,0:T(8,128)S(1)}, u32[]{:S(2)}, u32[]{:S(2)}) collective-permute-start(f32[32,128]{1,0:T(8,128)S(1)} %get-tuple-element.52), channel_id=1, source_target_pairs={{128,0},{256,128},{384,256},{512,384},{640,512},{768,640},{896,768... | collective-permute-start | bytes 49160 | tf_op jit(solution)/shard_map/ppermute | solution.py:664
  78.6 3.5 %collective-permute-start.6 = (f32[8,128]{1,0:T(8,128)S(1)}, f32[8,128]{1,0:T(8,128)S(1)}, u32[]{:S(2)}, u32[]{:S(2)}) collective-permute-start(f32[8,128]{1,0:T(8,128)S(1)} %get-tuple-element.53), channel_id=1, source_target_pairs={{0,16},{16,32},{32,48},{48,64},{64,80},{80,96},{96,112},{112,240},... | collective-permute-start | bytes 12296 | tf_op jit(solution)/shard_map/ppermute | solution.py:665
  81.3 1.4 %collective-permute-start.7 = (f32[8,128]{1,0:T(8,128)S(1)}, f32[8,128]{1,0:T(8,128)S(1)}, u32[]{:S(2)}, u32[]{:S(2)}) collective-permute-start(f32[8,128]{1,0:T(8,128)S(1)} %get-tuple-element.54), channel_id=1, source_target_pairs={{16,0},{32,16},{48,32},{64,48},{80,64},{96,80},{112,96},{240,112},... | collective-permute-start | bytes 12296 | tf_op jit(solution)/shard_map/ppermute | solution.py:666

commit v7 on v4

--- a/solution.py
+++ b/solution.py
@@ -87,11 +87,23 @@
 
 
 def write_planes(field, planes):
-    xlo, xhi, ylo, yhi = planes
-    xlo[...] = field[0]
-    xhi[...] = field[CX - 1]
-    ylo[...] = field[:, 0, :]
-    yhi[...] = field[:, CY - 1, :]
+    x_one, x_two, y_one, y_two = planes
+    even = lax.axis_index("gy") % 2 == 0
+    low, high = field[0], field[CX - 1]
+    x_one[...] = jnp.where(even, high, low)
+    x_two[...] = jnp.where(even, low, high)
+    even = lax.axis_index("gx") % 2 == 0
+    low, high = field[:, 0, :], field[:, CY - 1, :]
+    y_one[...] = jnp.where(even, high, low)
+    y_two[...] = jnp.where(even, low, high)
+
+
+def low_and_high(halos):
+    x_one, x_two, y_one, y_two = [h[...] for h in halos]
+    even_y, even_x = lax.axis_index("gy") % 2 == 0, lax.axis_index("gx") % 2 == 0
+    xlo, xhi = jnp.where(even_y, x_one, x_two), jnp.where(even_y, x_two, x_one)
+    ylo, yhi = jnp.where(even_x, y_one, y_two), jnp.where(even_x, y_two, y_one)
+    return xlo, xhi, ylo, yhi
 
 
 def begin_kernel(
@@ -387,7 +399,7 @@
         axis=0,
     )
     lines = dot(rows, to_cells())
-    xlo, xhi, ylo, yhi = [h[...] for h in halos]
+    xlo, xhi, ylo, yhi = low_and_high(halos)
     xlo = jnp.where(mx > 0, xlo + lines[64:96] + c_xlo, 0.0)
     xhi = jnp.where(mx < nx - 1, xhi + lines[96:128] + c_xhi, 0.0)
     ylo = jnp.where(my > 0, ylo + lines[128:136] + c_ylo, 0.0)
@@ -462,10 +474,11 @@
 ):
     nx, ny, nz = sizes
     mx, my, mz = lax.axis_index("gx"), lax.axis_index("gy"), lax.axis_index("gz")
-    xlo = jnp.where(mx > 0, h0[...], 0.0)
-    xhi = jnp.where(mx < nx - 1, h1[...], 0.0)
-    ylo = jnp.where(my > 0, h2[...], 0.0)
-    yhi = jnp.where(my < ny - 1, h3[...], 0.0)
+    xlo, xhi, ylo, yhi = low_and_high((h0, h1, h2, h3))
+    xlo = jnp.where(mx > 0, xlo, 0.0)
+    xhi = jnp.where(mx < nx - 1, xhi, 0.0)
+    ylo = jnp.where(my > 0, ylo, 0.0)
+    yhi = jnp.where(my < ny - 1, yhi, 0.0)
     face = zhalo_ref[...]
     high, low = jnp.where(mz > 0, face, 0.0), jnp.where(mz < nz - 1, face, 0.0)
     ends = ends_of(jnp.where(iota((8, 128), 1) >= HIGH_AT, high, low))
@@ -642,16 +655,20 @@
     planes = [plane, plane, tile, tile]
     to_xy = (nx * ny, 2, 128)
 
+    def folded(lanes):
+        pairs = []
+        for up, down in lanes:
+            ring = up + down[::-1]
+            pairs += zip(ring, ring[1:] + ring[:1])
+        return pairs
+
+    along_x = folded([[[x * ny + y + k for x in range(nx)] for k in (0, 1)] for y in range(0, ny, 2)])
+    along_y = folded([[[(x + k) * ny + y for y in range(ny)] for k in (0, 1)] for x in range(0, nx, 2)])
+    back = lambda pairs: [(b, a) for a, b in pairs]
+
     def halo(parts):
-        xlo, xhi, ylo, yhi = parts
-        up = lambda n: [(i, (i + 1) % n) for i in range(n)]
-        down = lambda n: [((i + 1) % n, i) for i in range(n)]
-        return (
-            lax.ppermute(xhi, "gx", up(nx)),
-            lax.ppermute(xlo, "gx", down(nx)),
-            lax.ppermute(yhi, "gy", up(ny)),
-            lax.ppermute(ylo, "gy", down(ny)),
-        )
+        rings = (along_x, back(along_x), along_y, back(along_y))
+        return tuple(lax.ppermute(p, ("gx", "gy"), ring) for p, ring in zip(parts, rings))
 
     def along_z(message):
         return lax.all_to_all(message, "gz", split_axis=0, concat_axis=0, tiled=True)

time: 125 us -> 122 us (0.976)
  starting transfers between devices: 49.6 us -> 46.9 us
  waiting for transfers between devices: 12.9 us -> 15.3 us
  blocking collectives: 51.9 us -> 49.7 us
    all_to_all x1, waiting for transfers between devices: 3.51 us -> 8.3 us  [along_z(): lax.all_to_all(message, 'gz', split_axis=0, concat_axis=0, tiled=True)]
    all_to_all x2, blocking collectives: 33.6 us -> 29.6 us  [along_z(): lax.all_to_all(message, 'gz', split_axis=0, concat_axis=0, tiled=True)]
    all_to_all x1, waiting for transfers between devices: 4.31 us -> 0.54 us  [along_xy(): lax.all_to_all(message, ('gx', 'gy'), split_axis=0, concat_axis=0, tiled=...]
    ppermute x8, starting transfers between devices: 17.9 us -> 15.2 us  [halo(): lax.ppermute(p, ('gx', 'gy'), ring)]
    all_to_all x1, blocking collectives: 18.4 us -> 20.1 us  [along_xy(): lax.all_to_all(message, ('gx', 'gy'), split_axis=0, concat_axis=0, tiled=...]
    ppermute x8, waiting for transfers between devices: 5.04 us -> 6.46 us  [halo(): lax.ppermute(p, ('gx', 'gy'), ring)]
  transfers between devices with their start and end apart: 10 -> 10, of which waited for: 6 -> 8; matrix products, arithmetic and copies ran while one was open for 0% -> 0% of each run, Pallas kernels for 0% -> 0%
where the time goes in v7:
time: 122 us
  blocking collectives  49.7 us (41%)
  starting transfers between devices  46.9 us (38%)
  waiting for transfers between devices  15.3 us (13%)
  Pallas kernels  8.21 us (7%)
    all_to_all x2, blocking collectives, along_z(): lax.all_to_all(message, 'gz', split_axis=0, concat_axis=0, tiled=True)  29.6 us
    all_to_all x1, blocking collectives, along_xy(): lax.all_to_all(message, ('gx', 'gy'), split_axis=0, concat_axis=0, tiled=...  20.1 us
    all_to_all x1, starting transfers between devices, along_z(): lax.all_to_all(message, 'gz', split_axis=0, concat_axis=0, tiled=True)  19.6 us
    ppermute x8, starting transfers between devices, halo(): lax.ppermute(p, ('gx', 'gy'), ring)  15.2 us
    all_to_all x1, starting transfers between devices, along_xy(): lax.all_to_all(message, ('gx', 'gy'), split_axis=0, concat_axis=0, tiled=...  12.2 us
    all_to_all x1, waiting for transfers between devices, along_z(): lax.all_to_all(message, 'gz', split_axis=0, concat_axis=0, tiled=True)  8.3 us
    pallas_call x7, Pallas kernels, run(): pl.pallas_call(kernel, out_shape=[jax.ShapeDtypeStruct(s, F32) for s in o...  8.21 us
    ppermute x8, waiting for transfers between devices, halo(): lax.ppermute(p, ('gx', 'gy'), ring)  6.46 us
  transfers between devices with their start and end apart: 10, of which 8 were waited for; matrix products, arithmetic and copies ran while one was open for 0% of the time, Pallas kernels for 0%

profile of v7, /device:TPU:1, one launch (start us, length us, event | category | flops | bytes accessed | tf_op | source)
XLA Modules:
  0.0 121.6 jit_solution(316671115176862395)
XLA Ops:
  0.6 0.0 copy-start.3
  0.6 0.7 copy-done.3
  1.3 0.0 copy-start
  1.3 2.9 %begin.1 = (f32[80,1,128]{2,1,0:T(1,128)}, f32[3,16,128]{2,1,0:T(8,128)S(1)}, f32[16,128]{1,0:T(8,128)S(1)}, f32[8,128]{1,0:T(8,128)S(1)}, f32[32,128]{1,0:T(8,1...) custom-call(f32[8,32,128]{2,1,0:T(8,128)} %r_ref.5, f32[8,32,128]{2,1,0:T(8,128)} %sigma_ref.5, ...), custom_call_target="tpu_custom_call" | custom-call | tf_op jit(solution)/shard_map/begin/pallas_call | solution.py:639
  4.2 0.0 copy-start.2
  4.2 19.6 %all-to-all-start = ((f32[80,1,128]{2,1,0:T(1,128)}), f32[80,1,128]{2,1,0:T(1,128)S(1)}, u32[]{:S(2)}, u32[]{:S(2)}) async-start(f32[80,1,128]{2,1,0:T(1,128)} %get-tuple-element.31), calls=%async_computation | async-start | bytes 81920 | tf_op jit(solution)/shard_map/all_to_all | solution.py:674
  23.8 0.0 copy-start.1
  23.8 1.0 collective-permute-start
  24.8 0.5 collective-permute-start.1
  25.3 1.0 collective-permute-done.h2
  26.3 0.7 collective-permute-done.1.h3
  27.0 8.3 %all-to-all-done.zrec_ref = f32[80,1,128]{2,1,0:T(1,128)S(1)} async-done(((f32[80,1,128]{2,1,0:T(1,128)}), f32[80,1,128]{2,1,0:T(1,128)S(1)}, u32[]{:S(2)}, u32[]{:S(2)}) %all-to-all-start) | async-done | bytes 40992 | tf_op jit(solution)/shard_map/all_to_all | solution.py:674
  35.3 1.3 %lines_first.1 = (f32[64,2,128]{2,1,0:T(2,128)}, f32[8,128]{1,0:T(8,128)S(1)}, f32[8,128]{1,0:T(8,128)S(1)}, f32[4,16,128]{2,1,0:T(8,128)S(1)}, f32[8,128]{1,0:T(8,128)S(1)}) custom-call(f32[80,1,128]{2,1,0:T(1,128)S(1)} %all-to-all-done.zrec_ref, f32[3,16,128]{2,1,0:T(8,128)S(1)} %get-tuple-element.32.loc_ref, f32[16,128]{1,0:T(8,128)S(1)} %get-tuple-element.33.alpha_ref, ...), custom_call_target="tpu_custom_call" | custom-call | tf_op jit(solution)/shard_map/lines_first/pallas_call | solution.py:639
  36.6 12.2 %all-to-all-start.1 = ((f32[64,2,128]{2,1,0:T(2,128)}), f32[64,2,128]{2,1,0:T(2,128)S(1)}, u32[]{:S(2)}, u32[]{:S(2)}) async-start(f32[64,2,128]{2,1,0:T(2,128)} %get-tuple-element.36), calls=%async_computation.1 | async-start | bytes 131072 | tf_op jit(solution)/shard_map/all_to_all | solution.py:677
  48.8 3.5 %collective-permute-start.2 = (f32[32,128]{1,0:T(8,128)S(1)}, f32[32,128]{1,0:T(8,128)S(1)}, u32[]{:S(2)}, u32[]{:S(2)}) collective-permute-start(f32[32,128]{1,0:T(8,128)S(1)} %get-tuple-element.39), channel_id=1, source_target_pairs={{0,128},{128,256},{256,384},{384,512},{512,640},{640,768},{768,896... | collective-permute-start | bytes 49160 | tf_op jit(solution)/shard_map/ppermute | solution.py:671
  52.4 1.9 %collective-permute-start.3 = (f32[32,128]{1,0:T(8,128)S(1)}, f32[32,128]{1,0:T(8,128)S(1)}, u32[]{:S(2)}, u32[]{:S(2)}) collective-permute-start(f32[32,128]{1,0:T(8,128)S(1)} %get-tuple-element.40), channel_id=1, source_target_pairs={{128,0},{256,128},{384,256},{512,384},{640,512},{768,640},{896,768... | collective-permute-start | bytes 49160 | tf_op jit(solution)/shard_map/ppermute | solution.py:671
  54.3 0.0 collective-permute-done.2.h0
  54.3 3.4 %collective-permute-done.3.h1 = f32[32,128]{1,0:T(8,128)S(1)} collective-permute-done((f32[32,128]{1,0:T(8,128)S(1)}, f32[32,128]{1,0:T(8,128)S(1)}, u32[]{:S(2)}, u32[]{:S(2)}) %collective-permute-start.3) | collective-permute-done | bytes 16416 | tf_op jit(solution)/shard_map/ppermute | solution.py:671
  57.7 0.5 all-to-all-done.1.xrec_ref
  58.3 0.0 copy-done
  58.3 0.0 copy-done.2
  58.3 0.0 copy-done.1
  58.3 1.2 operator_first.1
  59.5 15.8 %all_to_all.25.zrec_ref = f32[64,1,128]{2,1,0:T(1,128)S(1)} all-to-all(f32[64,1,128]{2,1,0:T(1,128)S(1)} %get-tuple-element.43), channel_id=1, replica_groups=mesh['gx'=8,'gy'=8,'gz'=16] {'gz'}, dimensions={0} | all-to-all | bytes 65536 | tf_op jit(solution)/shard_map/all_to_all | solution.py:674
  75.3 0.7 lines_second.1
  75.9 4.5 %collective-permute-start.4 = (f32[32,128]{1,0:T(8,128)S(1)}, f32[32,128]{1,0:T(8,128)S(1)}, u32[]{:S(2)}, u32[]{:S(2)}) collective-permute-start(f32[32,128]{1,0:T(8,128)S(1)} %get-tuple-element.51), channel_id=1, source_target_pairs={{0,128},{128,256},{256,384},{384,512},{512,640},{640,768},{768,896... | collective-permute-start | bytes 49160 | tf_op jit(solution)/shard_map/ppermute | solution.py:671
  80.4 1.9 %collective-permute-start.5 = (f32[32,128]{1,0:T(8,128)S(1)}, f32[32,128]{1,0:T(8,128)S(1)}, u32[]{:S(2)}, u32[]{:S(2)}) collective-permute-start(f32[32,128]{1,0:T(8,128)S(1)} %get-tuple-element.52), channel_id=1, source_target_pairs={{128,0},{256,128},{384,256},{512,384},{640,512},{768,640},{896,768... | collective-permute-start | bytes 49160 | tf_op jit(solution)/shard_map/ppermute | solution.py:671
  82.4 1.8 %collective-permute-start.6 = (f32[8,128]{1,0:T(8,128)S(1)}, f32[8,128]{1,0:T(8,128)S(1)}, u32[]{:S(2)}, u32[]{:S(2)}) collective-permute-start(f32[8,128]{1,0:T(8,128)S(1)} %get-tuple-element.53), channel_id=1, source_target_pairs={{0,16},{16,32},{32,48},{48,64},{64,80},{80,96},{96,112},{112,240},... | collective-permute-start | bytes 12296 | tf_op jit(solution)/shard_map/ppermute | solution.py:671
  84.2 0.0 collective-permute-start.7
  84.2 0.8 collective-permute-done.6.h2
  85.0 0.3 collective-permute-done.7.h3
  85.3 0.0 collective-permute-done.4.h0
  85.3 0.2 collective-permute-done.5.h1
  85.5 1.0 operator_second.1
  86.5 20.1 %all_to_all.26.xrec_ref = f32[64,2,128]{2,1,0:T(2,128)S(1)} all-to-all(f32[64,2,128]{2,1,0:T(2,128)S(1)} %get-tuple-element.55), channel_id=1, replica_groups=mesh['gx'=8,'gy'=8,'gz'=16] {'gx','gy'}, dimensions={0} | all-to-all | bytes 131072 | tf_op jit(solution)/shard_map/all_to_all | solution.py:677
  106.6 0.3 plane.1
  107.0 13.8 %all_to_all.27.all_ref = f32[16,1,128]{2,1,0:T(1,128)S(1)} all-to-all(f32[16,1,128]{2,1,0:T(1,128)S(1)} %broadcast_in_dim.9), channel_id=1, replica_groups=mesh['gx'=8,'gy'=8,'gz'=16] {'gz'}, dimensions={0} | all-to-all | bytes 16384 | tf_op jit(solution)/shard_map/all_to_all | solution.py:674
  120.8 0.8 end.1
  (1 shorter events, 0.0 us)
Async XLA Ops:
  0.6 0.7 copy-start.3
  1.3 56.9 %copy-start = (f32[3,8,32,128]{3,2,1,0:T(8,128)S(1)}, f32[3,8,32,128]{3,2,1,0:T(8,128)}, u32[]{:S(2)}) copy-start(f32[3,8,32,128]{3,2,1,0:T(8,128)} %kappa_ref.5) | copy-start | bytes 1179652
  4.2 54.1 %copy-start.2 = (f32[8,32,128]{2,1,0:T(8,128)S(1)}, f32[8,32,128]{2,1,0:T(8,128)}, u32[]{:S(2)}) copy-start(f32[8,32,128]{2,1,0:T(8,128)} %sigma_ref.5) | copy-start | bytes 393220
  4.2 31.1 %all-to-all-start = ((f32[80,1,128]{2,1,0:T(1,128)}), f32[80,1,128]{2,1,0:T(1,128)S(1)}, u32[]{:S(2)}, u32[]{:S(2)}) async-start(f32[80,1,128]{2,1,0:T(1,128)} %get-tuple-element.31), calls=%async_computation | async-start | bytes 81920 | tf_op jit(solution)/shard_map/all_to_all | solution.py:674
  23.8 34.5 %copy-start.1 = (f32[8,32,128]{2,1,0:T(8,128)S(1)}, f32[8,32,128]{2,1,0:T(8,128)}, u32[]{:S(2)}) copy-start(f32[8,32,128]{2,1,0:T(8,128)} %r_ref.5) | copy-start | bytes 393220
  23.8 2.5 %collective-permute-start = (f32[8,128]{1,0:T(8,128)S(1)}, f32[8,128]{1,0:T(8,128)S(1)}, u32[]{:S(2)}, u32[]{:S(2)}) collective-permute-start(f32[8,128]{1,0:T(8,128)S(1)} %get-tuple-element.34), channel_id=1, source_target_pairs={{0,16},{16,32},{32,48},{48,64},{64,80},{80,96},{96,112},{112,240},... | collective-permute-start | bytes 12296 | tf_op jit(solution)/shard_map/ppermute | solution.py:671
  24.8 2.2 %collective-permute-start.1 = (f32[8,128]{1,0:T(8,128)S(1)}, f32[8,128]{1,0:T(8,128)S(1)}, u32[]{:S(2)}, u32[]{:S(2)}) collective-permute-start(f32[8,128]{1,0:T(8,128)S(1)} %get-tuple-element.35), channel_id=1, source_target_pairs={{16,0},{32,16},{48,32},{64,48},{80,64},{96,80},{112,96},{240,112},... | collective-permute-start | bytes 12296 | tf_op jit(solution)/shard_map/ppermute | solution.py:671
  36.6 21.6 %all-to-all-start.1 = ((f32[64,2,128]{2,1,0:T(2,128)}), f32[64,2,128]{2,1,0:T(2,128)S(1)}, u32[]{:S(2)}, u32[]{:S(2)}) async-start(f32[64,2,128]{2,1,0:T(2,128)} %get-tuple-element.36), calls=%async_computation.1 | async-start | bytes 131072 | tf_op jit(solution)/shard_map/all_to_all | solution.py:677
  48.8 5.5 %collective-permute-start.2 = (f32[32,128]{1,0:T(8,128)S(1)}, f32[32,128]{1,0:T(8,128)S(1)}, u32[]{:S(2)}, u32[]{:S(2)}) collective-permute-start(f32[32,128]{1,0:T(8,128)S(1)} %get-tuple-element.39), channel_id=1, source_target_pairs={{0,128},{128,256},{256,384},{384,512},{512,640},{640,768},{768,896... | collective-permute-start | bytes 49160 | tf_op jit(solution)/shard_map/ppermute | solution.py:671
  52.4 5.4 %collective-permute-start.3 = (f32[32,128]{1,0:T(8,128)S(1)}, f32[32,128]{1,0:T(8,128)S(1)}, u32[]{:S(2)}, u32[]{:S(2)}) collective-permute-start(f32[32,128]{1,0:T(8,128)S(1)} %get-tuple-element.40), channel_id=1, source_target_pairs={{128,0},{256,128},{384,256},{512,384},{640,512},{768,640},{896,768... | collective-permute-start | bytes 49160 | tf_op jit(solution)/shard_map/ppermute | solution.py:671
  75.9 9.4 %collective-permute-start.4 = (f32[32,128]{1,0:T(8,128)S(1)}, f32[32,128]{1,0:T(8,128)S(1)}, u32[]{:S(2)}, u32[]{:S(2)}) collective-permute-start(f32[32,128]{1,0:T(8,128)S(1)} %get-tuple-element.51), channel_id=1, source_target_pairs={{0,128},{128,256},{256,384},{384,512},{512,640},{640,768},{768,896... | collective-permute-start | bytes 49160 | tf_op jit(solution)/shard_map/ppermute | solution.py:671
  80.4 5.1 %collective-permute-start.5 = (f32[32,128]{1,0:T(8,128)S(1)}, f32[32,128]{1,0:T(8,128)S(1)}, u32[]{:S(2)}, u32[]{:S(2)}) collective-permute-start(f32[32,128]{1,0:T(8,128)S(1)} %get-tuple-element.52), channel_id=1, source_target_pairs={{128,0},{256,128},{384,256},{512,384},{640,512},{768,640},{896,768... | collective-permute-start | bytes 49160 | tf_op jit(solution)/shard_map/ppermute | solution.py:671
  82.4 2.6 %collective-permute-start.6 = (f32[8,128]{1,0:T(8,128)S(1)}, f32[8,128]{1,0:T(8,128)S(1)}, u32[]{:S(2)}, u32[]{:S(2)}) collective-permute-start(f32[8,128]{1,0:T(8,128)S(1)} %get-tuple-element.53), channel_id=1, source_target_pairs={{0,16},{16,32},{32,48},{48,64},{64,80},{80,96},{96,112},{112,240},... | collective-permute-start | bytes 12296 | tf_op jit(solution)/shard_map/ppermute | solution.py:671
  84.2 1.2 collective-permute-start.7

commit v8 on v6

--- a/solution.py
+++ b/solution.py
@@ -280,7 +280,7 @@
 
 
 def first_lines_kernel(
-    sizes, zrec_ref, loc_ref, alpha_ref, h2, h3, xmsg_ref, own_ref, zhalo_ref, chain_ref, final_ref, sol_ref
+    sizes, zrec_ref, loc_ref, alpha_ref, h0, h1, h2, h3, xmsg_ref, own_ref, zhalo_ref, chain_ref, final_ref, sol_ref
 ):
     nx, ny, nz = sizes
     mx, my = lax.axis_index("gx"), lax.axis_index("gy")
@@ -681,7 +681,7 @@
     halos = halo(sides)
     xmsg, own, zhalo, chain, final = call(
         bind(first_lines_kernel), [to_xy, tile, tile, (4, nz, 128), tile], [coarse], "lines_first"
-    )(zrec, loc, alpha, *halos[2:])
+    )(zrec, loc, alpha, *halos)
     xrec = along_xy(xmsg)
     z1, w1, jac, zmsg, alpha = call(
         bind(first_kernel), [field, field, field, (nz * 4, 1, 128), coarse], name="operator_first"

time: 115 us -> 116 us (level)
  blocking collectives: 45.6 us -> 68.8 us
  starting transfers between devices: 40.2 us -> 28.7 us
  waiting for transfers between devices: 19.2 us -> 8.99 us
    all_to_all x1 -> x2, blocking collectives: 16 us -> 37.4 us  [along_xy(): lax.all_to_all(message, ('gx', 'gy'), split_axis=0, concat_axis=0, tiled=...]
    all_to_all x1 -> x0, starting transfers between devices: 12.2 us -> none  [along_xy(): lax.all_to_all(message, ('gx', 'gy'), split_axis=0, concat_axis=0, tiled=...]
    all_to_all x1 -> x0, waiting for transfers between devices: 4.31 us -> none  [along_xy(): lax.all_to_all(message, ('gx', 'gy'), split_axis=0, concat_axis=0, tiled=...]
    all_to_all x1, waiting for transfers between devices: 8.3 us -> 5.35 us  [along_z(): lax.all_to_all(message, 'gz', split_axis=0, concat_axis=0, tiled=True)]
    ppermute x2, waiting for transfers between devices: 2.62 us -> 0.01 us  [halo(): lax.ppermute(xlo, 'gx', [((i + 1) % nx, i) for i in range(nx)])]
    all_to_all x2, blocking collectives: 29.6 us -> 31.4 us  [along_z(): lax.all_to_all(message, 'gz', split_axis=0, concat_axis=0, tiled=True)]
  transfers between devices with their start and end apart: 10 -> 9, of which waited for: 8 -> 5; matrix products, arithmetic and copies ran while one was open for 0% -> 0% of each run, Pallas kernels for 0% -> 0%
where the time goes in v8:
time: 116 us; the launch traced here: 115 us
  blocking collectives  68.8 us (59%)
  starting transfers between devices  28.7 us (25%)
  waiting for transfers between devices  8.99 us (8%)
  Pallas kernels  7.58 us (7%)
    all_to_all x2, blocking collectives, along_xy(): lax.all_to_all(message, ('gx', 'gy'), split_axis=0, concat_axis=0, tiled=...  37.4 us
    all_to_all x2, blocking collectives, along_z(): lax.all_to_all(message, 'gz', split_axis=0, concat_axis=0, tiled=True)  31.4 us
    all_to_all x1, starting transfers between devices, along_z(): lax.all_to_all(message, 'gz', split_axis=0, concat_axis=0, tiled=True)  19.4 us
    pallas_call x7, Pallas kernels, run(): pl.pallas_call(kernel, out_shape=[jax.ShapeDtypeStruct(s, F32) for s in o...  7.58 us
    all_to_all x1, waiting for transfers between devices, along_z(): lax.all_to_all(message, 'gz', split_axis=0, concat_axis=0, tiled=True)  5.35 us
    ppermute x2, starting transfers between devices, halo(): lax.ppermute(xhi, 'gx', [(i, (i + 1) % nx) for i in range(nx)])  4.71 us
    ppermute x2, starting transfers between devices, halo(): lax.ppermute(y_one, ('gx', 'gy'), fold)  4.53 us
  transfers between devices with their start and end apart: 9, of which 5 were waited for; matrix products, arithmetic and copies ran while one was open for 0% of the time, Pallas kernels for 0%

profile of v8, /device:TPU:1, one launch (start us, length us, event | category | flops | bytes accessed | tf_op | source)
XLA Modules:
  0.0 115.4 jit_solution(14513007117148618360)
XLA Ops:
  0.6 0.0 copy-start.3
  0.6 0.7 copy-done.3
  1.3 0.0 copy-start
  1.3 2.9 %begin.1 = (f32[80,1,128]{2,1,0:T(1,128)}, f32[3,16,128]{2,1,0:T(8,128)S(1)}, f32[16,128]{1,0:T(8,128)S(1)}, f32[8,128]{1,0:T(8,128)S(1)}, f32[32,128]{1,0:T(8,1...) custom-call(f32[8,32,128]{2,1,0:T(8,128)} %r_ref.5, f32[8,32,128]{2,1,0:T(8,128)} %sigma_ref.5, ...), custom_call_target="tpu_custom_call" | custom-call | tf_op jit(solution)/shard_map/begin/pallas_call | solution.py:635
  4.2 19.4 %all-to-all-start = ((f32[80,1,128]{2,1,0:T(1,128)}), f32[80,1,128]{2,1,0:T(1,128)S(1)}, u32[]{:S(2)}, u32[]{:S(2)}) async-start(f32[80,1,128]{2,1,0:T(1,128)} %get-tuple-element.31), calls=%async_computation | async-start | bytes 81920 | tf_op jit(solution)/shard_map/all_to_all | solution.py:670
  23.6 2.1 %collective-permute-start = (f32[32,128]{1,0:T(8,128)S(1)}, f32[32,128]{1,0:T(8,128)S(1)}, u32[]{:S(2)}, u32[]{:S(2)}) collective-permute-start(f32[32,128]{1,0:T(8,128)S(1)} %get-tuple-element.34), channel_id=1, source_target_pairs={{0,128},{128,256},{256,384},{384,512},{512,640},{640,768},{768,896... | collective-permute-start | bytes 49160 | tf_op jit(solution)/shard_map/ppermute | solution.py:663
  25.7 0.0 copy-start.2
  25.7 0.0 copy-start.1
  25.7 0.0 collective-permute-start.1
  25.7 1.9 %collective-permute-start.2 = (f32[8,128]{1,0:T(8,128)S(1)}, f32[8,128]{1,0:T(8,128)S(1)}, u32[]{:S(2)}, u32[]{:S(2)}) collective-permute-start(f32[8,128]{1,0:T(8,128)S(1)} %get-tuple-element.36), channel_id=1, source_target_pairs={{0,16},{16,32},{32,48},{48,64},{64,80},{80,96},{96,112},{112,240},... | collective-permute-start | bytes 12296 | tf_op jit(solution)/shard_map/ppermute | solution.py:665
  27.6 0.0 collective-permute-start.3
  27.6 0.9 collective-permute-done.2.h2
  28.5 1.3 %collective-permute-done.3.h3 = f32[8,128]{1,0:T(8,128)S(1)} collective-permute-done((f32[8,128]{1,0:T(8,128)S(1)}, f32[8,128]{1,0:T(8,128)S(1)}, u32[]{:S(2)}, u32[]{:S(2)}) %collective-permute-start.3) | collective-permute-done | bytes 4128 | tf_op jit(solution)/shard_map/ppermute | solution.py:666
  29.8 0.0 collective-permute-done.h0
  29.8 0.0 collective-permute-done.1.h1
  29.8 5.3 %all-to-all-done.zrec_ref = f32[80,1,128]{2,1,0:T(1,128)S(1)} async-done(((f32[80,1,128]{2,1,0:T(1,128)}), f32[80,1,128]{2,1,0:T(1,128)S(1)}, u32[]{:S(2)}, u32[]{:S(2)}) %all-to-all-start) | async-done | bytes 40992 | tf_op jit(solution)/shard_map/all_to_all | solution.py:670
  35.2 0.7 lines_first.1
  35.9 21.4 %all_to_all.25.xrec_ref = f32[64,2,128]{2,1,0:T(2,128)S(1)} all-to-all(f32[64,2,128]{2,1,0:T(2,128)S(1)} %get-tuple-element.38), channel_id=1, replica_groups=mesh['gx'=8,'gy'=8,'gz'=16] {'gx','gy'}, dimensions={0} | all-to-all | bytes 131072 | tf_op jit(solution)/shard_map/all_to_all | solution.py:673
  57.3 0.0 copy-done
  57.3 0.0 copy-done.2
  57.3 0.0 copy-done.1
  57.3 1.2 %operator_first.1 = (f32[8,32,128]{2,1,0:T(8,128)S(1)}, f32[8,32,128]{2,1,0:T(8,128)S(1)}, f32[8,32,128]{2,1,0:T(8,128)S(1)}, f32[64,1,128]{2,1,0:T(1,128)S(1)}, f32[16,128]{1,0:T(8,128)S(1)}) custom-call(f32[8,32,128]{2,1,0:T(8,128)S(1)} %copy-done.1, f32[8,32,128]{2,1,0:T(8,128)S(1)} %copy-done.2, f32[3,8,32,128]{3,2,1,0:T(8,128)S(1)} %copy-done, ...), custom_call_target="tpu_custom_call" | custom-call | tf_op jit(solution)/shard_map/operator_first/pallas_call | solution.py:635
  58.5 17.6 %all_to_all.26.zrec_ref = f32[64,1,128]{2,1,0:T(1,128)S(1)} all-to-all(f32[64,1,128]{2,1,0:T(1,128)S(1)} %get-tuple-element.43), channel_id=1, replica_groups=mesh['gx'=8,'gy'=8,'gz'=16] {'gz'}, dimensions={0} | all-to-all | bytes 65536 | tf_op jit(solution)/shard_map/all_to_all | solution.py:670
  76.0 0.7 lines_second.1
  76.7 2.7 %collective-permute-start.4 = (f32[32,128]{1,0:T(8,128)S(1)}, f32[32,128]{1,0:T(8,128)S(1)}, u32[]{:S(2)}, u32[]{:S(2)}) collective-permute-start(f32[32,128]{1,0:T(8,128)S(1)} %get-tuple-element.51), channel_id=1, source_target_pairs={{0,128},{128,256},{256,384},{384,512},{512,640},{640,768},{768,896... | collective-permute-start | bytes 49160 | tf_op jit(solution)/shard_map/ppermute | solution.py:663
  79.3 0.0 collective-permute-start.5
  79.3 2.7 %collective-permute-start.6 = (f32[8,128]{1,0:T(8,128)S(1)}, f32[8,128]{1,0:T(8,128)S(1)}, u32[]{:S(2)}, u32[]{:S(2)}) collective-permute-start(f32[8,128]{1,0:T(8,128)S(1)} %get-tuple-element.53), channel_id=1, source_target_pairs={{0,16},{16,32},{32,48},{48,64},{64,80},{80,96},{96,112},{112,240},... | collective-permute-start | bytes 12296 | tf_op jit(solution)/shard_map/ppermute | solution.py:665
  82.0 0.0 collective-permute-start.7
  82.0 0.8 collective-permute-done.6.h2
  82.8 0.6 collective-permute-done.7.h3
  83.4 0.0 collective-permute-done.4.h0
  83.4 0.0 collective-permute-done.5.h1
  83.4 1.0 operator_second.1
  84.4 16.0 %all_to_all.27.xrec_ref = f32[64,2,128]{2,1,0:T(2,128)S(1)} all-to-all(f32[64,2,128]{2,1,0:T(2,128)S(1)} %get-tuple-element.55), channel_id=1, replica_groups=mesh['gx'=8,'gy'=8,'gz'=16] {'gx','gy'}, dimensions={0} | all-to-all | bytes 131072 | tf_op jit(solution)/shard_map/all_to_all | solution.py:673
  100.4 0.3 plane.1
  100.8 13.8 %all_to_all.28.all_ref = f32[16,1,128]{2,1,0:T(1,128)S(1)} all-to-all(f32[16,1,128]{2,1,0:T(1,128)S(1)} %broadcast_in_dim.9), channel_id=1, replica_groups=mesh['gx'=8,'gy'=8,'gz'=16] {'gz'}, dimensions={0} | all-to-all | bytes 16384 | tf_op jit(solution)/shard_map/all_to_all | solution.py:670
  114.6 0.8 end.1
  (1 shorter events, 0.0 us)
Async XLA Ops:
  0.6 0.7 copy-start.3
  1.3 56.0 %copy-start = (f32[3,8,32,128]{3,2,1,0:T(8,128)S(1)}, f32[3,8,32,128]{3,2,1,0:T(8,128)}, u32[]{:S(2)}) copy-start(f32[3,8,32,128]{3,2,1,0:T(8,128)} %kappa_ref.5) | copy-start | bytes 1179652
  4.2 31.0 %all-to-all-start = ((f32[80,1,128]{2,1,0:T(1,128)}), f32[80,1,128]{2,1,0:T(1,128)S(1)}, u32[]{:S(2)}, u32[]{:S(2)}) async-start(f32[80,1,128]{2,1,0:T(1,128)} %get-tuple-element.31), calls=%async_computation | async-start | bytes 81920 | tf_op jit(solution)/shard_map/all_to_all | solution.py:670
  23.6 6.2 %collective-permute-start = (f32[32,128]{1,0:T(8,128)S(1)}, f32[32,128]{1,0:T(8,128)S(1)}, u32[]{:S(2)}, u32[]{:S(2)}) collective-permute-start(f32[32,128]{1,0:T(8,128)S(1)} %get-tuple-element.34), channel_id=1, source_target_pairs={{0,128},{128,256},{256,384},{384,512},{512,640},{640,768},{768,896... | collective-permute-start | bytes 49160 | tf_op jit(solution)/shard_map/ppermute | solution.py:663
  25.7 31.6 %copy-start.2 = (f32[8,32,128]{2,1,0:T(8,128)S(1)}, f32[8,32,128]{2,1,0:T(8,128)}, u32[]{:S(2)}) copy-start(f32[8,32,128]{2,1,0:T(8,128)} %sigma_ref.5) | copy-start | bytes 393220
  25.7 31.6 %copy-start.1 = (f32[8,32,128]{2,1,0:T(8,128)S(1)}, f32[8,32,128]{2,1,0:T(8,128)}, u32[]{:S(2)}) copy-start(f32[8,32,128]{2,1,0:T(8,128)} %r_ref.5) | copy-start | bytes 393220
  25.7 4.1 %collective-permute-start.1 = (f32[32,128]{1,0:T(8,128)S(1)}, f32[32,128]{1,0:T(8,128)S(1)}, u32[]{:S(2)}, u32[]{:S(2)}) collective-permute-start(f32[32,128]{1,0:T(8,128)S(1)} %get-tuple-element.35), channel_id=1, source_target_pairs={{128,0},{256,128},{384,256},{512,384},{640,512},{768,640},{896,768... | collective-permute-start | bytes 49160 | tf_op jit(solution)/shard_map/ppermute | solution.py:664
  25.7 2.8 %collective-permute-start.2 = (f32[8,128]{1,0:T(8,128)S(1)}, f32[8,128]{1,0:T(8,128)S(1)}, u32[]{:S(2)}, u32[]{:S(2)}) collective-permute-start(f32[8,128]{1,0:T(8,128)S(1)} %get-tuple-element.36), channel_id=1, source_target_pairs={{0,16},{16,32},{32,48},{48,64},{64,80},{80,96},{96,112},{112,240},... | collective-permute-start | bytes 12296 | tf_op jit(solution)/shard_map/ppermute | solution.py:665
  27.6 2.2 %collective-permute-start.3 = (f32[8,128]{1,0:T(8,128)S(1)}, f32[8,128]{1,0:T(8,128)S(1)}, u32[]{:S(2)}, u32[]{:S(2)}) collective-permute-start(f32[8,128]{1,0:T(8,128)S(1)} %get-tuple-element.37), channel_id=1, source_target_pairs={{16,0},{32,16},{48,32},{64,48},{80,64},{96,80},{112,96},{240,112},... | collective-permute-start | bytes 12296 | tf_op jit(solution)/shard_map/ppermute | solution.py:666
  76.7 6.7 %collective-permute-start.4 = (f32[32,128]{1,0:T(8,128)S(1)}, f32[32,128]{1,0:T(8,128)S(1)}, u32[]{:S(2)}, u32[]{:S(2)}) collective-permute-start(f32[32,128]{1,0:T(8,128)S(1)} %get-tuple-element.51), channel_id=1, source_target_pairs={{0,128},{128,256},{256,384},{384,512},{512,640},{640,768},{768,896... | collective-permute-start | bytes 49160 | tf_op jit(solution)/shard_map/ppermute | solution.py:663
  79.3 4.1 %collective-permute-start.5 = (f32[32,128]{1,0:T(8,128)S(1)}, f32[32,128]{1,0:T(8,128)S(1)}, u32[]{:S(2)}, u32[]{:S(2)}) collective-permute-start(f32[32,128]{1,0:T(8,128)S(1)} %get-tuple-element.52), channel_id=1, source_target_pairs={{128,0},{256,128},{384,256},{512,384},{640,512},{768,640},{896,768... | collective-permute-start | bytes 49160 | tf_op jit(solution)/shard_map/ppermute | solution.py:664
  79.3 3.5 %collective-permute-start.6 = (f32[8,128]{1,0:T(8,128)S(1)}, f32[8,128]{1,0:T(8,128)S(1)}, u32[]{:S(2)}, u32[]{:S(2)}) collective-permute-start(f32[8,128]{1,0:T(8,128)S(1)} %get-tuple-element.53), channel_id=1, source_target_pairs={{0,16},{16,32},{32,48},{48,64},{64,80},{80,96},{96,112},{112,240},... | collective-permute-start | bytes 12296 | tf_op jit(solution)/shard_map/ppermute | solution.py:665
  82.0 1.4 %collective-permute-start.7 = (f32[8,128]{1,0:T(8,128)S(1)}, f32[8,128]{1,0:T(8,128)S(1)}, u32[]{:S(2)}, u32[]{:S(2)}) collective-permute-start(f32[8,128]{1,0:T(8,128)S(1)} %get-tuple-element.54), channel_id=1, source_target_pairs={{16,0},{32,16},{48,32},{64,48},{80,64},{96,80},{112,96},{240,112},... | collective-permute-start | bytes 12296 | tf_op jit(solution)/shard_map/ppermute | solution.py:666

commit v9 on v8

--- a/solution.py
+++ b/solution.py
@@ -280,7 +280,7 @@
 
 
 def first_lines_kernel(
-    sizes, zrec_ref, loc_ref, alpha_ref, h0, h1, h2, h3, xmsg_ref, own_ref, zhalo_ref, chain_ref, final_ref, sol_ref
+    sizes, zrec_ref, loc_ref, alpha_ref, xmsg_ref, own_ref, zhalo_ref, chain_ref, final_ref, sol_ref
 ):
     nx, ny, nz = sizes
     mx, my = lax.axis_index("gx"), lax.axis_index("gy")
@@ -681,7 +681,7 @@
     halos = halo(sides)
     xmsg, own, zhalo, chain, final = call(
         bind(first_lines_kernel), [to_xy, tile, tile, (4, nz, 128), tile], [coarse], "lines_first"
-    )(zrec, loc, alpha, *halos)
+    )(zrec, loc, alpha)
     xrec = along_xy(xmsg)
     z1, w1, jac, zmsg, alpha = call(
         bind(first_kernel), [field, field, field, (nz * 4, 1, 128), coarse], name="operator_first"

time: 116 us -> 115 us (level)
  blocking collectives: 68.8 us -> 77.8 us
  starting transfers between devices: 28.7 us -> 20.6 us
  waiting for transfers between devices: 8.99 us -> 7.47 us
    all_to_all x2 -> x3, blocking collectives: 31.4 us -> 58.6 us  [along_z(): lax.all_to_all(message, 'gz', split_axis=0, concat_axis=0, tiled=True)]
    all_to_all x2 -> x1, blocking collectives: 37.4 us -> 19.2 us  [along_xy(): lax.all_to_all(message, ('gx', 'gy'), split_axis=0, concat_axis=0, tiled=...]
    all_to_all x1, starting transfers between devices: 19.4 us -> 12.2 us  [along_xy(): lax.all_to_all(message, ('gx', 'gy'), split_axis=0, concat_axis=0, tiled=...]
    all_to_all x1, waiting for transfers between devices: 5.35 us -> 3.79 us  [along_xy(): lax.all_to_all(message, ('gx', 'gy'), split_axis=0, concat_axis=0, tiled=...]
where the time goes in v9:
time: 115 us
  blocking collectives  77.8 us (68%)
  starting transfers between devices  20.6 us (18%)
  Pallas kernels  7.59 us (7%)
  waiting for transfers between devices  7.47 us (6%)
    all_to_all x3, blocking collectives, along_z(): lax.all_to_all(message, 'gz', split_axis=0, concat_axis=0, tiled=True)  58.6 us
    all_to_all x1, blocking collectives, along_xy(): lax.all_to_all(message, ('gx', 'gy'), split_axis=0, concat_axis=0, tiled=...  19.2 us
    all_to_all x1, starting transfers between devices, along_xy(): lax.all_to_all(message, ('gx', 'gy'), split_axis=0, concat_axis=0, tiled=...  12.2 us
    pallas_call x7, Pallas kernels, run(): pl.pallas_call(kernel, out_shape=[jax.ShapeDtypeStruct(s, F32) for s in o...  7.59 us
    ppermute x2, starting transfers between devices, halo(): lax.ppermute(y_one, ('gx', 'gy'), fold)  4.45 us
    ppermute x2, starting transfers between devices, halo(): lax.ppermute(xhi, 'gx', [(i, (i + 1) % nx) for i in range(nx)])  3.96 us
    all_to_all x1, waiting for transfers between devices, along_xy(): lax.all_to_all(message, ('gx', 'gy'), split_axis=0, concat_axis=0, tiled=...  3.79 us
  transfers between devices with their start and end apart: 9, of which 5 were waited for; matrix products, arithmetic and copies ran while one was open for 0% of the time, Pallas kernels for 0%

profile of v9, /device:TPU:1, one launch (start us, length us, event | category | flops | bytes accessed | tf_op | source)
XLA Modules:
  0.0 114.9 jit_solution(17325629851242876003)
XLA Ops:
  0.6 0.0 copy-start.3
  0.6 0.7 copy-done.3
  1.3 0.0 copy-start
  1.3 2.3 %begin.1 = (f32[80,1,128]{2,1,0:T(1,128)S(1)}, f32[3,16,128]{2,1,0:T(8,128)S(1)}, f32[16,128]{1,0:T(8,128)S(1)}, f32[8,128]{1,0:T(8,128)S(1)}, f32[32,128]{1,0:T...) custom-call(f32[8,32,128]{2,1,0:T(8,128)} %r_ref.5, f32[8,32,128]{2,1,0:T(8,128)} %sigma_ref.5, ...), custom_call_target="tpu_custom_call" | custom-call | tf_op jit(solution)/shard_map/begin/pallas_call | solution.py:635
  3.6 0.0 copy-start.2
  3.6 30.9 %all_to_all.25.zrec_ref = f32[80,1,128]{2,1,0:T(1,128)S(1)} all-to-all(f32[80,1,128]{2,1,0:T(1,128)S(1)} %get-tuple-element.31), channel_id=1, replica_groups=mesh['gx'=8,'gy'=8,'gz'=16] {'gz'}, dimensions={0} | all-to-all | bytes 81920 | tf_op jit(solution)/shard_map/all_to_all | solution.py:670
  34.5 0.0 copy-start.1
  34.5 1.3 %lines_first.1 = (f32[64,2,128]{2,1,0:T(2,128)}, f32[8,128]{1,0:T(8,128)S(1)}, f32[8,128]{1,0:T(8,128)S(1)}, f32[4,16,128]{2,1,0:T(8,128)S(1)}, f32[8,128]{1,0:T(8,128)S(1)}) custom-call(f32[80,1,128]{2,1,0:T(1,128)S(1)} %all_to_all.25.zrec_ref, f32[3,16,128]{2,1,0:T(8,128)S(1)} %get-tuple-element.32.loc_ref, f32[16,128]{1,0:T(8,128)S(1)} %get-tuple-element.33.alpha_ref), custom_call_target="tpu_custom_call" | custom-call | tf_op jit(solution)/shard_map/lines_first/pallas_call | solution.py:635
  35.8 12.2 %all-to-all-start.1 = ((f32[64,2,128]{2,1,0:T(2,128)}), f32[64,2,128]{2,1,0:T(2,128)S(1)}, u32[]{:S(2)}, u32[]{:S(2)}) async-start(f32[64,2,128]{2,1,0:T(2,128)} %get-tuple-element.34), calls=%async_computation.1 | async-start | bytes 131072 | tf_op jit(solution)/shard_map/all_to_all | solution.py:673
  48.0 1.6 %collective-permute-start = (f32[32,128]{1,0:T(8,128)S(1)}, f32[32,128]{1,0:T(8,128)S(1)}, u32[]{:S(2)}, u32[]{:S(2)}) collective-permute-start(f32[32,128]{1,0:T(8,128)S(1)} %get-tuple-element.37), channel_id=1, source_target_pairs={{0,128},{128,256},{256,384},{384,512},{512,640},{640,768},{768,896... | collective-permute-start | bytes 49160 | tf_op jit(solution)/shard_map/ppermute | solution.py:663
  49.6 0.0 collective-permute-start.1
  49.6 1.8 %collective-permute-start.2 = (f32[8,128]{1,0:T(8,128)S(1)}, f32[8,128]{1,0:T(8,128)S(1)}, u32[]{:S(2)}, u32[]{:S(2)}) collective-permute-start(f32[8,128]{1,0:T(8,128)S(1)} %get-tuple-element.39), channel_id=1, source_target_pairs={{0,16},{16,32},{32,48},{48,64},{64,80},{80,96},{96,112},{112,240},... | collective-permute-start | bytes 12296 | tf_op jit(solution)/shard_map/ppermute | solution.py:665
  51.4 0.0 collective-permute-start.3
  51.4 1.0 collective-permute-done.2.h2
  52.4 1.2 %collective-permute-done.3.h3 = f32[8,128]{1,0:T(8,128)S(1)} collective-permute-done((f32[8,128]{1,0:T(8,128)S(1)}, f32[8,128]{1,0:T(8,128)S(1)}, u32[]{:S(2)}, u32[]{:S(2)}) %collective-permute-start.3) | collective-permute-done | bytes 4128 | tf_op jit(solution)/shard_map/ppermute | solution.py:666
  53.6 0.0 collective-permute-done.h0
  53.6 0.0 collective-permute-done.1.h1
  53.6 3.8 %all-to-all-done.1.xrec_ref = f32[64,2,128]{2,1,0:T(2,128)S(1)} async-done(((f32[64,2,128]{2,1,0:T(2,128)}), f32[64,2,128]{2,1,0:T(2,128)S(1)}, u32[]{:S(2)}, u32[]{:S(2)}) %all-to-all-start.1) | async-done | bytes 65568 | tf_op jit(solution)/shard_map/all_to_all | solution.py:673
  57.4 0.0 copy-done
  57.4 0.0 copy-done.2
  57.4 0.0 copy-done.1
  57.4 1.2 %operator_first.1 = (f32[8,32,128]{2,1,0:T(8,128)S(1)}, f32[8,32,128]{2,1,0:T(8,128)S(1)}, f32[8,32,128]{2,1,0:T(8,128)S(1)}, f32[64,1,128]{2,1,0:T(1,128)S(1)}, f32[16,128]{1,0:T(8,128)S(1)}) custom-call(f32[8,32,128]{2,1,0:T(8,128)S(1)} %copy-done.1, f32[8,32,128]{2,1,0:T(8,128)S(1)} %copy-done.2, f32[3,8,32,128]{3,2,1,0:T(8,128)S(1)} %copy-done, ...), custom_call_target="tpu_custom_call" | custom-call | tf_op jit(solution)/shard_map/operator_first/pallas_call | solution.py:635
  58.6 14.0 %all_to_all.26.zrec_ref = f32[64,1,128]{2,1,0:T(1,128)S(1)} all-to-all(f32[64,1,128]{2,1,0:T(1,128)S(1)} %get-tuple-element.43), channel_id=1, replica_groups=mesh['gx'=8,'gy'=8,'gz'=16] {'gz'}, dimensions={0} | all-to-all | bytes 65536 | tf_op jit(solution)/shard_map/all_to_all | solution.py:670
  72.6 0.7 lines_second.1
  73.2 2.3 %collective-permute-start.4 = (f32[32,128]{1,0:T(8,128)S(1)}, f32[32,128]{1,0:T(8,128)S(1)}, u32[]{:S(2)}, u32[]{:S(2)}) collective-permute-start(f32[32,128]{1,0:T(8,128)S(1)} %get-tuple-element.51), channel_id=1, source_target_pairs={{0,128},{128,256},{256,384},{384,512},{512,640},{640,768},{768,896... | collective-permute-start | bytes 49160 | tf_op jit(solution)/shard_map/ppermute | solution.py:663
  75.6 0.0 collective-permute-start.5
  75.6 2.7 %collective-permute-start.6 = (f32[8,128]{1,0:T(8,128)S(1)}, f32[8,128]{1,0:T(8,128)S(1)}, u32[]{:S(2)}, u32[]{:S(2)}) collective-permute-start(f32[8,128]{1,0:T(8,128)S(1)} %get-tuple-element.53), channel_id=1, source_target_pairs={{0,16},{16,32},{32,48},{48,64},{64,80},{80,96},{96,112},{112,240},... | collective-permute-start | bytes 12296 | tf_op jit(solution)/shard_map/ppermute | solution.py:665
  78.2 0.0 collective-permute-start.7
  78.2 0.8 collective-permute-done.6.h2
  79.1 0.6 collective-permute-done.7.h3
  79.7 0.0 collective-permute-done.4.h0
  79.7 0.0 collective-permute-done.5.h1
  79.7 1.0 operator_second.1
  80.7 19.2 %all_to_all.27.xrec_ref = f32[64,2,128]{2,1,0:T(2,128)S(1)} all-to-all(f32[64,2,128]{2,1,0:T(2,128)S(1)} %get-tuple-element.55), channel_id=1, replica_groups=mesh['gx'=8,'gy'=8,'gz'=16] {'gx','gy'}, dimensions={0} | all-to-all | bytes 131072 | tf_op jit(solution)/shard_map/all_to_all | solution.py:673
  99.8 0.3 plane.1
  100.2 13.8 %all_to_all.28.all_ref = f32[16,1,128]{2,1,0:T(1,128)S(1)} all-to-all(f32[16,1,128]{2,1,0:T(1,128)S(1)} %broadcast_in_dim.9), channel_id=1, replica_groups=mesh['gx'=8,'gy'=8,'gz'=16] {'gz'}, dimensions={0} | all-to-all | bytes 16384 | tf_op jit(solution)/shard_map/all_to_all | solution.py:670
  114.0 0.8 end.1
  (1 shorter events, 0.0 us)
Async XLA Ops:
  0.6 0.7 copy-start.3
  1.3 56.1 %copy-start = (f32[3,8,32,128]{3,2,1,0:T(8,128)S(1)}, f32[3,8,32,128]{3,2,1,0:T(8,128)}, u32[]{:S(2)}) copy-start(f32[3,8,32,128]{3,2,1,0:T(8,128)} %kappa_ref.5) | copy-start | bytes 1179652
  3.6 53.8 %copy-start.2 = (f32[8,32,128]{2,1,0:T(8,128)S(1)}, f32[8,32,128]{2,1,0:T(8,128)}, u32[]{:S(2)}) copy-start(f32[8,32,128]{2,1,0:T(8,128)} %sigma_ref.5) | copy-start | bytes 393220
  34.5 23.0 %copy-start.1 = (f32[8,32,128]{2,1,0:T(8,128)S(1)}, f32[8,32,128]{2,1,0:T(8,128)}, u32[]{:S(2)}) copy-start(f32[8,32,128]{2,1,0:T(8,128)} %r_ref.5) | copy-start | bytes 393220
  35.8 21.6 %all-to-all-start.1 = ((f32[64,2,128]{2,1,0:T(2,128)}), f32[64,2,128]{2,1,0:T(2,128)S(1)}, u32[]{:S(2)}, u32[]{:S(2)}) async-start(f32[64,2,128]{2,1,0:T(2,128)} %get-tuple-element.34), calls=%async_computation.1 | async-start | bytes 131072 | tf_op jit(solution)/shard_map/all_to_all | solution.py:673
  48.0 5.7 %collective-permute-start = (f32[32,128]{1,0:T(8,128)S(1)}, f32[32,128]{1,0:T(8,128)S(1)}, u32[]{:S(2)}, u32[]{:S(2)}) collective-permute-start(f32[32,128]{1,0:T(8,128)S(1)} %get-tuple-element.37), channel_id=1, source_target_pairs={{0,128},{128,256},{256,384},{384,512},{512,640},{640,768},{768,896... | collective-permute-start | bytes 49160 | tf_op jit(solution)/shard_map/ppermute | solution.py:663
  49.6 4.0 %collective-permute-start.1 = (f32[32,128]{1,0:T(8,128)S(1)}, f32[32,128]{1,0:T(8,128)S(1)}, u32[]{:S(2)}, u32[]{:S(2)}) collective-permute-start(f32[32,128]{1,0:T(8,128)S(1)} %get-tuple-element.38), channel_id=1, source_target_pairs={{128,0},{256,128},{384,256},{512,384},{640,512},{768,640},{896,768... | collective-permute-start | bytes 49160 | tf_op jit(solution)/shard_map/ppermute | solution.py:664
  49.6 2.8 %collective-permute-start.2 = (f32[8,128]{1,0:T(8,128)S(1)}, f32[8,128]{1,0:T(8,128)S(1)}, u32[]{:S(2)}, u32[]{:S(2)}) collective-permute-start(f32[8,128]{1,0:T(8,128)S(1)} %get-tuple-element.39), channel_id=1, source_target_pairs={{0,16},{16,32},{32,48},{48,64},{64,80},{80,96},{96,112},{112,240},... | collective-permute-start | bytes 12296 | tf_op jit(solution)/shard_map/ppermute | solution.py:665
  51.4 2.2 %collective-permute-start.3 = (f32[8,128]{1,0:T(8,128)S(1)}, f32[8,128]{1,0:T(8,128)S(1)}, u32[]{:S(2)}, u32[]{:S(2)}) collective-permute-start(f32[8,128]{1,0:T(8,128)S(1)} %get-tuple-element.40), channel_id=1, source_target_pairs={{16,0},{32,16},{48,32},{64,48},{80,64},{96,80},{112,96},{240,112},... | collective-permute-start | bytes 12296 | tf_op jit(solution)/shard_map/ppermute | solution.py:666
  73.2 6.4 %collective-permute-start.4 = (f32[32,128]{1,0:T(8,128)S(1)}, f32[32,128]{1,0:T(8,128)S(1)}, u32[]{:S(2)}, u32[]{:S(2)}) collective-permute-start(f32[32,128]{1,0:T(8,128)S(1)} %get-tuple-element.51), channel_id=1, source_target_pairs={{0,128},{128,256},{256,384},{384,512},{512,640},{640,768},{768,896... | collective-permute-start | bytes 49160 | tf_op jit(solution)/shard_map/ppermute | solution.py:663
  75.6 4.1 %collective-permute-start.5 = (f32[32,128]{1,0:T(8,128)S(1)}, f32[32,128]{1,0:T(8,128)S(1)}, u32[]{:S(2)}, u32[]{:S(2)}) collective-permute-start(f32[32,128]{1,0:T(8,128)S(1)} %get-tuple-element.52), channel_id=1, source_target_pairs={{128,0},{256,128},{384,256},{512,384},{640,512},{768,640},{896,768... | collective-permute-start | bytes 49160 | tf_op jit(solution)/shard_map/ppermute | solution.py:664
  75.6 3.5 %collective-permute-start.6 = (f32[8,128]{1,0:T(8,128)S(1)}, f32[8,128]{1,0:T(8,128)S(1)}, u32[]{:S(2)}, u32[]{:S(2)}) collective-permute-start(f32[8,128]{1,0:T(8,128)S(1)} %get-tuple-element.53), channel_id=1, source_target_pairs={{0,16},{16,32},{32,48},{48,64},{64,80},{80,96},{96,112},{112,240},... | collective-permute-start | bytes 12296 | tf_op jit(solution)/shard_map/ppermute | solution.py:665
  78.2 1.4 %collective-permute-start.7 = (f32[8,128]{1,0:T(8,128)S(1)}, f32[8,128]{1,0:T(8,128)S(1)}, u32[]{:S(2)}, u32[]{:S(2)}) collective-permute-start(f32[8,128]{1,0:T(8,128)S(1)} %get-tuple-element.54), channel_id=1, source_target_pairs={{16,0},{32,16},{48,32},{64,48},{80,64},{96,80},{112,96},{240,112},... | collective-permute-start | bytes 12296 | tf_op jit(solution)/shard_map/ppermute | solution.py:666

commit v10 on v9

--- a/solution.py
+++ b/solution.py
@@ -280,7 +280,7 @@
 
 
 def first_lines_kernel(
-    sizes, zrec_ref, loc_ref, alpha_ref, xmsg_ref, own_ref, zhalo_ref, chain_ref, final_ref, sol_ref
+    sizes, zrec_ref, loc_ref, alpha_ref, h0, h1, xmsg_ref, own_ref, zhalo_ref, chain_ref, final_ref, sol_ref
 ):
     nx, ny, nz = sizes
     mx, my = lax.axis_index("gx"), lax.axis_index("gy")
@@ -681,7 +681,7 @@
     halos = halo(sides)
     xmsg, own, zhalo, chain, final = call(
         bind(first_lines_kernel), [to_xy, tile, tile, (4, nz, 128), tile], [coarse], "lines_first"
-    )(zrec, loc, alpha)
+    )(zrec, loc, alpha, *halos[:2])
     xrec = along_xy(xmsg)
     z1, w1, jac, zmsg, alpha = call(
         bind(first_kernel), [field, field, field, (nz * 4, 1, 128), coarse], name="operator_first"

time: 115 us -> 115 us (level)
  blocking collectives: 77.8 us -> 45.8 us
  starting transfers between devices: 20.6 us -> 40.6 us
  waiting for transfers between devices: 7.47 us -> 18.8 us
    all_to_all x3 -> x2, blocking collectives: 58.6 us -> 28.6 us  [along_z(): lax.all_to_all(message, 'gz', split_axis=0, concat_axis=0, tiled=True)]
    all_to_all x0 -> x1, starting transfers between devices: none -> 19.6 us  [along_z(): lax.all_to_all(message, 'gz', split_axis=0, concat_axis=0, tiled=True)]
    all_to_all x0 -> x1, waiting for transfers between devices: none -> 5.98 us  [along_z(): lax.all_to_all(message, 'gz', split_axis=0, concat_axis=0, tiled=True)]
    all_to_all x1, waiting for transfers between devices: 3.79 us -> 6.69 us  [along_xy(): lax.all_to_all(message, ('gx', 'gy'), split_axis=0, concat_axis=0, tiled=...]
    ppermute x2, waiting for transfers between devices: 0.01 us -> 2.59 us  [halo(): lax.ppermute(xlo, 'gx', [((i + 1) % nx, i) for i in range(nx)])]
    all_to_all x1, blocking collectives: 19.2 us -> 17.2 us  [along_xy(): lax.all_to_all(message, ('gx', 'gy'), split_axis=0, concat_axis=0, tiled=...]
    ppermute x2, starting transfers between devices: 4.45 us -> 3.14 us  [halo(): lax.ppermute(y_one, ('gx', 'gy'), fold)]
    ppermute x2, waiting for transfers between devices: 1.86 us -> 0.62 us  [halo(): lax.ppermute(y_two, ('gx', 'gy'), unfold)]
  transfers between devices with their start and end apart: 9 -> 10, of which waited for: 5 -> 7; matrix products, arithmetic and copies ran while one was open for 0% -> 0% of each run, Pallas kernels for 0% -> 0%
where the time goes in v10:
time: 115 us
  blocking collectives  45.8 us (40%)
  starting transfers between devices  40.6 us (35%)
  waiting for transfers between devices  18.8 us (16%)
  Pallas kernels  8.21 us (7%)
    all_to_all x2, blocking collectives, along_z(): lax.all_to_all(message, 'gz', split_axis=0, concat_axis=0, tiled=True)  28.6 us
    all_to_all x1, starting transfers between devices, along_z(): lax.all_to_all(message, 'gz', split_axis=0, concat_axis=0, tiled=True)  19.6 us
    all_to_all x1, blocking collectives, along_xy(): lax.all_to_all(message, ('gx', 'gy'), split_axis=0, concat_axis=0, tiled=...  17.2 us
    all_to_all x1, starting transfers between devices, along_xy(): lax.all_to_all(message, ('gx', 'gy'), split_axis=0, concat_axis=0, tiled=...  12.2 us
    pallas_call x7, Pallas kernels, run(): pl.pallas_call(kernel, out_shape=[jax.ShapeDtypeStruct(s, F32) for s in o...  8.21 us
    all_to_all x1, waiting for transfers between devices, along_xy(): lax.all_to_all(message, ('gx', 'gy'), split_axis=0, concat_axis=0, tiled=...  6.69 us
    all_to_all x1, waiting for transfers between devices, along_z(): lax.all_to_all(message, 'gz', split_axis=0, concat_axis=0, tiled=True)  5.98 us
    ppermute x2, starting transfers between devices, halo(): lax.ppermute(xhi, 'gx', [(i, (i + 1) % nx) for i in range(nx)])  4.71 us
  transfers between devices with their start and end apart: 10, of which 7 were waited for; matrix products, arithmetic and copies ran while one was open for 0% of the time, Pallas kernels for 0%

profile of v10, /device:TPU:1, one launch (start us, length us, event | category | flops | bytes accessed | tf_op | source)
XLA Modules:
  0.0 114.9 jit_solution(5395486317104691433)
XLA Ops:
  0.6 0.0 copy-start.3
  0.6 0.7 copy-done.3
  1.3 0.0 copy-start
  1.3 2.9 %begin.1 = (f32[80,1,128]{2,1,0:T(1,128)}, f32[3,16,128]{2,1,0:T(8,128)S(1)}, f32[16,128]{1,0:T(8,128)S(1)}, f32[8,128]{1,0:T(8,128)S(1)}, f32[32,128]{1,0:T(8,1...) custom-call(f32[8,32,128]{2,1,0:T(8,128)} %r_ref.5, f32[8,32,128]{2,1,0:T(8,128)} %sigma_ref.5, ...), custom_call_target="tpu_custom_call" | custom-call | tf_op jit(solution)/shard_map/begin/pallas_call | solution.py:635
  4.2 0.0 copy-start.2
  4.2 19.6 %all-to-all-start = ((f32[80,1,128]{2,1,0:T(1,128)}), f32[80,1,128]{2,1,0:T(1,128)S(1)}, u32[]{:S(2)}, u32[]{:S(2)}) async-start(f32[80,1,128]{2,1,0:T(1,128)} %get-tuple-element.31), calls=%async_computation | async-start | bytes 81920 | tf_op jit(solution)/shard_map/all_to_all | solution.py:670
  23.8 0.0 copy-start.1
  23.8 2.1 %collective-permute-start = (f32[32,128]{1,0:T(8,128)S(1)}, f32[32,128]{1,0:T(8,128)S(1)}, u32[]{:S(2)}, u32[]{:S(2)}) collective-permute-start(f32[32,128]{1,0:T(8,128)S(1)} %get-tuple-element.34), channel_id=1, source_target_pairs={{0,128},{128,256},{256,384},{384,512},{512,640},{640,768},{768,896... | collective-permute-start | bytes 49160 | tf_op jit(solution)/shard_map/ppermute | solution.py:663
  25.9 0.0 collective-permute-start.1
  25.9 0.9 collective-permute-done.h0
  26.7 2.6 %collective-permute-done.1.h1 = f32[32,128]{1,0:T(8,128)S(1)} collective-permute-done((f32[32,128]{1,0:T(8,128)S(1)}, f32[32,128]{1,0:T(8,128)S(1)}, u32[]{:S(2)}, u32[]{:S(2)}) %collective-permute-start.1) | collective-permute-done | bytes 16416 | tf_op jit(solution)/shard_map/ppermute | solution.py:664
  29.3 6.0 %all-to-all-done.zrec_ref = f32[80,1,128]{2,1,0:T(1,128)S(1)} async-done(((f32[80,1,128]{2,1,0:T(1,128)}), f32[80,1,128]{2,1,0:T(1,128)S(1)}, u32[]{:S(2)}, u32[]{:S(2)}) %all-to-all-start) | async-done | bytes 40992 | tf_op jit(solution)/shard_map/all_to_all | solution.py:670
  35.3 1.3 %lines_first.1 = (f32[64,2,128]{2,1,0:T(2,128)}, f32[8,128]{1,0:T(8,128)S(1)}, f32[8,128]{1,0:T(8,128)S(1)}, f32[4,16,128]{2,1,0:T(8,128)S(1)}, f32[8,128]{1,0:T(8,128)S(1)}) custom-call(f32[80,1,128]{2,1,0:T(1,128)S(1)} %all-to-all-done.zrec_ref, f32[3,16,128]{2,1,0:T(8,128)S(1)} %get-tuple-element.32.loc_ref, f32[16,128]{1,0:T(8,128)S(1)} %get-tuple-element.33.alpha_ref, ...), custom_call_target="tpu_custom_call" | custom-call | tf_op jit(solution)/shard_map/lines_first/pallas_call | solution.py:635
  36.6 12.2 %all-to-all-start.1 = ((f32[64,2,128]{2,1,0:T(2,128)}), f32[64,2,128]{2,1,0:T(2,128)S(1)}, u32[]{:S(2)}, u32[]{:S(2)}) async-start(f32[64,2,128]{2,1,0:T(2,128)} %get-tuple-element.36), calls=%async_computation.1 | async-start | bytes 131072 | tf_op jit(solution)/shard_map/all_to_all | solution.py:673
  48.8 0.5 collective-permute-start.2
  49.3 1.0 collective-permute-start.3
  50.3 1.3 %collective-permute-done.2.h2 = f32[8,128]{1,0:T(8,128)S(1)} collective-permute-done((f32[8,128]{1,0:T(8,128)S(1)}, f32[8,128]{1,0:T(8,128)S(1)}, u32[]{:S(2)}, u32[]{:S(2)}) %collective-permute-start.2) | collective-permute-done | bytes 4128 | tf_op jit(solution)/shard_map/ppermute | solution.py:665
  51.6 0.0 collective-permute-done.3.h3
  51.6 6.7 %all-to-all-done.1.xrec_ref = f32[64,2,128]{2,1,0:T(2,128)S(1)} async-done(((f32[64,2,128]{2,1,0:T(2,128)}), f32[64,2,128]{2,1,0:T(2,128)S(1)}, u32[]{:S(2)}, u32[]{:S(2)}) %all-to-all-start.1) | async-done | bytes 65568 | tf_op jit(solution)/shard_map/all_to_all | solution.py:673
  58.3 0.0 copy-done
  58.3 0.0 copy-done.2
  58.3 0.0 copy-done.1
  58.3 1.2 %operator_first.1 = (f32[8,32,128]{2,1,0:T(8,128)S(1)}, f32[8,32,128]{2,1,0:T(8,128)S(1)}, f32[8,32,128]{2,1,0:T(8,128)S(1)}, f32[64,1,128]{2,1,0:T(1,128)S(1)}, f32[16,128]{1,0:T(8,128)S(1)}) custom-call(f32[8,32,128]{2,1,0:T(8,128)S(1)} %copy-done.1, f32[8,32,128]{2,1,0:T(8,128)S(1)} %copy-done.2, f32[3,8,32,128]{3,2,1,0:T(8,128)S(1)} %copy-done, ...), custom_call_target="tpu_custom_call" | custom-call | tf_op jit(solution)/shard_map/operator_first/pallas_call | solution.py:635
  59.5 14.7 %all_to_all.25.zrec_ref = f32[64,1,128]{2,1,0:T(1,128)S(1)} all-to-all(f32[64,1,128]{2,1,0:T(1,128)S(1)} %get-tuple-element.43), channel_id=1, replica_groups=mesh['gx'=8,'gy'=8,'gz'=16] {'gz'}, dimensions={0} | all-to-all | bytes 65536 | tf_op jit(solution)/shard_map/all_to_all | solution.py:670
  74.2 0.7 lines_second.1
  74.9 2.7 %collective-permute-start.4 = (f32[32,128]{1,0:T(8,128)S(1)}, f32[32,128]{1,0:T(8,128)S(1)}, u32[]{:S(2)}, u32[]{:S(2)}) collective-permute-start(f32[32,128]{1,0:T(8,128)S(1)} %get-tuple-element.51), channel_id=1, source_target_pairs={{0,128},{128,256},{256,384},{384,512},{512,640},{640,768},{768,896... | collective-permute-start | bytes 49160 | tf_op jit(solution)/shard_map/ppermute | solution.py:663
  77.5 0.0 collective-permute-start.5
  77.5 2.7 %collective-permute-start.6 = (f32[8,128]{1,0:T(8,128)S(1)}, f32[8,128]{1,0:T(8,128)S(1)}, u32[]{:S(2)}, u32[]{:S(2)}) collective-permute-start(f32[8,128]{1,0:T(8,128)S(1)} %get-tuple-element.53), channel_id=1, source_target_pairs={{0,16},{16,32},{32,48},{48,64},{64,80},{80,96},{96,112},{112,240},... | collective-permute-start | bytes 12296 | tf_op jit(solution)/shard_map/ppermute | solution.py:665
  80.2 0.0 collective-permute-start.7
  80.2 0.8 collective-permute-done.6.h2
  81.0 0.6 collective-permute-done.7.h3
  81.6 0.0 collective-permute-done.4.h0
  81.6 0.0 collective-permute-done.5.h1
  81.6 1.0 operator_second.1
  82.6 17.2 %all_to_all.26.xrec_ref = f32[64,2,128]{2,1,0:T(2,128)S(1)} all-to-all(f32[64,2,128]{2,1,0:T(2,128)S(1)} %get-tuple-element.55), channel_id=1, replica_groups=mesh['gx'=8,'gy'=8,'gz'=16] {'gx','gy'}, dimensions={0} | all-to-all | bytes 131072 | tf_op jit(solution)/shard_map/all_to_all | solution.py:673
  99.8 0.3 plane.1
  100.2 13.8 %all_to_all.27.all_ref = f32[16,1,128]{2,1,0:T(1,128)S(1)} all-to-all(f32[16,1,128]{2,1,0:T(1,128)S(1)} %broadcast_in_dim.9), channel_id=1, replica_groups=mesh['gx'=8,'gy'=8,'gz'=16] {'gz'}, dimensions={0} | all-to-all | bytes 16384 | tf_op jit(solution)/shard_map/all_to_all | solution.py:670
  114.0 0.8 end.1
  (1 shorter events, 0.0 us)
Async XLA Ops:
  0.6 0.7 copy-start.3
  1.3 56.9 %copy-start = (f32[3,8,32,128]{3,2,1,0:T(8,128)S(1)}, f32[3,8,32,128]{3,2,1,0:T(8,128)}, u32[]{:S(2)}) copy-start(f32[3,8,32,128]{3,2,1,0:T(8,128)} %kappa_ref.5) | copy-start | bytes 1179652
  4.2 54.1 %copy-start.2 = (f32[8,32,128]{2,1,0:T(8,128)S(1)}, f32[8,32,128]{2,1,0:T(8,128)}, u32[]{:S(2)}) copy-start(f32[8,32,128]{2,1,0:T(8,128)} %sigma_ref.5) | copy-start | bytes 393220
  4.2 31.1 %all-to-all-start = ((f32[80,1,128]{2,1,0:T(1,128)}), f32[80,1,128]{2,1,0:T(1,128)S(1)}, u32[]{:S(2)}, u32[]{:S(2)}) async-start(f32[80,1,128]{2,1,0:T(1,128)} %get-tuple-element.31), calls=%async_computation | async-start | bytes 81920 | tf_op jit(solution)/shard_map/all_to_all | solution.py:670
  23.8 34.5 %copy-start.1 = (f32[8,32,128]{2,1,0:T(8,128)S(1)}, f32[8,32,128]{2,1,0:T(8,128)}, u32[]{:S(2)}) copy-start(f32[8,32,128]{2,1,0:T(8,128)} %r_ref.5) | copy-start | bytes 393220
  23.8 2.9 %collective-permute-start = (f32[32,128]{1,0:T(8,128)S(1)}, f32[32,128]{1,0:T(8,128)S(1)}, u32[]{:S(2)}, u32[]{:S(2)}) collective-permute-start(f32[32,128]{1,0:T(8,128)S(1)} %get-tuple-element.34), channel_id=1, source_target_pairs={{0,128},{128,256},{256,384},{384,512},{512,640},{640,768},{768,896... | collective-permute-start | bytes 49160 | tf_op jit(solution)/shard_map/ppermute | solution.py:663
  25.9 3.5 %collective-permute-start.1 = (f32[32,128]{1,0:T(8,128)S(1)}, f32[32,128]{1,0:T(8,128)S(1)}, u32[]{:S(2)}, u32[]{:S(2)}) collective-permute-start(f32[32,128]{1,0:T(8,128)S(1)} %get-tuple-element.35), channel_id=1, source_target_pairs={{128,0},{256,128},{384,256},{512,384},{640,512},{768,640},{896,768... | collective-permute-start | bytes 49160 | tf_op jit(solution)/shard_map/ppermute | solution.py:664
  36.6 21.6 %all-to-all-start.1 = ((f32[64,2,128]{2,1,0:T(2,128)}), f32[64,2,128]{2,1,0:T(2,128)S(1)}, u32[]{:S(2)}, u32[]{:S(2)}) async-start(f32[64,2,128]{2,1,0:T(2,128)} %get-tuple-element.36), calls=%async_computation.1 | async-start | bytes 131072 | tf_op jit(solution)/shard_map/all_to_all | solution.py:673
  48.8 2.8 %collective-permute-start.2 = (f32[8,128]{1,0:T(8,128)S(1)}, f32[8,128]{1,0:T(8,128)S(1)}, u32[]{:S(2)}, u32[]{:S(2)}) collective-permute-start(f32[8,128]{1,0:T(8,128)S(1)} %get-tuple-element.39), channel_id=1, source_target_pairs={{0,16},{16,32},{32,48},{48,64},{64,80},{80,96},{96,112},{112,240},... | collective-permute-start | bytes 12296 | tf_op jit(solution)/shard_map/ppermute | solution.py:665
  49.3 2.3 %collective-permute-start.3 = (f32[8,128]{1,0:T(8,128)S(1)}, f32[8,128]{1,0:T(8,128)S(1)}, u32[]{:S(2)}, u32[]{:S(2)}) collective-permute-start(f32[8,128]{1,0:T(8,128)S(1)} %get-tuple-element.40), channel_id=1, source_target_pairs={{16,0},{32,16},{48,32},{64,48},{80,64},{96,80},{112,96},{240,112},... | collective-permute-start | bytes 12296 | tf_op jit(solution)/shard_map/ppermute | solution.py:666
  74.9 6.8 %collective-permute-start.4 = (f32[32,128]{1,0:T(8,128)S(1)}, f32[32,128]{1,0:T(8,128)S(1)}, u32[]{:S(2)}, u32[]{:S(2)}) collective-permute-start(f32[32,128]{1,0:T(8,128)S(1)} %get-tuple-element.51), channel_id=1, source_target_pairs={{0,128},{128,256},{256,384},{384,512},{512,640},{640,768},{768,896... | collective-permute-start | bytes 49160 | tf_op jit(solution)/shard_map/ppermute | solution.py:663
  77.5 4.1 %collective-permute-start.5 = (f32[32,128]{1,0:T(8,128)S(1)}, f32[32,128]{1,0:T(8,128)S(1)}, u32[]{:S(2)}, u32[]{:S(2)}) collective-permute-start(f32[32,128]{1,0:T(8,128)S(1)} %get-tuple-element.52), channel_id=1, source_target_pairs={{128,0},{256,128},{384,256},{512,384},{640,512},{768,640},{896,768... | collective-permute-start | bytes 49160 | tf_op jit(solution)/shard_map/ppermute | solution.py:664
  77.5 3.5 %collective-permute-start.6 = (f32[8,128]{1,0:T(8,128)S(1)}, f32[8,128]{1,0:T(8,128)S(1)}, u32[]{:S(2)}, u32[]{:S(2)}) collective-permute-start(f32[8,128]{1,0:T(8,128)S(1)} %get-tuple-element.53), channel_id=1, source_target_pairs={{0,16},{16,32},{32,48},{48,64},{64,80},{80,96},{96,112},{112,240},... | collective-permute-start | bytes 12296 | tf_op jit(solution)/shard_map/ppermute | solution.py:665
  80.2 1.4 %collective-permute-start.7 = (f32[8,128]{1,0:T(8,128)S(1)}, f32[8,128]{1,0:T(8,128)S(1)}, u32[]{:S(2)}, u32[]{:S(2)}) collective-permute-start(f32[8,128]{1,0:T(8,128)S(1)} %get-tuple-element.54), channel_id=1, source_target_pairs={{16,0},{32,16},{48,32},{64,48},{80,64},{96,80},{112,96},{240,112},... | collective-permute-start | bytes 12296 | tf_op jit(solution)/shard_map/ppermute | solution.py:666
